TPU v7x, 128 devices: a whole 4x4x4 slice. The times are simulated.
128 devices in a mesh: gx: 16 (over z, y), gy: 8 (over x, core).
Axes of the slice: x: 4, y: 4, z: 4, core: 2. Of those that a mesh axis runs over, the one named last changes fastest.
Arguments:
- atm_flux: bfloat16 [128, 128, 1, 16, 256], P(('gx', 'gy')), may hold values from -6 to 6
- owner_map: int32 [128, 128], P(None, ('gx', 'gy')), may hold values from 0 to 127, as said below
- wet_mask: int32 [512, 16], P('gy', 'gx'), may hold values from 0 to 1, as said below
- stem_weight: bfloat16 [200, 16, 2, 2], replicated, may hold values from -0.75 to 0.75
- depth_weight: float32 [2, 200, 7, 7], replicated, may hold values from -0.875 to 0.875
- depth_bias: float32 [2, 200], replicated, may hold values from -3 to 3
- norm_gain: float32 [2, 200], replicated, may hold values from 0.1 to 1.9
- expand_weight: bfloat16 [2, 200, 800], replicated, may hold values from -0.4375 to 0.4375
- expand_bias: float32 [2, 800], replicated, may hold values from -3 to 3
- reduce_weight: bfloat16 [2, 800, 200], replicated, may hold values from -0.21875 to 0.21875
Outputs:
- ocean_state: bfloat16 [200, 512, 2048], P(None, 'gy', 'gx')
Inputs may be any that keep to these rules, and one draw needn't show every extreme that they name: For every ocean tile k, the column owner_map[:, k] is a permutation of 0 to 127. Every ocean tile (the 64 rows of wet_mask that one index pair of gx and gy holds) has at most 48 rows equal to 1, and some tile has exactly 48.
All inputs are finite; a program needn't handle non-finite values.
Results may differ from a plain program's by a relative error of at most 0.0062.
Values may be sent and summed in bfloat16 or wider, within the bound.
No kernel may reach another device: no remote copies, remote signals or barrier semaphores. Data moves between devices by JAX's collectives and lax.ppermute only.
A program may use at most 128 MiB of HBM per device.

v0:
```python
import jax
import jax.numpy as jnp
from jax import lax
from jax.sharding import PartitionSpec as P


def padded_2(block, sides, width):
    for axis, dim in sides:
        count = lax.axis_size(axis)
        forward = [(i, i + 1) for i in range(count - 1)]
        forward.append((count - 1, 0))
        backward = [(target, source) for source, target in forward]
        low = lax.ppermute(
            lax.slice_in_dim(block, block.shape[dim] - width, None, axis=dim), axis, forward
        )
        high = lax.ppermute(lax.slice_in_dim(block, 0, width, axis=dim), axis, backward)
        block = jnp.concatenate([low, block, high], axis=dim)
    return block


def from_partner(shard, axis, bit):
    return lax.ppermute(shard, axis, [(i, i ^ 1 << bit) for i in range(lax.axis_size(axis))])


def depth_conv(padded, kernel, offset, height, breadth):
    total = jnp.zeros((padded.shape[0], height, breadth), jnp.float32) + offset[:, None, None]
    for tap_row in range(7):
        for tap_col in range(7):
            window = padded[:, tap_row : tap_row + height, tap_col : tap_col + breadth].astype(
                jnp.float32
            )
            total = total + window * kernel[:, tap_row, tap_col][:, None, None]
    return total


def channel_mix(depth_rows, gain, expand_weight, expand_bias, reduce_weight):
    width = depth_rows.shape[0]
    flat = depth_rows.reshape(width, -1)
    center = jnp.mean(flat, axis=0, keepdims=True)
    spread = jnp.mean((flat - center) ** 2, axis=0, keepdims=True)
    normed = ((flat - center) * lax.rsqrt(spread + 1e-06) * gain[:, None]).astype(jnp.bfloat16)
    hidden = (
        jnp.einsum("ch,cn->hn", expand_weight, normed, preferred_element_type=jnp.float32)
        + expand_bias[:, None]
    )
    hidden = jax.nn.gelu(hidden, approximate=True).astype(jnp.bfloat16)
    branch = jnp.einsum("hc,hn->cn", reduce_weight, hidden, preferred_element_type=jnp.float32)
    return branch.reshape(depth_rows.shape)


def body(
    atm_flux,
    owner_map,
    wet_mask,
    stem_weight,
    depth_weight,
    depth_bias,
    norm_gain,
    expand_weight,
    expand_bias,
    reduce_weight,
):
    lon_count = lax.axis_size("gx")
    lat_count = lax.axis_size("gy")
    lat_index = lax.axis_index("gy")
    outgoing = atm_flux[0]
    arrived = lax.all_to_all(outgoing, ("gx", "gy"), split_axis=0, concat_axis=0, tiled=True)
    placed = jnp.zeros_like(arrived).at[owner_map[:, 0]].set(arrived)
    piece_count, piece_rows, flux_count, fine_cols = placed.shape
    height = piece_count * piece_rows // 2
    breadth = fine_cols // 2
    fine = placed.reshape(height, 2, flux_count, breadth, 2)
    stem = jnp.einsum("idkjc,okdc->oij", fine, stem_weight, preferred_element_type=jnp.float32)
    wet_rows = wet_mask[:, 0]
    row_mask = wet_rows.astype(jnp.float32)[None, :, None]
    state = (stem * row_mask).astype(jnp.bfloat16)
    for block_index in range(depth_weight.shape[0]):
        padded = padded_2(state, (("gx", 2), ("gy", 1)), 3)
        strip = padded[:, height : height + 3, :]
        mirrored = strip
        for bit_number in range(lon_count.bit_length() - 1):
            mirrored = from_partner(mirrored, "gx", bit_number)
        upper = jnp.where(
            lat_index == lat_count - 1, mirrored[:, ::-1, ::-1], padded[:, height + 3 :, :]
        )
        lower = jnp.where(lat_index == 0, jnp.zeros_like(strip), padded[:, :3, :])
        padded = jnp.concatenate([lower, padded[:, 3 : height + 3, :], upper], axis=1)
        depth_out = depth_conv(
            padded, depth_weight[block_index], depth_bias[block_index], height, breadth
        )
        branch = channel_mix(
            depth_out,
            norm_gain[block_index],
            expand_weight[block_index],
            expand_bias[block_index],
            reduce_weight[block_index],
        )
        state = ((state.astype(jnp.float32) + branch) * row_mask).astype(jnp.bfloat16)
    return state


def solution(mesh):
    return jax.shard_map(
        body,
        mesh=mesh,
        in_specs=(
            P(("gx", "gy"), None, None, None, None),
            P(None, ("gx", "gy")),
            P("gy", "gx"),
            P(),
            P(),
            P(),
            P(),
            P(),
            P(),
            P(),
        ),
        out_specs=P(None, "gy", "gx"),
        check_vma=False,
    )
```

profile of v0, /device:TPU:0, one launch (start us, length us, event | category | flops | bytes accessed | tf_op | source)
XLA Modules:
  0.0 506.8 jit_solution(17584365956552801041)
XLA Ops:
  0.0 11.1 %all-to-all-start = ((bf16[128,1,16,256]{3,2,1,0:T(8,128)(2,1)}), bf16[128,1,16,256]{3,2,1,0:T(8,128)(2,1)S(1)}, u32[]{:S(2)}, u32[]{:S(2)}) async-start(bf16[128,1,16,256]{3,2,1,0:T(8,128)(2,1)} %bitcast.188), calls=%async_computation | async-start | bytes 2097152 | tf_op jit(solution)/shard_map/all_to_all | solution.py:67
  14.2 16.1 %all-to-all-done = bf16[128,1,16,256]{3,2,1,0:T(8,128)(2,1)S(1)} async-done(((bf16[128,1,16,256]{3,2,1,0:T(8,128)(2,1)}), bf16[128,1,16,256]{3,2,1,0:T(8,128)(2,1)S(1)}, u32[]{:S(2)}, u32[]{:S(2)}) %all-to-all-start) | async-done | bytes 1048608 | tf_op jit(solution)/shard_map/all_to_all | solution.py:67
  30.4 4.3 scatter_fusion
  34.7 5.9 %copy.32 = bf16[128,16,256]{1,2,0:T(8,128)(2,1)} copy(bf16[128,16,256]{2,1,0:T(8,128)(2,1)S(1)} %scatter_fusion) | data formatting | bytes 2097152 | tf_op jit(solution)/shard_map/scatter | solution.py:68
  40.7 6.3 %fusion.77 = bf16[200,64,128]{2,0,1:T(8,128)(2,1)S(1)} fusion(f32[64]{0:T(128)S(1)} %convert_bitcast_fusion, bf16[64,2,16,128,2]{2,4,3,1,0:T(2,128)(2,1)} %bitcast.186, bf16[200,16,2,2]{0,3,2,1:T(2,128)(2,1)S(1)} %copy-done.33), kind=kOutput, calls=%fused_computation.109 | convolution fusion | flops 212992000 | bytes 4351232 | tf_op jit(solution)/shard_map/idkjc,okdc->oij/dot_general | solution.py:73
  47.0 3.9 fusion.130
  54.6 4.1 copy.36
  58.8 5.1 %collective-permute-start.1 = (bf16[200,64,3]{0,1,2:T(8,128)(2,1)}, bf16[200,64,3]{0,1,2:T(8,128)(2,1)}, u32[]{:S(2)}, u32[]{:S(2)}) collective-permute-start(bf16[200,64,3]{0,1,2:T(8,128)(2,1)} %copy.36), channel_id=1, source_target_pairs={{8,0},{16,8},{24,16},{32,24},{40,32},{48,40},{56,48},{64,56},{72,6... | collective-permute-start | bytes 230408 | tf_op jit(solution)/shard_map/ppermute | solution.py:16
  68.3 3.9 copy.38
  74.5 8.8 %collective-permute-done.3 = bf16[200,3,134]{2,0,1:T(8,128)(2,1)S(1)} collective-permute-done((bf16[200,3,134]{2,0,1:T(8,128)(2,1)}, bf16[200,3,134]{2,0,1:T(8,128)(2,1)S(1)}, u32[]{:S(2)}, u32[]{:S(2)}) %collective-permute-start.3) | collective-permute-done | bytes 160832 | tf_op jit(solution)/shard_map/ppermute | solution.py:22
  83.9 8.0 %collective-permute-done.4 = bf16[200,3,134]{2,0,1:T(8,128)(2,1)} collective-permute-done((bf16[200,3,134]{2,0,1:T(8,128)(2,1)S(1)}, bf16[200,3,134]{2,0,1:T(8,128)(2,1)}, u32[]{:S(2)}, u32[]{:S(2)}) %collective-permute-start.4) | collective-permute-done | bytes 160832 | tf_op jit(solution)/shard_map/ppermute | solution.py:22
  93.1 6.5 %collective-permute-done.5 = bf16[200,3,134]{2,0,1:T(8,128)(2,1)} collective-permute-done((bf16[200,3,134]{2,0,1:T(8,128)(2,1)}, bf16[200,3,134]{2,0,1:T(8,128)(2,1)}, u32[]{:S(2)}, u32[]{:S(2)}) %collective-permute-start.5) | collective-permute-done | bytes 160832 | tf_op jit(solution)/shard_map/ppermute | solution.py:22
  100.9 7.9 %collective-permute-done.6 = bf16[200,3,134]{2,0,1:T(8,128)(2,1)} collective-permute-done((bf16[200,3,134]{2,0,1:T(8,128)(2,1)}, bf16[200,3,134]{2,0,1:T(8,128)(2,1)}, u32[]{:S(2)}, u32[]{:S(2)}) %collective-permute-start.6) | collective-permute-done | bytes 160832 | tf_op jit(solution)/shard_map/ppermute | solution.py:22
  108.8 6.6 %reverse = bf16[200,3,256]{2,0,1:T(8,128)(2,1)} reverse(bf16[200,3,256]{2,0,1:T(8,128)(2,1)} %bitcast.178), dimensions={1,2} | reverse | bytes 614400
  116.8 14.2 %maximum_maximum_fusion = (bf16[200,67,134]{2,0,1:T(8,128)(2,1)}, bf16[200,67,134]{2,0,1:T(8,128)(2,1)}) fusion(bf16[200,64,3]{2,0,1:T(8,128)(2,1)} %copy.38, bf16[200,64,128]{2,0,1:T(8,128)(2,1)S(1)} %fusion.77, bf16[200,64,3]{2,0,1:T(8,128)(2,1)} %copy.37, bf16[200,3,134]{2,0,1:T(8,128)(2,1)} %broadcast_select_fusion.3, ...), kind=kLoop, calls=%fused_computation.41 | loop fusion | flops 28729600 | bytes 10934400 | tf_op jit(solution)/shard_map/concatenate | solution.py:87
  131.2 119.8 %fusion.127 = (f32[64,128]{1,0:T(8,128)S(1)}, f32[200,64,128]{2,0,1:T(8,128)}) fusion(f32[200]{0:T(256)S(1)} %bitcast.190, bf16[200,67,134]{2,0,1:T(8,128)(2,1)} %get-tuple-element.16, f32[200]{0:T(256)S(1)} %bitcast.191, f32[200]{0:T(256)S(1)} %bitcast.192, f32[200]{0:T(256)S(1)} %bitcast.193, f32[200]{0:T(256)S(1)} %bitcast.194, f32[200]{0:T(256)S(1)} %bitcast.195, ...), kind=kLoop, calls=%fused_computation.168 | loop fusion | flops 271966208 | bytes 147682368 | tf_op jit(solution)/shard_map/reduce_sum | solution.py:39
  251.1 4.0 multiply_reduce_fusion.1
  255.1 16.3 %fusion.94 = f32[25,64,8,128]{3,2,1,0:T(8,128)} fusion(f32[800]{0:T(1024)S(1)} %get-tuple-element.6, bf16[2,800,200]{1,2,0:T(8,128)(2,1)S(1)} %copy-done.31, bf16[2,200,800]{2,1,0:T(8,128)(2,1)S(1)} %copy-done.32, f32[200,64,128]{2,0,1:T(8,128)} %get-tuple-element.10, f32[200]{0:T(256)S(1)} %bitcast.290, f32[64,128]{1,0:T(8,128)S(1)} %add_rsqrt_fusion.1, ...), kind=kOutput, calls=%fused_computation.126 | convolution fusion | flops 5314969600 | bytes 13894656 | tf_op jit(solution)/shard_map/hc,hn->cn/dot_general | solution.py:47
  271.4 4.8 fusion.44
  276.2 3.9 fusion.129
  284.9 4.1 copy.45
  289.1 4.1 collective-permute-start.9
  302.1 8.9 %collective-permute-done.11 = bf16[200,3,134]{2,0,1:T(8,128)(2,1)S(1)} collective-permute-done((bf16[200,3,134]{2,0,1:T(8,128)(2,1)S(1)}, bf16[200,3,134]{2,0,1:T(8,128)(2,1)S(1)}, u32[]{:S(2)}, u32[]{:S(2)}) %collective-permute-start.11) | collective-permute-done | bytes 160832 | tf_op jit(solution)/shard_map/ppermute | solution.py:22
  312.4 6.9 %collective-permute-done.12 = bf16[200,3,134]{2,0,1:T(8,128)(2,1)S(1)} collective-permute-done((bf16[200,3,134]{2,0,1:T(8,128)(2,1)S(1)}, bf16[200,3,134]{2,0,1:T(8,128)(2,1)S(1)}, u32[]{:S(2)}, u32[]{:S(2)}) %collective-permute-start.12) | collective-permute-done | bytes 160832 | tf_op jit(solution)/shard_map/ppermute | solution.py:22
  319.3 10.0 %collective-permute-done.13 = bf16[200,3,134]{2,0,1:T(8,128)(2,1)S(1)} collective-permute-done((bf16[200,3,134]{2,0,1:T(8,128)(2,1)S(1)}, bf16[200,3,134]{2,0,1:T(8,128)(2,1)S(1)}, u32[]{:S(2)}, u32[]{:S(2)}) %collective-permute-start.13) | collective-permute-done | bytes 160832 | tf_op jit(solution)/shard_map/ppermute | solution.py:22
  330.3 7.7 %collective-permute-done.14 = bf16[200,3,134]{2,0,1:T(8,128)(2,1)} collective-permute-done((bf16[200,3,134]{2,0,1:T(8,128)(2,1)S(1)}, bf16[200,3,134]{2,0,1:T(8,128)(2,1)}, u32[]{:S(2)}, u32[]{:S(2)}) %collective-permute-start.14) | collective-permute-done | bytes 160832 | tf_op jit(solution)/shard_map/ppermute | solution.py:22
  338.0 6.6 %reverse.1 = bf16[200,3,256]{2,0,1:T(8,128)(2,1)} reverse(bf16[200,3,256]{2,0,1:T(8,128)(2,1)} %bitcast.179), dimensions={1,2} | reverse | bytes 614400
  345.8 14.2 %maximum_maximum_fusion.1 = (bf16[200,67,134]{2,0,1:T(8,128)(2,1)}, bf16[200,67,134]{2,0,1:T(8,128)(2,1)}) fusion(bf16[200,64,3]{2,0,1:T(8,128)(2,1)} %copy.47, bf16[200,64,128]{2,0,1:T(8,128)(2,1)S(1)} %fusion.44, bf16[200,64,3]{2,0,1:T(8,128)(2,1)} %copy.46, bf16[200,3,134]{2,0,1:T(8,128)(2,1)} %broadcast_select_fusion.2, ...), kind=kLoop, calls=%fused_computation.43 | loop fusion | flops 28729600 | bytes 10934400 | tf_op jit(solution)/shard_map/concatenate | solution.py:87
  360.0 119.5 %fusion.125 = (f32[64,128]{1,0:T(8,128)S(1)}, f32[200,64,128]{2,0,1:T(8,128)}) fusion(f32[200]{0:T(256)S(1)} %bitcast.239, bf16[200,67,134]{2,0,1:T(8,128)(2,1)} %get-tuple-element.12, f32[200]{0:T(256)S(1)} %bitcast.240, f32[200]{0:T(256)S(1)} %bitcast.241, f32[200]{0:T(256)S(1)} %bitcast.242, f32[200]{0:T(256)S(1)} %bitcast.243, f32[200]{0:T(256)S(1)} %bitcast.244, ...), kind=kLoop, calls=%fused_computation.167 | loop fusion | flops 271966208 | bytes 147682368 | tf_op jit(solution)/shard_map/reduce_sum | solution.py:39
  479.5 3.9 multiply_reduce_fusion
  483.5 16.5 %fusion.97 = f32[25,64,8,128]{3,2,1,0:T(8,128)} fusion(f32[800]{0:T(1024)S(1)} %copy-done.2, bf16[2,800,200]{1,2,0:T(8,128)(2,1)} %param.19, bf16[2,200,800]{2,1,0:T(8,128)(2,1)} %param.17, f32[200,64,128]{2,0,1:T(8,128)} %get-tuple-element.8, f32[200]{0:T(256)S(1)} %bitcast.289, f32[64,128]{1,0:T(8,128)S(1)} %add_rsqrt_fusion, ...), kind=kOutput, calls=%fused_computation.127 | convolution fusion | flops 5314969600 | bytes 13893536 | tf_op jit(solution)/shard_map/hc,hn->cn/dot_general | solution.py:47
  500.0 3.8 fusion.71
  (120 shorter events, 38.0 us)
Async XLA Ops:
  0.0 30.3 %all-to-all-start = ((bf16[128,1,16,256]{3,2,1,0:T(8,128)(2,1)}), bf16[128,1,16,256]{3,2,1,0:T(8,128)(2,1)S(1)}, u32[]{:S(2)}, u32[]{:S(2)}) async-start(bf16[128,1,16,256]{3,2,1,0:T(8,128)(2,1)} %bitcast.188), calls=%async_computation | async-start | bytes 2097152 | tf_op jit(solution)/shard_map/all_to_all | solution.py:67
  11.8 28.9 %copy-start.26 = (f32[64]{0:T(128)}, f32[64]{0:T(128)S(1)}, u32[]{:S(2)}) copy-start(f32[64]{0:T(128)S(1)} %convert_bitcast_fusion) | copy-start | bytes 772
  47.0 84.1 %copy-start = (bf16[200,64,128]{2,0,1:T(8,128)(2,1)}, bf16[200,64,128]{2,0,1:T(8,128)(2,1)S(1)}, u32[]{:S(2)}) copy-start(bf16[200,64,128]{2,0,1:T(8,128)(2,1)S(1)} %fusion.77) | copy-start | bytes 9830404
  54.4 10.2 %collective-permute-start = (bf16[200,64,3]{0,1,2:T(8,128)(2,1)S(1)}, bf16[200,64,3]{0,1,2:T(8,128)(2,1)}, u32[]{:S(2)}, u32[]{:S(2)}) collective-permute-start(bf16[200,64,3]{0,1,2:T(8,128)(2,1)S(1)} %copy.35), channel_id=1, source_target_pairs={{0,8},{8,16},{16,24},{24,32},{32,40},{40,48},{48,56},{56,64},{64,7... | collective-permute-start | bytes 230408 | tf_op jit(solution)/shard_map/ppermute | solution.py:13
  58.8 9.5 %collective-permute-start.1 = (bf16[200,64,3]{0,1,2:T(8,128)(2,1)}, bf16[200,64,3]{0,1,2:T(8,128)(2,1)}, u32[]{:S(2)}, u32[]{:S(2)}) collective-permute-start(bf16[200,64,3]{0,1,2:T(8,128)(2,1)} %copy.36), channel_id=1, source_target_pairs={{8,0},{16,8},{24,16},{32,24},{40,32},{48,40},{56,48},{64,56},{72,6... | collective-permute-start | bytes 230408 | tf_op jit(solution)/shard_map/ppermute | solution.py:16
  68.3 15.0 %copy-start.28 = (f32[2,200]{1,0:T(2,128)S(1)}, f32[2,200]{1,0:T(2,128)}, u32[]{:S(2)}) copy-start(f32[2,200]{1,0:T(2,128)} %param.15) | copy-start | bytes 4804
  68.3 23.6 %copy-start.29 = (f32[2,200]{1,0:T(2,128)S(1)}, f32[2,200]{1,0:T(2,128)}, u32[]{:S(2)}) copy-start(f32[2,200]{1,0:T(2,128)} %param.16) | copy-start | bytes 4804
  68.3 24.2 %copy-start.1 = (f32[2,800]{1,0:T(2,128)S(1)}, f32[2,800]{1,0:T(2,128)}, u32[]{:S(2)}) copy-start(f32[2,800]{1,0:T(2,128)} %param.18) | copy-start | bytes 19204
  74.5 8.8 %collective-permute-start.3 = (bf16[200,3,134]{2,0,1:T(8,128)(2,1)}, bf16[200,3,134]{2,0,1:T(8,128)(2,1)S(1)}, u32[]{:S(2)}, u32[]{:S(2)}) collective-permute-start(bf16[200,3,134]{2,0,1:T(8,128)(2,1)} %get-tuple-element.18), channel_id=1, source_target_pairs={{0,8},{8,0},{16,24},{24,16},{32,40},{40,32},{48,56},{56,48},{64,72... | collective-permute-start | bytes 482408 | tf_op jit(solution)/shard_map/ppermute | solution.py:22
  83.3 8.6 %collective-permute-start.4 = (bf16[200,3,134]{2,0,1:T(8,128)(2,1)S(1)}, bf16[200,3,134]{2,0,1:T(8,128)(2,1)}, u32[]{:S(2)}, u32[]{:S(2)}) collective-permute-start(bf16[200,3,134]{2,0,1:T(8,128)(2,1)S(1)} %collective-permute-done.3), channel_id=1, source_target_pairs={{0,16},{8,24},{16,0},{24,8},{32,48},{40,56},{48,32},{56,40},{64,80... | collective-permute-start | bytes 482408 | tf_op jit(solution)/shard_map/ppermute | solution.py:22
  83.9 16.2 %collective-permute-start.2 = (bf16[200,3,134]{2,0,1:T(8,128)(2,1)}, bf16[200,3,134]{2,0,1:T(8,128)(2,1)}, u32[]{:S(2)}, u32[]{:S(2)}) collective-permute-start(bf16[200,3,134]{2,0,1:T(8,128)(2,1)} %get-tuple-element.18), channel_id=1, source_target_pairs={{0,1},{1,2},{2,3},{3,4},{4,5},{5,6},{6,7},{7,0},{8,9},{9,10},{10,1... | collective-permute-start | bytes 482408 | tf_op jit(solution)/shard_map/ppermute | solution.py:13
  91.9 7.7 %collective-permute-start.5 = (bf16[200,3,134]{2,0,1:T(8,128)(2,1)}, bf16[200,3,134]{2,0,1:T(8,128)(2,1)}, u32[]{:S(2)}, u32[]{:S(2)}) collective-permute-start(bf16[200,3,134]{2,0,1:T(8,128)(2,1)} %collective-permute-done.4), channel_id=1, source_target_pairs={{0,32},{8,40},{16,48},{24,56},{32,0},{40,8},{48,16},{56,24},{64,96... | collective-permute-start | bytes 482408 | tf_op jit(solution)/shard_map/ppermute | solution.py:22
  93.1 22.2 %collective-permute-start.7 = (bf16[200,3,134]{2,0,1:T(8,128)(2,1)}, bf16[200,3,134]{2,0,1:T(8,128)(2,1)}, u32[]{:S(2)}, u32[]{:S(2)}) collective-permute-start(bf16[200,3,134]{2,0,1:T(8,128)(2,1)} %get-tuple-element.17), channel_id=1, source_target_pairs={{1,0},{2,1},{3,2},{4,3},{5,4},{6,5},{7,6},{0,7},{9,8},{10,9},{11,1... | collective-permute-start | bytes 482408 | tf_op jit(solution)/shard_map/ppermute | solution.py:16
  99.7 9.1 %collective-permute-start.6 = (bf16[200,3,134]{2,0,1:T(8,128)(2,1)}, bf16[200,3,134]{2,0,1:T(8,128)(2,1)}, u32[]{:S(2)}, u32[]{:S(2)}) collective-permute-start(bf16[200,3,134]{2,0,1:T(8,128)(2,1)} %collective-permute-done.5), channel_id=1, source_target_pairs={{0,64},{8,72},{16,80},{24,88},{32,96},{40,104},{48,112},{56,120},{... | collective-permute-start | bytes 482408 | tf_op jit(solution)/shard_map/ppermute | solution.py:22
  116.6 14.5 %copy-start.3 = (f32[200,1,1]{0,2,1:T(1,128)S(1)}, f32[200,1,1]{0,2,1:T(1,128)}, u32[]{:S(2)}) copy-start(f32[200,1,1]{0,2,1:T(1,128)} %get-tuple-element.90) | copy-start | bytes 2404
  116.6 14.5 %copy-start.4 = (f32[200,1,1]{0,2,1:T(1,128)S(1)}, f32[200,1,1]{0,2,1:T(1,128)}, u32[]{:S(2)}) copy-start(f32[200,1,1]{0,2,1:T(1,128)} %get-tuple-element.91) | copy-start | bytes 2404
  116.6 14.5 %copy-start.5 = (f32[200,1,1]{0,2,1:T(1,128)S(1)}, f32[200,1,1]{0,2,1:T(1,128)}, u32[]{:S(2)}) copy-start(f32[200,1,1]{0,2,1:T(1,128)} %get-tuple-element.92) | copy-start | bytes 2404
  116.6 14.5 %copy-start.6 = (f32[200,1,1]{0,2,1:T(1,128)S(1)}, f32[200,1,1]{0,2,1:T(1,128)}, u32[]{:S(2)}) copy-start(f32[200,1,1]{0,2,1:T(1,128)} %get-tuple-element.93) | copy-start | bytes 2404
  116.6 14.5 %copy-start.7 = (f32[200,1,1]{0,2,1:T(1,128)S(1)}, f32[200,1,1]{0,2,1:T(1,128)}, u32[]{:S(2)}) copy-start(f32[200,1,1]{0,2,1:T(1,128)} %get-tuple-element.94) | copy-start | bytes 2404
  116.6 14.5 %copy-start.8 = (f32[200,1,1]{0,2,1:T(1,128)S(1)}, f32[200,1,1]{0,2,1:T(1,128)}, u32[]{:S(2)}) copy-start(f32[200,1,1]{0,2,1:T(1,128)} %get-tuple-element.95) | copy-start | bytes 2404
  116.6 14.5 %copy-start.9 = (f32[200,1,1]{0,2,1:T(1,128)S(1)}, f32[200,1,1]{0,2,1:T(1,128)}, u32[]{:S(2)}) copy-start(f32[200,1,1]{0,2,1:T(1,128)} %get-tuple-element.96) | copy-start | bytes 2404
  116.6 14.5 %copy-start.10 = (f32[200,1,1]{0,2,1:T(1,128)S(1)}, f32[200,1,1]{0,2,1:T(1,128)}, u32[]{:S(2)}) copy-start(f32[200,1,1]{0,2,1:T(1,128)} %get-tuple-element.97) | copy-start | bytes 2404
  116.6 14.5 %copy-start.11 = (f32[200,1,1]{0,2,1:T(1,128)S(1)}, f32[200,1,1]{0,2,1:T(1,128)}, u32[]{:S(2)}) copy-start(f32[200,1,1]{0,2,1:T(1,128)} %get-tuple-element.98) | copy-start | bytes 2404
  255.1 16.3 %copy-start.27 = (f32[64]{0:T(128)S(1)}, f32[64]{0:T(128)}, u32[]{:S(2)}) copy-start(f32[64]{0:T(128)} %copy-done.26) | copy-start | bytes 772
  283.6 9.6 %collective-permute-start.8 = (bf16[200,64,3]{0,1,2:T(8,128)(2,1)S(1)}, bf16[200,64,3]{0,1,2:T(8,128)(2,1)S(1)}, u32[]{:S(2)}, u32[]{:S(2)}) collective-permute-start(bf16[200,64,3]{0,1,2:T(8,128)(2,1)S(1)} %copy.44), channel_id=1, source_target_pairs={{0,8},{8,16},{16,24},{24,32},{32,40},{40,48},{48,56},{56,64},{64,7... | collective-permute-start | bytes 230408 | tf_op jit(solution)/shard_map/ppermute | solution.py:13
  289.1 7.0 %collective-permute-start.9 = (bf16[200,64,3]{0,1,2:T(8,128)(2,1)}, bf16[200,64,3]{0,1,2:T(8,128)(2,1)}, u32[]{:S(2)}, u32[]{:S(2)}) collective-permute-start(bf16[200,64,3]{0,1,2:T(8,128)(2,1)} %copy.45), channel_id=1, source_target_pairs={{8,0},{16,8},{24,16},{32,24},{40,32},{48,40},{56,48},{64,56},{72,6... | collective-permute-start | bytes 230408 | tf_op jit(solution)/shard_map/ppermute | solution.py:16
  302.0 8.9 %collective-permute-start.11 = (bf16[200,3,134]{2,0,1:T(8,128)(2,1)S(1)}, bf16[200,3,134]{2,0,1:T(8,128)(2,1)S(1)}, u32[]{:S(2)}, u32[]{:S(2)}) collective-permute-start(bf16[200,3,134]{2,0,1:T(8,128)(2,1)S(1)} %get-tuple-element.14), channel_id=1, source_target_pairs={{0,8},{8,0},{16,24},{24,16},{32,40},{40,32},{48,56},{56,48},{64,72... | collective-permute-start | bytes 482408 | tf_op jit(solution)/shard_map/ppermute | solution.py:22
  310.9 8.4 %collective-permute-start.12 = (bf16[200,3,134]{2,0,1:T(8,128)(2,1)S(1)}, bf16[200,3,134]{2,0,1:T(8,128)(2,1)S(1)}, u32[]{:S(2)}, u32[]{:S(2)}) collective-permute-start(bf16[200,3,134]{2,0,1:T(8,128)(2,1)S(1)} %collective-permute-done.11), channel_id=1, source_target_pairs={{0,16},{8,24},{16,0},{24,8},{32,48},{40,56},{48,32},{56,40},{64,80... | collective-permute-start | bytes 482408 | tf_op jit(solution)/shard_map/ppermute | solution.py:22
  312.4 17.1 %collective-permute-start.10 = (bf16[200,3,134]{2,0,1:T(8,128)(2,1)S(1)}, bf16[200,3,134]{2,0,1:T(8,128)(2,1)S(1)}, u32[]{:S(2)}, u32[]{:S(2)}) collective-permute-start(bf16[200,3,134]{2,0,1:T(8,128)(2,1)S(1)} %get-tuple-element.14), channel_id=1, source_target_pairs={{0,1},{1,2},{2,3},{3,4},{4,5},{5,6},{6,7},{7,0},{8,9},{9,10},{10,1... | collective-permute-start | bytes 482408 | tf_op jit(solution)/shard_map/ppermute | solution.py:13
  319.3 10.0 %collective-permute-start.13 = (bf16[200,3,134]{2,0,1:T(8,128)(2,1)S(1)}, bf16[200,3,134]{2,0,1:T(8,128)(2,1)S(1)}, u32[]{:S(2)}, u32[]{:S(2)}) collective-permute-start(bf16[200,3,134]{2,0,1:T(8,128)(2,1)S(1)} %collective-permute-done.12), channel_id=1, source_target_pairs={{0,32},{8,40},{16,48},{24,56},{32,0},{40,8},{48,16},{56,24},{64,96... | collective-permute-start | bytes 482408 | tf_op jit(solution)/shard_map/ppermute | solution.py:22
  319.3 25.2 %collective-permute-start.15 = (bf16[200,3,134]{2,0,1:T(8,128)(2,1)}, bf16[200,3,134]{2,0,1:T(8,128)(2,1)}, u32[]{:S(2)}, u32[]{:S(2)}) collective-permute-start(bf16[200,3,134]{2,0,1:T(8,128)(2,1)} %get-tuple-element.13), channel_id=1, source_target_pairs={{1,0},{2,1},{3,2},{4,3},{5,4},{6,5},{7,6},{0,7},{9,8},{10,9},{11,1... | collective-permute-start | bytes 482408 | tf_op jit(solution)/shard_map/ppermute | solution.py:16
  329.3 8.7 %collective-permute-start.14 = (bf16[200,3,134]{2,0,1:T(8,128)(2,1)S(1)}, bf16[200,3,134]{2,0,1:T(8,128)(2,1)}, u32[]{:S(2)}, u32[]{:S(2)}) collective-permute-start(bf16[200,3,134]{2,0,1:T(8,128)(2,1)S(1)} %collective-permute-done.13), channel_id=1, source_target_pairs={{0,64},{8,72},{16,80},{24,88},{32,96},{40,104},{48,112},{56,120},{... | collective-permute-start | bytes 482408 | tf_op jit(solution)/shard_map/ppermute | solution.py:22
  (19 other events, 228.7 us)
where the time goes:
time: 516 us; the launch traced here: 507 us
  other arithmetic  294 us (57%)
  waiting for transfers between devices  80.8 us (16%)
  local copies, waits for them, and re-layouts  67.6 us (13%)
  matrix products  39 us (8%)
  starting transfers between devices  24.1 us (5%)
    reduce_sum x2, other arithmetic, channel_mix(): center = jnp.mean(flat, axis=0, keepdims=True)  239 us
    ppermute x8, waiting for transfers between devices, from_partner(): lax.ppermute(shard, axis, [(i, i ^ 1 << bit) for i in range(lax.axis_size...  64.7 us
    dot_general x2, matrix products, channel_mix(): jnp.einsum('hc,hn->cn', reduce_weight, hidden, preferred_element_type=jnp...  32.7 us
    concatenate x2, other arithmetic, body(): padded = jnp.concatenate([lower, padded[:, 3:height + 3, :], upper], axis=1)  28.5 us
    all_to_all x1, waiting for transfers between devices, body(): lax.all_to_all(outgoing, ('gx', 'gy'), split_axis=0, concat_axis=0, tiled...  16.1 us
    slice x4, local copies, waits for them, and re-layouts, padded_2(): lax.slice_in_dim(block, block.shape[dim] - width, None, axis=dim)  14.8 us
    unnamed x70, local copies, waits for them, and re-layouts  13.3 us
    all_to_all x1, starting transfers between devices, body(): lax.all_to_all(outgoing, ('gx', 'gy'), split_axis=0, concat_axis=0, tiled...  11.1 us
  transfers between devices with their start and end apart: 17, of which 9 were waited for; matrix products, arithmetic and copies ran while one was open for 7% of the time, Pallas kernels for 0%

commit v1 on v0

v1 whole, which is shorter than its diff:
```python
import functools

import jax
import jax.numpy as jnp
import numpy as np
from jax import lax
from jax.experimental import pallas as pl
from jax.experimental.pallas import tpu as pltpu
from jax.sharding import PartitionSpec as P

LANES = 128
GROUP = 8
HALF = LANES // 2
ROOT = float(np.sqrt(2.0 / np.pi))
VMEM_BYTES = 56 * 1024 * 1024
BF16 = jnp.bfloat16
F32 = jnp.float32


def fourier_tables():
    spot = np.arange(LANES)[:, None]
    wave = np.arange(HALF)[None, :]
    angle = 2.0 * np.pi * (spot * wave % LANES) / LANES
    cos, sin = np.cos(angle), np.sin(angle)
    plain = np.concatenate([cos, -sin], axis=1)
    plain[:, HALF] = np.where(np.arange(LANES) % 2 == 0, 1.0, -1.0)
    swapped = np.concatenate([-sin, cos], axis=1)
    swapped[:, 0] = 0.0
    swapped[:, HALF] = 0.0
    forward = np.concatenate([plain, swapped], axis=1)
    inverse = plain.T * (2.0 / LANES)
    inverse[0] /= 2.0
    inverse[HALF] /= 2.0
    edges = np.zeros((LANES, LANES))
    for j in range(3):
        edges[j, j] = 1.0
        edges[4 + j, LANES - 3 + j] = 1.0
    edges[3, :] = 1.0
    edges[7, :] = 1.0
    inverse = np.concatenate([inverse, edges], axis=0)
    return forward, inverse


def deinterleave_table():
    table = np.zeros((2 * LANES, 2 * LANES))
    spot = np.arange(LANES)
    table[2 * spot, spot] = 1.0
    table[2 * spot + 1, LANES + spot] = 1.0
    return table


def fold_table():
    table = np.zeros((LANES, LANES))
    spot = np.arange(LANES - 1)
    table[LANES - 2 - spot, spot] = 1.0
    return table


def dot(left, right):
    return jnp.dot(left, right, preferred_element_type=F32)


def lane_ids(shape):
    return lax.broadcasted_iota(jnp.int32, shape, len(shape) - 1)


def pack_edges(value, row, low_ref, high_ref):
    group = row // 32
    start = 4 * (row % 32)
    lane = lane_ids(value.shape)
    hit = (lane >= start) & (lane < start + 3)
    low = pltpu.roll(value, start, 1)
    high = pltpu.roll(value, lax.rem(start + 3, LANES), 1)
    low_ref[group] = jnp.where(hit, low, low_ref[group])
    high_ref[group] = jnp.where(hit, high, high_ref[group])


def stem_kernel(rows_ref, inverse_ref, arrived_ref, table_ref, weight_ref, state_ref, low_ref, high_ref,
                split_ref):
    pieces = arrived_ref.shape[0]
    flux = arrived_ref.shape[1]
    height = state_ref.shape[0]
    step = 16

    def split(index, _):
        part = arrived_ref[pl.ds(index * step, step)].reshape(step * flux, 2 * LANES)
        split_ref[pl.ds(index * step, step)] = dot(part, table_ref[...]).astype(BF16).reshape(step, flux, 2 * LANES)
        return 0

    lax.fori_loop(0, pieces // step, split, 0)
    state_ref[...] = jnp.zeros_like(state_ref)
    low_ref[...] = jnp.zeros_like(low_ref)
    high_ref[...] = jnp.zeros_like(high_ref)

    def pair(index, _):
        rows = [rows_ref[1 + GROUP * index + at] for at in range(GROUP)]
        columns = []
        for row in rows:
            one = split_ref[inverse_ref[2 * row]]
            two = split_ref[inverse_ref[2 * row + 1]]
            columns.append(jnp.concatenate([one[:, :LANES], one[:, LANES:], two[:, :LANES], two[:, LANES:]], axis=0))
        out = dot(weight_ref[...], jnp.concatenate(columns, axis=1))
        for at, row in enumerate(rows):
            value = out[:, at * LANES:(at + 1) * LANES].astype(BF16)
            state_ref[row] = value
            pack_edges(value, row, low_ref, high_ref)
        return 0

    @pl.when(rows_ref[0] > 0)
    def _():
        lax.fori_loop(0, (rows_ref.shape[0] - 1) // GROUP, pair, 0)


def block_kernel(last, rows_ref, flags_ref, state_ref, south_ref, north_ref, fold_ref, left_ref, right_ref,
                 mix_ref, forward_ref, flipped_ref, inverse_ref, turn_ref, left_weight_ref, right_weight_ref,
                 bias_ref, gain_ref, expand_ref, reduce_ref, *rest):
    if last:
        out_ref, wave_ref, prod_ref, edge_ref, grid_ref, normed_ref, held_ref = rest
    else:
        out_ref, low_ref, high_ref, wave_ref, prod_ref, edge_ref, grid_ref, normed_ref = rest
    height, width, _ = state_ref.shape
    channels = 200
    groups = (rows_ref.shape[0] - 1) // GROUP
    count = rows_ref[0]
    fold = flags_ref[0]

    def transform(index, _):
        part = state_ref[pl.ds(index * 16, 16)].reshape(16 * width, LANES)
        wave_ref[pl.ds(3 + index * 16, 16)] = dot(part, forward_ref[...]).astype(BF16).reshape(16, width, 2 * LANES)
        return 0

    lax.fori_loop(0, height // 16, transform, 0)
    wave_ref[0:3] = dot(south_ref[0:3].reshape(3 * width, LANES), forward_ref[...]).astype(BF16).reshape(3, width, 2 * LANES)

    for side, ref in enumerate((left_ref, right_ref)):
        grid_ref[side, 0] = south_ref[3 + side]
        grid_ref[side, 1] = ref[0]
        grid_ref[side, 2] = ref[1]

    @pl.when(fold == 0)
    def _():
        wave_ref[height + 3:height + 6] = dot(north_ref[0:3].reshape(3 * width, LANES), forward_ref[...]).astype(BF16).reshape(3, width, 2 * LANES)
        grid_ref[0, 3] = north_ref[3]
        grid_ref[1, 3] = north_ref[4]

    @pl.when(fold != 0)
    def _():
        for m in range(3):
            wave_ref[height + 3 + m] = dot(fold_ref[2 - m], flipped_ref[...]).astype(BF16)
        grid_ref[0, 3] = dot(fold_ref[4], turn_ref[...]).astype(BF16)
        grid_ref[1, 3] = dot(fold_ref[3], turn_ref[...]).astype(BF16)

    def corrections(index, _):
        span = pl.ds(pl.multiple_of(index * 16, 16), 16)
        lane = lane_ids((16, LANES))
        for side in range(2):
            weight_ref = (left_weight_ref, right_weight_ref)[side]
            totals = [jnp.where(lane % 4 == 3, bias_ref[side, span], 0.0)] * 2
            slabs = [grid_ref[side, k, span] for k in range(4)]
            for tap_row in range(7):
                terms = [None, None]
                for tap in range(3):
                    shift = 4 * (tap_row - 3) + (tap if side == 0 else -tap)
                    weight = weight_ref[tap_row * 3 + tap, span]
                    moved = [pltpu.roll(slab, -shift % LANES, 1) if shift else slab for slab in slabs]
                    for group in range(2):
                        value = moved[group + 1]
                        if shift > 0:
                            value = jnp.where(lane < LANES - shift, value, moved[group + 2])
                        if shift < 0:
                            value = jnp.where(lane >= -shift, value, moved[group])
                        value = weight * value
                        terms[group] = value if terms[group] is None else terms[group] + value
                totals = [total + term.astype(F32) for total, term in zip(totals, terms)]
            for group in range(2):
                edge_ref[side, group, span] = totals[group].astype(BF16)
        return 0

    lax.fori_loop(0, width // 16, corrections, 0)

    def channel_band(band, _):
        span = pl.ds(pl.multiple_of(band * 16, 16), 16)
        weights = [mix_ref[tap, span] for tap in range(7)]

        def some_rows(index, _):
            for at in range(GROUP):
                spot = index * GROUP + at
                row = rows_ref[1 + spot]
                terms = []
                for tap in range(7):
                    wave = wave_ref[row + tap, span]
                    terms.append(wave[:, :LANES] * weights[tap][:, :LANES])
                    terms.append(wave[:, LANES:] * weights[tap][:, LANES:])
                while len(terms) > 1:
                    terms = [a + b for a, b in zip(terms[::2], terms[1::2])] + terms[len(terms) - len(terms) % 2:]
                prod_ref[spot, span] = terms[0]
            return 0

        lax.fori_loop(0, groups, some_rows, 0)
        return 0

    lax.fori_loop(0, width // 16, channel_band, 0)

    if last:
        held_ref[...] = jnp.zeros_like(held_ref)
    else:
        out_ref[...] = jnp.zeros_like(out_ref)
        low_ref[...] = jnp.zeros_like(low_ref)
        high_ref[...] = jnp.zeros_like(high_ref)

    def normalise(index, slot):
        rows = [rows_ref[1 + GROUP * index + at] for at in range(GROUP)]
        lane = lane_ids((width, LANES))
        joined = []
        for at, row in enumerate(rows):
            group = row // 32
            turn = lax.rem(LANES - 4 * (row % 32), LANES)
            left = pltpu.roll(edge_ref[0, group], turn, 1)
            right = pltpu.roll(edge_ref[1, group], lax.rem(turn + 4, LANES), 1)
            joined.append(jnp.concatenate([prod_ref[GROUP * index + at], jnp.where(lane < 4, left, right)], axis=1))
        depth = dot(jnp.concatenate(joined, axis=0), inverse_ref[...])
        for at in range(GROUP):
            real = depth[at * width:at * width + channels]
            center = jnp.mean(real, axis=0, keepdims=True)
            real = real - center
            spread = jnp.mean(real * real, axis=0, keepdims=True)
            normed = real * lax.rsqrt(spread + 1e-06) * gain_ref[...]
            normed = jnp.concatenate([normed, jnp.ones((width - channels, LANES), F32)], axis=0).astype(BF16)
            normed_ref[slot, :, at * LANES:(at + 1) * LANES] = normed

    def pointwise(index, slot):
        half = dot(expand_ref[...], normed_ref[slot])
        half = half.astype(GELU)
        bend = jnp.tanh(half * (half * half * GELU(8.0 * 0.044715 * ROOT) + GELU(2.0 * ROOT)))
        hidden = (half + half * bend).astype(BF16)
        branch = dot(reduce_ref[...], hidden)
        for at in range(GROUP):
            row = rows_ref[1 + GROUP * index + at]
            value = branch[:, at * LANES:(at + 1) * LANES] + state_ref[row].astype(F32)
            if last:
                held_ref[pl.ds(row, channels, stride=height), :] = value[:channels]
            else:
                value = value.astype(BF16)
                out_ref[row] = value
                pack_edges(value, row, low_ref, high_ref)

    def mix(index, _):
        normalise(2 * index, 0)
        pointwise(2 * index, 0)
        normalise(2 * index + 1, 1)
        pointwise(2 * index + 1, 1)
        return 0

    @pl.when(count > 0)
    def _():
        lax.fori_loop(0, groups // 2, mix, 0)

    if last:
        def finish(index, _):
            out_ref[pl.ds(index * 8, 8)] = held_ref[pl.ds(index * 8 * height, 8 * height), :].astype(BF16).reshape(8, height, LANES)
            return 0

        lax.fori_loop(0, channels // 8, finish, 0)


GELU = jnp.bfloat16


def smem():
    return pl.BlockSpec(memory_space=pltpu.SMEM)


def vmem():
    return pl.BlockSpec(memory_space=pltpu.VMEM)


def run_stem(rows, inverse, arrived, table, weight, height, width):
    return pl.pallas_call(
        stem_kernel,
        out_shape=[
            jax.ShapeDtypeStruct((height, width, LANES), BF16),
            jax.ShapeDtypeStruct((2, width, LANES), BF16),
            jax.ShapeDtypeStruct((2, width, LANES), BF16),
        ],
        in_specs=[smem(), smem(), vmem(), vmem(), vmem()],
        out_specs=[vmem()] * 3,
        scratch_shapes=[
            pltpu.VMEM(arrived.shape, BF16),
        ],
        compiler_params=pltpu.CompilerParams(vmem_limit_bytes=VMEM_BYTES),
        name="stem",
    )(rows, inverse, arrived, table, weight)


def run_block(last, rows, flags, state, *arrays):
    height, width, _ = state.shape
    edge = jax.ShapeDtypeStruct((2, width, LANES), BF16)
    if last:
        out_shape = [jax.ShapeDtypeStruct((200, height, LANES), BF16)]
        extra = [pltpu.VMEM((200 * height, LANES), F32)]
    else:
        out_shape = [jax.ShapeDtypeStruct(state.shape, BF16), edge, edge]
        extra = []
    return pl.pallas_call(
        functools.partial(block_kernel, last),
        out_shape=out_shape,
        in_specs=[smem(), smem()] + [vmem()] * (1 + len(arrays)),
        out_specs=[vmem()] * len(out_shape),
        scratch_shapes=[
            pltpu.VMEM((height + 6, width, 2 * LANES), BF16),
            pltpu.VMEM((rows.shape[0] - 1, width, LANES), BF16),
            pltpu.VMEM((2, 2, width, LANES), BF16),
            pltpu.VMEM((2, 4, width, LANES), BF16),
            pltpu.VMEM((2, width, GROUP * LANES), BF16),
        ] + extra,
        compiler_params=pltpu.CompilerParams(vmem_limit_bytes=VMEM_BYTES),
        name="block",
    )(rows, flags, state, *arrays)


def wet_rows(wet, most):
    height = wet.shape[0]
    count = jnp.sum(wet)
    rank = jnp.cumsum(wet) - 1
    spot = jnp.minimum(jnp.arange(most), count - 1)
    hits = (rank[None, :] == spot[:, None]) & (wet[None, :] > 0)
    rows = jnp.sum(jnp.where(hits, jnp.arange(height)[None, :], 0), axis=1)
    return jnp.concatenate([count[None], rows]).astype(jnp.int32)


def block_weights(depth_weight, depth_bias, norm_gain, expand_weight, expand_bias, reduce_weight, width):
    channels = depth_weight.shape[0]
    spare = width - channels
    taps = jnp.pad(depth_weight, ((0, spare), (0, 0), (0, 0)))
    angle = 2.0 * np.pi * np.arange(HALF + 1)[None, :] * (np.arange(7)[:, None] - 3) / LANES
    cos, sin = np.cos(angle), np.sin(angle)
    real = np.concatenate([cos[:, :HALF], cos[:, HALF:], cos[:, 1:HALF]], axis=1)
    none = np.zeros((7, 1))
    imag = np.concatenate([none, -sin[:, 1:HALF], none, sin[:, 1:HALF]], axis=1)
    table = jnp.asarray(np.concatenate([real, imag], axis=1), F32)
    mix = jnp.einsum("cuv,vk->uck", taps, table, precision=lax.Precision.HIGHEST).astype(BF16)
    phase = np.arange(LANES) % 4
    left = np.stack([(phase + t <= 2) for t in range(3)]).astype(np.float32)
    right = np.stack([(phase >= t) & (phase <= 2) for t in range(3)]).astype(np.float32)
    by_tap = jnp.transpose(taps, (1, 2, 0))
    left_weight = (by_tap[:, :3, :, None] * left[None, :, None, :]).reshape(21, width, LANES).astype(BF16)
    right_weight = (by_tap[:, 6:3:-1, :, None] * right[None, :, None, :]).reshape(21, width, LANES).astype(BF16)
    bias = jnp.pad(depth_bias, (0, spare))
    high = bias.astype(BF16).astype(F32)
    bias = jnp.broadcast_to(jnp.stack([high, bias - high])[:, :, None], (2, width, LANES))
    gain = jnp.broadcast_to(norm_gain[:, None], (channels, LANES))
    half_bias = 0.5 * expand_bias
    high = half_bias.astype(BF16)
    low = (half_bias - high.astype(F32)).astype(BF16)
    expand = jnp.concatenate(
        [(expand_weight.T * BF16(0.5)), high[:, None], low[:, None], jnp.zeros((expand_weight.shape[1], spare - 2), BF16)], axis=1
    )
    reduce = jnp.pad(reduce_weight.T, ((0, spare), (0, 0)))
    return mix, left_weight, right_weight, bias, gain, expand, reduce


def body(
    atm_flux,
    owner_map,
    wet_mask,
    stem_weight,
    depth_weight,
    depth_bias,
    norm_gain,
    expand_weight,
    expand_bias,
    reduce_weight,
):
    lon_count = lax.axis_size("gx")
    lat_count = lax.axis_size("gy")
    lat_index = lax.axis_index("gy")
    channels = depth_weight.shape[1]
    width = (channels + 15) // 16 * 16
    height = wet_mask.shape[0]
    arrived = lax.all_to_all(atm_flux[0], ("gx", "gy"), split_axis=0, concat_axis=0, tiled=True)[:, 0]
    pieces = owner_map.shape[0]
    owner = owner_map[:, 0]
    inverse = jnp.sum(
        jnp.where(owner[None, :] == jnp.arange(pieces)[:, None], jnp.arange(pieces)[None, :], 0), axis=1
    ).astype(jnp.int32)
    rows = wet_rows(wet_mask[:, 0], 48)
    flags = (lat_index == lat_count - 1).astype(jnp.int32)[None]
    stem = jnp.transpose(stem_weight, (0, 2, 3, 1)).reshape(channels, -1)
    stem = jnp.pad(stem, ((0, width - channels), (0, 0)))
    forward, back = fourier_tables()
    flipped = jnp.asarray(forward[::-1], BF16)
    forward = jnp.asarray(forward, BF16)
    back = jnp.asarray(back, BF16)
    turn = jnp.asarray(fold_table(), BF16)
    state, low, high = run_stem(rows, inverse, arrived, jnp.asarray(deinterleave_table(), BF16), stem, height, width)
    east = [(i, (i + 1) % lon_count) for i in range(lon_count)]
    west = [(b, a) for a, b in east]
    up = [(i, i + 1) for i in range(lat_count - 1)]
    down = [(b, a) for a, b in up]
    top = lat_count - 1
    over = [(i * lat_count + top, (lon_count - 1 - i) * lat_count + top) for i in range(lon_count)]
    blocks = depth_weight.shape[0]
    for index in range(blocks):
        last = index == blocks - 1
        mix, left_weight, right_weight, bias, gain, expand, reduce = block_weights(
            depth_weight[index], depth_bias[index], norm_gain[index], expand_weight[index], expand_bias[index],
            reduce_weight[index], width,
        )
        left = lax.ppermute(high, "gx", east) - high
        right = lax.ppermute(low, "gx", west) - low
        upper = jnp.concatenate([state[height - 3:], left[1:], right[1:]])
        lower = jnp.concatenate([state[:3], left[:1], right[:1]])
        south = lax.ppermute(upper, "gy", up)
        north = lax.ppermute(lower, "gy", down)
        mirrored = lax.ppermute(upper, ("gx", "gy"), over)
        out = run_block(
            last, rows, flags, state, south, north, mirrored, left, right, mix, forward, flipped, back, turn,
            left_weight, right_weight, bias, gain, expand, reduce,
        )
        if last:
            return out[0]
        state, low, high = out


def solution(mesh):
    return jax.shard_map(
        body,
        mesh=mesh,
        in_specs=(
            P(("gx", "gy"), None, None, None, None),
            P(None, ("gx", "gy")),
            P("gy", "gx"),
            P(),
            P(),
            P(),
            P(),
            P(),
            P(),
            P(),
        ),
        out_specs=P(None, "gy", "gx"),
        check_vma=False,
    )
```

time: 516 us -> 159 us (0.31)
  the two profiles are of different devices: /device:TPU:0 before, /device:TPU:7 now
where the time goes in v1:
time: 159 us; the launch traced here: 157 us
  Pallas kernels  67.7 us (43%)
  starting transfers between devices  37.1 us (23%)
  local copies, waits for them, and re-layouts  21.1 us (13%)
  other arithmetic  19.5 us (12%)
  waiting for transfers between devices  5.81 us (4%)
  matrix products  4.56 us (3%)
    pallas_call x2, Pallas kernels, run_block(): pl.pallas_call(functools.partial(block_kernel, last), out_shape=out_shape...  59.8 us
    all_to_all x1, starting transfers between devices, body(): lax.all_to_all(atm_flux[0], ('gx', 'gy'), split_axis=0, concat_axis=0, ti...  10.8 us
    ppermute x2, starting transfers between devices, body(): mirrored = lax.ppermute(upper, ('gx', 'gy'), over)  10.8 us
    ppermute x2, starting transfers between devices, body(): right = lax.ppermute(low, 'gx', west) - low  9 us
    pallas_call x1, Pallas kernels, run_stem(): pl.pallas_call(stem_kernel, out_shape=[jax.ShapeDtypeStruct((height, widt...  7.92 us
    ppermute x2, waiting for transfers between devices, body(): left = lax.ppermute(high, 'gx', east) - high  4.64 us
    convert_element_type x1, other arithmetic, block_weights(): (by_tap[:, 6:3:-1, :, None] * right[None, :, None, :]).reshape(21, width,...  4.59 us
    dot_general x2, matrix products, block_weights(): jnp.einsum('cuv,vk->uck', taps, table, precision=lax.Precision.HIGHEST)  4.56 us
  transfers between devices with their start and end apart: 11, of which 4 were waited for; matrix products, arithmetic and copies ran while one was open for 24% of the time, Pallas kernels for 0%

profile of v1, /device:TPU:7, one launch (start us, length us, event | category | flops | bytes accessed | tf_op | source)
XLA Modules:
  0.0 157.0 jit_solution(16594431559822801011)
XLA Ops:
  0.0 10.8 %all-to-all-start = ((bf16[128,1,16,256]{3,2,1,0:T(8,128)(2,1)}), bf16[128,1,16,256]{3,2,1,0:T(8,128)(2,1)S(1)}, u32[]{:S(2)}, u32[]{:S(2)}) async-start(bf16[128,1,16,256]{3,2,1,0:T(8,128)(2,1)} %bitcast.64), calls=%async_computation | async-start | bytes 2097152 | tf_op jit(solution)/shard_map/all_to_all | solution.py:380
  13.0 1.4 fusion.9
  16.8 2.3 %fusion.mix_ref = bf16[7,208,256]{2,1,0:T(8,128)(2,1)} fusion(f32[7,256,1]{1,0,2:T(8,128)S(1)} %copy-done.25, f32[200,7,7]{0,2,1:T(8,128)S(1)} %bitcast.68), kind=kOutput, calls=%fused_computation.6 | convolution fusion | flops 31682560 | bytes 791840 | tf_op jit(solution)/shard_map/cuv,vk->uck/dot_general | solution.py:341
  19.1 1.0 slice_bitcast_fusion
  22.0 1.3 pad_add_fusion.rows_ref
  23.7 1.0 copy.71
  24.7 1.0 copy.72
  29.0 1.4 mul.159
  32.2 1.4 select_reduce_fusion.inverse_ref
  33.6 1.2 subtract_convert_fusion
  34.9 4.6 %multiply_convert_fusion = (bf16[21,208,128]{2,1,0:T(8,128)(2,1)}, bf16[21,208,128]{2,1,0:T(8,128)(2,1)}, bf16[21,208,128]{2,1,0:T(8,128)(2,1)}, bf16[21,208,128]{2,1,0:T(8,128)(2,1)}) fusion(f32[21,208]{1,0:T(8,128)S(1)} %copy-done.20, f32[21,128]{1,0:T(8,128)S(1)} %copy-done.24, f32[21,208]{1,0:T(8,128)S(1)} %copy-done.19, f32[21,128]{1,0:T(8,128)S(1)} %copy-done.23, ...), kind=kLoop, calls=%fused_computation | loop fusion | flops 4472832 | bytes 4564224 | tf_op jit(solution)/shard_map/convert_element_type | solution.py:347
  39.5 1.0 copy-done
  40.5 7.9 %stem.1 = (bf16[64,208,128]{2,1,0:T(8,128)(2,1)}, bf16[2,208,128]{2,1,0:T(8,128)(2,1)}, bf16[2,208,128]{2,1,0:T(8,128)(2,1)}) custom-call(s32[49]{0:T(128)} %pad_add_fusion.rows_ref, s32[128]{0:T(128)} %select_reduce_fusion.inverse_ref, bf16[128,16,256]{2,1,0:T(8,128)(2,1)} %bitcast.63, bf16[256,256]{1,0:T(8,128)(2,1)} %constant.46.clone.table_ref, ...), custom_call_target="tpu_custom_call" | custom-call | tf_op jit(solution)/shard_map/stem/pallas_call | solution.py:278
  48.5 1.2 collective-permute-start
  49.7 4.2 %collective-permute-start.1 = (bf16[2,208,128]{2,1,0:T(8,128)(2,1)}, bf16[2,208,128]{2,1,0:T(8,128)(2,1)S(1)}, u32[]{:S(2)}, u32[]{:S(2)}) collective-permute-start(bf16[2,208,128]{2,1,0:T(8,128)(2,1)} %get-tuple-element.13), channel_id=1, source_target_pairs={{8,0},{16,8},{24,16},{32,24},{40,32},{48,40},{56,48},{64,56},{72,6... | collective-permute-start | bytes 319496 | tf_op jit(solution)/shard_map/ppermute | solution.py:410
  53.9 1.0 fusion.11
  54.9 2.2 %collective-permute-done = bf16[2,208,128]{2,1,0:T(8,128)(2,1)S(1)} collective-permute-done((bf16[2,208,128]{2,1,0:T(8,128)(2,1)}, bf16[2,208,128]{2,1,0:T(8,128)(2,1)S(1)}, u32[]{:S(2)}, u32[]{:S(2)}) %collective-permute-start) | collective-permute-done | bytes 106528 | tf_op jit(solution)/shard_map/ppermute | solution.py:409
  58.1 0.9 sub.51.right_ref
  59.9 1.4 collective-permute-start.2
  61.3 5.4 %collective-permute-start.4 = (bf16[5,208,128]{2,1,0:T(8,128)(2,1)}, bf16[5,208,128]{2,1,0:T(8,128)(2,1)S(1)}, u32[]{:S(2)}, u32[]{:S(2)}) collective-permute-start(bf16[5,208,128]{2,1,0:T(8,128)(2,1)} %pad_maximum_fusion), channel_id=1, source_target_pairs={{7,127},{15,119},{23,111},{31,103},{39,95},{47,87},{55,79},{63,71}... | collective-permute-start | bytes 798728 | tf_op jit(solution)/shard_map/ppermute | solution.py:415
  67.4 1.3 collective-permute-start.3
  70.0 1.4 maximum_maximum_fusion.1
  73.6 28.0 %block.2 = (bf16[64,208,128]{2,1,0:T(8,128)(2,1)}, bf16[2,208,128]{2,1,0:T(8,128)(2,1)}, bf16[2,208,128]{2,1,0:T(8,128)(2,1)}) custom-call(s32[49]{0:T(128)} %pad_add_fusion.rows_ref, s32[1]{0:T(128)} %bitcast.2.flags_ref, bf16[64,208,128]{2,1,0:T(8,128)(2,1)} %get-tuple-element.11.state_ref, bf16[5,208,128]{2,1,0:T(8,128)(2,1)} %copy-done.14, ...), custom_call_target="tpu_custom_call" | custom-call | tf_op jit(solution)/shard_map/block/pallas_call | solution.py:304
  101.7 4.8 %collective-permute-start.6 = (bf16[2,208,128]{2,1,0:T(8,128)(2,1)}, bf16[2,208,128]{2,1,0:T(8,128)(2,1)S(1)}, u32[]{:S(2)}, u32[]{:S(2)}) collective-permute-start(bf16[2,208,128]{2,1,0:T(8,128)(2,1)} %get-tuple-element.16), channel_id=1, source_target_pairs={{8,0},{16,8},{24,16},{32,24},{40,32},{48,40},{56,48},{64,56},{72,6... | collective-permute-start | bytes 319496 | tf_op jit(solution)/shard_map/ppermute | solution.py:410
  106.5 1.0 fusion.10
  107.5 2.4 %collective-permute-done.5 = bf16[2,208,128]{2,1,0:T(8,128)(2,1)S(1)} collective-permute-done((bf16[2,208,128]{2,1,0:T(8,128)(2,1)}, bf16[2,208,128]{2,1,0:T(8,128)(2,1)S(1)}, u32[]{:S(2)}, u32[]{:S(2)}) %collective-permute-start.5) | collective-permute-done | bytes 106528 | tf_op jit(solution)/shard_map/ppermute | solution.py:409
  110.8 1.0 sub.55.right_ref
  111.9 1.3 collective-permute-start.7
  113.2 5.4 %collective-permute-start.9 = (bf16[5,208,128]{2,1,0:T(8,128)(2,1)S(1)}, bf16[5,208,128]{2,1,0:T(8,128)(2,1)S(1)}, u32[]{:S(2)}, u32[]{:S(2)}) collective-permute-start(bf16[5,208,128]{2,1,0:T(8,128)(2,1)S(1)} %pad_maximum_fusion.2), channel_id=1, source_target_pairs={{7,127},{15,119},{23,111},{31,103},{39,95},{47,87},{55,79},{63,71}... | collective-permute-start | bytes 798728 | tf_op jit(solution)/shard_map/ppermute | solution.py:415
  118.6 1.3 collective-permute-start.8
  120.7 2.3 %fusion.1.mix_ref = bf16[7,208,256]{2,1,0:T(8,128)(2,1)} fusion(f32[7,256,1]{1,0,2:T(8,128)S(1)} %copy-done.26, f32[200,7,7]{0,2,1:T(8,128)S(1)} %bitcast.66), kind=kOutput, calls=%fused_computation.7 | convolution fusion | flops 31682560 | bytes 791840 | tf_op jit(solution)/shard_map/cuv,vk->uck/dot_general | solution.py:341
  125.2 31.8 %block.3 = bf16[200,64,128]{2,1,0:T(8,128)(2,1)} custom-call(s32[49]{0:T(128)} %pad_add_fusion.rows_ref, s32[1]{0:T(128)} %bitcast.2.flags_ref, bf16[64,208,128]{2,1,0:T(8,128)(2,1)} %get-tuple-element.14.state_ref, bf16[5,208,128]{2,1,0:T(8,128)(2,1)} %copy-done.11, bf16[5,208,128]{2,1,0:T(8,128)(2,1)} %copy-done.13, bf16[5,208,128]{2,1,0:T(8,128)(2,1)} %copy-done.12, ...), custom_call_target="tpu_custom_call" | custom-call | tf_op jit(solution)/shard_map/block/pallas_call | solution.py:304
  (147 shorter events, 21.4 us)
Async XLA Ops:
  0.0 14.5 %copy-start.38 = (s32[64,1]{0,1:T(1,128)S(1)}, s32[64,1]{0,1:T(1,128)}, u32[]{:S(2)}) copy-start(s32[64,1]{0,1:T(1,128)} %param.23) | copy-start | bytes 772
  0.0 14.4 %copy-start.7 = (bf16[2,200,800]{2,1,0:T(8,128)(2,1)S(1)}, bf16[2,200,800]{2,1,0:T(8,128)(2,1)}, u32[]{:S(2)}) copy-start(bf16[2,200,800]{2,1,0:T(8,128)(2,1)} %param.28) | copy-start | bytes 1920004
  0.0 16.0 %copy-start.18 = (f32[2,200,7,7]{1,0,3,2:T(2,128)S(1)}, f32[2,200,7,7]{1,0,3,2:T(2,128)}, u32[]{:S(2)}) copy-start(f32[2,200,7,7]{1,0,3,2:T(2,128)} %param.25) | copy-start | bytes 235204
  0.0 16.8 %copy-start.25 = (f32[7,256,1]{1,0,2:T(8,128)S(1)}, f32[7,256,1]{1,0,2:T(8,128)}, u32[]{:S(2)}) copy-start(f32[7,256,1]{1,0,2:T(8,128)} %constant.69) | copy-start | bytes 21508
  0.0 19.1 %copy-start.8 = (bf16[2,800,200]{1,2,0:T(8,128)(2,1)S(1)}, bf16[2,800,200]{1,2,0:T(8,128)(2,1)}, u32[]{:S(2)}) copy-start(bf16[2,800,200]{1,2,0:T(8,128)(2,1)} %param.30) | copy-start | bytes 1920004
  0.0 39.5 %all-to-all-start = ((bf16[128,1,16,256]{3,2,1,0:T(8,128)(2,1)}), bf16[128,1,16,256]{3,2,1,0:T(8,128)(2,1)S(1)}, u32[]{:S(2)}, u32[]{:S(2)}) async-start(bf16[128,1,16,256]{3,2,1,0:T(8,128)(2,1)} %bitcast.64), calls=%async_computation | async-start | bytes 2097152 | tf_op jit(solution)/shard_map/all_to_all | solution.py:380
  20.1 10.9 %copy-start.36 = (f32[3,128]{1,0:T(4,128)S(1)}, f32[3,128]{1,0:T(4,128)}, u32[]{:S(2)}) copy-start(f32[3,128]{1,0:T(4,128)} %constant.68) | copy-start | bytes 4612
  39.5 29.2 %copy-start.30 = (f32[1,200]{1,0:T(1,128)S(1)}, f32[1,200]{1,0:T(1,128)}, u32[]{:S(2)}) copy-start(f32[1,200]{1,0:T(1,128)} %copy-done.29) | copy-start | bytes 2404
  39.5 29.2 %copy-start.28 = (bf16[800,1]{0,1:T(2,128)(2,1)S(1)}, bf16[800,1]{0,1:T(2,128)(2,1)}, u32[]{:S(2)}) copy-start(bf16[800,1]{0,1:T(2,128)(2,1)} %get-tuple-element.45) | copy-start | bytes 4804
  39.5 29.4 %copy-start.27 = (bf16[800,1]{0,1:T(2,128)(2,1)S(1)}, bf16[800,1]{0,1:T(2,128)(2,1)}, u32[]{:S(2)}) copy-start(bf16[800,1]{0,1:T(2,128)(2,1)} %get-tuple-element.43) | copy-start | bytes 4804
  39.5 29.6 %copy-start.2 = (bf16[200,800]{1,0:T(8,128)(2,1)S(1)}, bf16[200,800]{1,0:T(8,128)(2,1)}, u32[]{:S(2)}) copy-start(bf16[200,800]{1,0:T(8,128)(2,1)} %get-tuple-element.22) | copy-start | bytes 960004
  48.5 8.7 %collective-permute-start = (bf16[2,208,128]{2,1,0:T(8,128)(2,1)}, bf16[2,208,128]{2,1,0:T(8,128)(2,1)S(1)}, u32[]{:S(2)}, u32[]{:S(2)}) collective-permute-start(bf16[2,208,128]{2,1,0:T(8,128)(2,1)} %get-tuple-element.12), channel_id=1, source_target_pairs={{0,8},{8,16},{16,24},{24,32},{32,40},{40,48},{48,56},{56,64},{64,7... | collective-permute-start | bytes 319496 | tf_op jit(solution)/shard_map/ppermute | solution.py:409
  49.7 8.5 %collective-permute-start.1 = (bf16[2,208,128]{2,1,0:T(8,128)(2,1)}, bf16[2,208,128]{2,1,0:T(8,128)(2,1)S(1)}, u32[]{:S(2)}, u32[]{:S(2)}) collective-permute-start(bf16[2,208,128]{2,1,0:T(8,128)(2,1)} %get-tuple-element.13), channel_id=1, source_target_pairs={{8,0},{16,8},{24,16},{32,24},{40,32},{48,40},{56,48},{64,56},{72,6... | collective-permute-start | bytes 319496 | tf_op jit(solution)/shard_map/ppermute | solution.py:410
  58.1 13.3 %copy-start.3 = (bf16[2,208,128]{2,1,0:T(8,128)(2,1)}, bf16[2,208,128]{2,1,0:T(8,128)(2,1)S(1)}, u32[]{:S(2)}) copy-start(bf16[2,208,128]{2,1,0:T(8,128)(2,1)S(1)} %sub.50.left_ref) | copy-start | bytes 319492
  59.1 12.3 %copy-start.4 = (bf16[2,208,128]{2,1,0:T(8,128)(2,1)}, bf16[2,208,128]{2,1,0:T(8,128)(2,1)S(1)}, u32[]{:S(2)}) copy-start(bf16[2,208,128]{2,1,0:T(8,128)(2,1)S(1)} %sub.51.right_ref) | copy-start | bytes 319492
  59.1 12.9 %copy-start.31 = (f32[2,208]{1,0:T(2,128)S(1)}, f32[2,208]{1,0:T(2,128)}, u32[]{:S(2)}) copy-start(f32[2,208]{1,0:T(2,128)} %pad_maximum_fusion.4) | copy-start | bytes 4996
  59.8 13.0 %copy-start.33 = (f32[1,200]{1,0:T(1,128)S(1)}, f32[1,200]{1,0:T(1,128)}, u32[]{:S(2)}) copy-start(f32[1,200]{1,0:T(1,128)} %get-tuple-element.50) | copy-start | bytes 2404
  59.9 11.6 %collective-permute-start.2 = (bf16[5,208,128]{2,1,0:T(8,128)(2,1)}, bf16[5,208,128]{2,1,0:T(8,128)(2,1)S(1)}, u32[]{:S(2)}, u32[]{:S(2)}) collective-permute-start(bf16[5,208,128]{2,1,0:T(8,128)(2,1)} %pad_maximum_fusion), channel_id=1, source_target_pairs={{0,1},{1,2},{2,3},{3,4},{4,5},{5,6},{6,7},{8,9},{9,10},{10,11},{11... | collective-permute-start | bytes 798728 | tf_op jit(solution)/shard_map/ppermute | solution.py:413
  61.3 10.7 %collective-permute-start.4 = (bf16[5,208,128]{2,1,0:T(8,128)(2,1)}, bf16[5,208,128]{2,1,0:T(8,128)(2,1)S(1)}, u32[]{:S(2)}, u32[]{:S(2)}) collective-permute-start(bf16[5,208,128]{2,1,0:T(8,128)(2,1)} %pad_maximum_fusion), channel_id=1, source_target_pairs={{7,127},{15,119},{23,111},{31,103},{39,95},{47,87},{55,79},{63,71}... | collective-permute-start | bytes 798728 | tf_op jit(solution)/shard_map/ppermute | solution.py:415
  67.4 4.6 %collective-permute-start.3 = (bf16[5,208,128]{2,1,0:T(8,128)(2,1)}, bf16[5,208,128]{2,1,0:T(8,128)(2,1)S(1)}, u32[]{:S(2)}, u32[]{:S(2)}) collective-permute-start(bf16[5,208,128]{2,1,0:T(8,128)(2,1)} %pad_maximum_fusion.1), channel_id=1, source_target_pairs={{1,0},{2,1},{3,2},{4,3},{5,4},{6,5},{7,6},{9,8},{10,9},{11,10},{12... | collective-permute-start | bytes 798728 | tf_op jit(solution)/shard_map/ppermute | solution.py:414
  101.6 18.3 %copy-start.34 = (f32[208]{0:T(256)S(1)}, f32[208]{0:T(256)}, u32[]{:S(2)}) copy-start(f32[208]{0:T(256)} %fusion.5) | copy-start | bytes 2500
  101.6 18.4 %copy-start.1 = (bf16[200,800]{1,0:T(8,128)(2,1)S(1)}, bf16[200,800]{1,0:T(8,128)(2,1)}, u32[]{:S(2)}) copy-start(bf16[200,800]{1,0:T(8,128)(2,1)} %get-tuple-element.21) | copy-start | bytes 960004
  101.6 19.1 %copy-start.10 = (f32[1,200,7,7]{1,3,2,0:T(8,128)S(1)}, f32[1,200,7,7]{1,3,2,0:T(8,128)}, u32[]{:S(2)}) copy-start(f32[1,200,7,7]{1,3,2,0:T(8,128)} %copy-done.9) | copy-start | bytes 117604
  101.6 19.1 %copy-start.26 = (f32[7,256,1]{1,0,2:T(8,128)S(1)}, f32[7,256,1]{1,0,2:T(8,128)}, u32[]{:S(2)}) copy-start(f32[7,256,1]{1,0,2:T(8,128)} %constant.69) | copy-start | bytes 21508
  101.6 8.3 %collective-permute-start.5 = (bf16[2,208,128]{2,1,0:T(8,128)(2,1)}, bf16[2,208,128]{2,1,0:T(8,128)(2,1)S(1)}, u32[]{:S(2)}, u32[]{:S(2)}) collective-permute-start(bf16[2,208,128]{2,1,0:T(8,128)(2,1)} %get-tuple-element.15), channel_id=1, source_target_pairs={{0,8},{8,16},{16,24},{24,32},{32,40},{40,48},{48,56},{56,64},{64,7... | collective-permute-start | bytes 319496 | tf_op jit(solution)/shard_map/ppermute | solution.py:409
  101.7 9.1 %collective-permute-start.6 = (bf16[2,208,128]{2,1,0:T(8,128)(2,1)}, bf16[2,208,128]{2,1,0:T(8,128)(2,1)S(1)}, u32[]{:S(2)}, u32[]{:S(2)}) collective-permute-start(bf16[2,208,128]{2,1,0:T(8,128)(2,1)} %get-tuple-element.16), channel_id=1, source_target_pairs={{8,0},{16,8},{24,16},{32,24},{40,32},{48,40},{56,48},{64,56},{72,6... | collective-permute-start | bytes 319496 | tf_op jit(solution)/shard_map/ppermute | solution.py:410
  106.5 18.0 %copy-start.32 = (f32[1,200]{1,0:T(1,128)S(1)}, f32[1,200]{1,0:T(1,128)}, u32[]{:S(2)}) copy-start(f32[1,200]{1,0:T(1,128)} %get-tuple-element.49) | copy-start | bytes 2404
  110.8 14.4 %copy-start.5 = (bf16[2,208,128]{2,1,0:T(8,128)(2,1)}, bf16[2,208,128]{2,1,0:T(8,128)(2,1)S(1)}, u32[]{:S(2)}) copy-start(bf16[2,208,128]{2,1,0:T(8,128)(2,1)S(1)} %sub.54.left_ref) | copy-start | bytes 319492
  111.8 13.4 %copy-start.6 = (bf16[2,208,128]{2,1,0:T(8,128)(2,1)}, bf16[2,208,128]{2,1,0:T(8,128)(2,1)S(1)}, u32[]{:S(2)}) copy-start(bf16[2,208,128]{2,1,0:T(8,128)(2,1)S(1)} %sub.55.right_ref) | copy-start | bytes 319492
  111.9 11.1 %collective-permute-start.7 = (bf16[5,208,128]{2,1,0:T(8,128)(2,1)S(1)}, bf16[5,208,128]{2,1,0:T(8,128)(2,1)S(1)}, u32[]{:S(2)}, u32[]{:S(2)}) collective-permute-start(bf16[5,208,128]{2,1,0:T(8,128)(2,1)S(1)} %pad_maximum_fusion.2), channel_id=1, source_target_pairs={{0,1},{1,2},{2,3},{3,4},{4,5},{5,6},{6,7},{8,9},{9,10},{10,11},{11... | collective-permute-start | bytes 798728 | tf_op jit(solution)/shard_map/ppermute | solution.py:413
  113.2 10.5 %collective-permute-start.9 = (bf16[5,208,128]{2,1,0:T(8,128)(2,1)S(1)}, bf16[5,208,128]{2,1,0:T(8,128)(2,1)S(1)}, u32[]{:S(2)}, u32[]{:S(2)}) collective-permute-start(bf16[5,208,128]{2,1,0:T(8,128)(2,1)S(1)} %pad_maximum_fusion.2), channel_id=1, source_target_pairs={{7,127},{15,119},{23,111},{31,103},{39,95},{47,87},{55,79},{63,71}... | collective-permute-start | bytes 798728 | tf_op jit(solution)/shard_map/ppermute | solution.py:415
  118.6 4.4 %collective-permute-start.8 = (bf16[5,208,128]{2,1,0:T(8,128)(2,1)S(1)}, bf16[5,208,128]{2,1,0:T(8,128)(2,1)S(1)}, u32[]{:S(2)}, u32[]{:S(2)}) collective-permute-start(bf16[5,208,128]{2,1,0:T(8,128)(2,1)S(1)} %pad_maximum_fusion.3), channel_id=1, source_target_pairs={{1,0},{2,1},{3,2},{4,3},{5,4},{6,5},{7,6},{9,8},{10,9},{11,10},{12... | collective-permute-start | bytes 798728 | tf_op jit(solution)/shard_map/ppermute | solution.py:414
  (18 other events, 79.2 us)

commit v2 on v1

v2 whole, which is shorter than its diff:
```python
import functools

import jax
import jax.numpy as jnp
import numpy as np
from jax import lax
from jax.experimental import pallas as pl
from jax.experimental.pallas import tpu as pltpu
from jax.sharding import PartitionSpec as P

LANES = 128
GROUP = 8
HALF = LANES // 2
ROOT = float(np.sqrt(2.0 / np.pi))
BF16 = jnp.bfloat16
F32 = jnp.float32


def fourier_tables():
    spot = np.arange(LANES)[:, None]
    wave = np.arange(HALF)[None, :]
    angle = 2.0 * np.pi * (spot * wave % LANES) / LANES
    cos, sin = np.cos(angle), np.sin(angle)
    plain = np.concatenate([cos, -sin], axis=1)
    plain[:, HALF] = np.where(np.arange(LANES) % 2 == 0, 1.0, -1.0)
    swapped = np.concatenate([-sin, cos], axis=1)
    swapped[:, 0] = 0.0
    swapped[:, HALF] = 0.0
    forward = np.concatenate([plain, swapped], axis=1)
    inverse = plain.T * (2.0 / LANES)
    inverse[0] /= 2.0
    inverse[HALF] /= 2.0
    edges = np.zeros((LANES, LANES))
    for j in range(3):
        edges[j, j] = 1.0
        edges[4 + j, LANES - 3 + j] = 1.0
    edges[3, :] = 1.0
    edges[7, :] = 1.0
    inverse = np.concatenate([inverse, edges], axis=0)
    return forward, inverse


def deinterleave_table():
    table = np.zeros((2 * LANES, 2 * LANES))
    spot = np.arange(LANES)
    table[2 * spot, spot] = 1.0
    table[2 * spot + 1, LANES + spot] = 1.0
    return table


def fold_table():
    table = np.zeros((LANES, LANES))
    spot = np.arange(LANES - 1)
    table[LANES - 2 - spot, spot] = 1.0
    return table


def dot(left, right):
    return jnp.dot(left, right, preferred_element_type=F32)


def lane_ids(shape):
    return lax.broadcasted_iota(jnp.int32, shape, len(shape) - 1)


def pack_edges(value, row, low_ref, high_ref):
    place = (row + 16) % 64
    group = place // 32
    start = 4 * (place % 32)
    lane = lane_ids(value.shape)
    hit = (lane >= start) & (lane < start + 3)
    low = pltpu.roll(value, start, 1)
    high = pltpu.roll(value, lax.rem(start + 3, LANES), 1)
    low_ref[group] = jnp.where(hit, low, low_ref[group])
    high_ref[group] = jnp.where(hit, high, high_ref[group])


def send_edges(flags_ref, state_ref, low_ref, high_ref, row_refs, column_refs):
    height = state_ref.shape[0]
    even_row = flags_ref[0] == 0
    even_column = flags_ref[1] == 0
    row_refs[0][...] = state_ref[pl.ds(jnp.where(even_row, height - 3, 0), 3)]
    row_refs[1][...] = state_ref[pl.ds(jnp.where(even_row, 0, height - 3), 3)]
    column_refs[0][...] = jnp.where(even_column, high_ref[...], low_ref[...])
    column_refs[1][...] = jnp.where(even_column, low_ref[...], high_ref[...])


def prepare_kernel(blocks, coef_ref, table_ref, *outs):
    for block in range(blocks):
        mix_ref, side_ref, gain_ref, bias_ref = outs[4 * block:4 * block + 4]
        coef = coef_ref[block]
        for tap in range(7):
            mix_ref[tap] = dot(coef, table_ref[:, tap * 256:(tap + 1) * 256]).astype(BF16)
        for pair in range(21):
            out = dot(coef, table_ref[:, 1792 + pair * 256:2048 + pair * 256]).astype(BF16)
            side_ref[2 * pair] = out[:, :LANES]
            side_ref[2 * pair + 1] = out[:, LANES:]
        out = dot(coef, table_ref[:, 7168:7552])
        gain_ref[...] = out[:, :LANES]
        bias_ref[0] = out[:, LANES:2 * LANES]
        bias_ref[1] = out[:, 2 * LANES:]


def prepare_table():
    table = np.zeros((160, 7552))
    angle = 2.0 * np.pi * np.arange(HALF + 1)[None, :] * (np.arange(7)[:, None] - 3) / LANES
    cos, sin = np.cos(angle), np.sin(angle)
    none = np.zeros((7, 1))
    real = np.concatenate([cos, cos[:, 1:HALF]], axis=1)
    imag = np.concatenate([none, -sin[:, 1:HALF], none, sin[:, 1:HALF]], axis=1)
    wave = np.concatenate([real, imag], axis=1)
    wave_high = wave.astype(BF16).astype(np.float64)
    phase = np.arange(LANES) % 4
    for row in range(7):
        for tap in range(7):
            spot = row * 7 + tap
            table[spot, row * 256:(row + 1) * 256] = wave_high[tap]
            table[49 + spot, row * 256:(row + 1) * 256] = wave_high[tap]
            table[98 + spot, row * 256:(row + 1) * 256] = wave[tap] - wave_high[tap]
        for tap in range(3):
            at = 1792 + (row * 3 + tap) * LANES
            for copy in (0, 49):
                table[copy + row * 7 + tap, at:at + LANES] = phase + tap <= 2
                table[copy + row * 7 + 6 - tap, at + 2688:at + 2688 + LANES] = (phase >= tap) & (phase <= 2)
    table[147:150, 7168:7296] = 1.0
    table[150, 7296:7424] = 1.0
    table[151, 7424:7552] = 1.0
    return table


def stem_kernel(rows_ref, flags_ref, inverse_ref, arrived_ref, table_ref, weight_ref, state_ref, row_even_ref,
                row_odd_ref, column_even_ref, column_odd_ref, split_ref, low_ref, high_ref):
    pieces = arrived_ref.shape[0]
    flux = arrived_ref.shape[1]
    step = 32

    def split(index, _):
        part = arrived_ref[pl.ds(index * step, step)].reshape(step * flux, 2 * LANES)
        split_ref[pl.ds(index * step, step)] = dot(part, table_ref[...]).astype(BF16).reshape(step, flux, 2 * LANES)
        return 0

    lax.fori_loop(0, pieces // step, split, 0)
    state_ref[...] = jnp.zeros_like(state_ref)
    low_ref[...] = jnp.zeros_like(low_ref)
    high_ref[...] = jnp.zeros_like(high_ref)

    def group(index, _):
        rows = [rows_ref[1 + GROUP * index + at] for at in range(GROUP)]
        columns = []
        for row in rows:
            one = split_ref[inverse_ref[2 * row]]
            two = split_ref[inverse_ref[2 * row + 1]]
            columns.append(jnp.concatenate([one[:, :LANES], one[:, LANES:], two[:, :LANES], two[:, LANES:]], axis=0))
        out = dot(weight_ref[...], jnp.concatenate(columns, axis=1))
        for at, row in enumerate(rows):
            value = out[:, at * LANES:(at + 1) * LANES].astype(BF16)
            state_ref[row] = value
            pack_edges(value, row, low_ref, high_ref)
        return 0

    @pl.when(rows_ref[0] > 0)
    def _():
        lax.fori_loop(0, MOST // GROUP, group, 0)

    send_edges(flags_ref, state_ref, low_ref, high_ref, (row_even_ref, row_odd_ref), (column_even_ref, column_odd_ref))


def transform_kernel(state_ref, forward_ref, wave_ref):
    rows, width, _ = state_ref.shape
    part = state_ref[...].reshape(rows * width, LANES)
    wave_ref[...] = dot(part, forward_ref[...]).astype(BF16).reshape(rows, width, 2 * LANES)


def tree_sum(terms):
    while len(terms) > 1:
        terms = [a + b for a, b in zip(terms[::2], terms[1::2])] + terms[len(terms) - len(terms) % 2:]
    return terms[0]


def product_kernel(first, rows_ref, wave_ref, mix_ref, after_ref, prod_ref, *rest):
    height, width, _ = wave_ref.shape
    if rest:
        rest[0][0:6] = wave_ref[0:6]
        rest[0][6:12] = wave_ref[height - 6:height]

    def channel_band(band, _):
        span = pl.ds(pl.multiple_of((band + first) * 16, 16), 16)
        target = pl.ds(pl.multiple_of(band * 16, 16), 16)
        weights = [mix_ref[tap, span] for tap in range(7)]

        def some_rows(index, _):
            for at in range(GROUP):
                spot = index * GROUP + at
                base = jnp.clip(rows_ref[1 + spot] - 3, 0, height - 7)
                terms = []
                for tap in range(7):
                    wave = wave_ref[base + tap, span]
                    terms.append(wave[:, :LANES] * weights[tap][:, :LANES])
                    terms.append(wave[:, LANES:] * weights[tap][:, LANES:])
                prod_ref[spot, target] = tree_sum(terms)
            return 0

        lax.fori_loop(0, MOST // GROUP, some_rows, 0)
        return 0

    lax.fori_loop(0, prod_ref.shape[1] // 16, channel_band, 0)


def block_kernel(last, block, rows_ref, flags_ref, state_ref, prod_one_ref, prod_two_ref, edge_wave_ref, row_even_ref, row_odd_ref,
                 column_even_ref, column_odd_ref, corner_even_ref, corner_odd_ref, own_even_ref, own_odd_ref,
                 mix_ref, side_ref, gain_ref, bias_ref, forward_ref, flipped_ref, inverse_ref, turn_ref, expand_ref,
                 reduce_ref, *rest):
    if last:
        out_ref, halo_ref, fix_ref, edge_ref, grid_ref, normed_ref, held_ref = rest
    else:
        (out_ref, send_row_even_ref, send_row_odd_ref, send_column_even_ref, send_column_odd_ref,
         halo_ref, fix_ref, edge_ref, grid_ref, normed_ref, low_ref, high_ref) = rest
    height, width, _ = state_ref.shape
    channels = 200
    pitch = height + 8
    count = rows_ref[0]
    even_row = flags_ref[0] == 0
    even_column = flags_ref[1] == 0
    fold = flags_ref[2] != 0

    def wave_of(rows, table):
        return dot(rows.reshape(3 * width, LANES), table).astype(BF16).reshape(3, width, 2 * LANES)

    left = jnp.where(even_column, column_odd_ref[...], column_even_ref[...])
    right = jnp.where(even_column, column_even_ref[...], column_odd_ref[...])
    low = jnp.where(even_column, own_odd_ref[...], own_even_ref[...])
    high = jnp.where(even_column, own_even_ref[...], own_odd_ref[...])
    grid_ref[0, 0:2] = left - high
    grid_ref[1, 0:2] = right - low
    halo_ref[0:3] = wave_of(jnp.where(even_row, row_odd_ref[...], row_even_ref[...]), forward_ref[...])
    for side in range(2):
        grid_ref[side, 2] = jnp.where(even_row, corner_odd_ref[side], corner_even_ref[side])

    @pl.when(jnp.logical_not(fold))
    def _():
        halo_ref[3:6] = wave_of(jnp.where(even_row, row_even_ref[...], row_odd_ref[...]), forward_ref[...])
        for side in range(2):
            grid_ref[side, 3] = jnp.where(even_row, corner_even_ref[side], corner_odd_ref[side])

    @pl.when(fold)
    def _():
        waves = wave_of(row_odd_ref[...], flipped_ref[...])
        for m in range(3):
            halo_ref[3 + m] = waves[2 - m]
        for side in range(2):
            grid_ref[side, 3] = dot(corner_odd_ref[1 - side], turn_ref[...]).astype(BF16)

    def corrections(index, _):
        span = pl.ds(pl.multiple_of(index * 16, 16), 16)
        lane = lane_ids((16, LANES))
        for side in range(2):
            totals = [jnp.where(lane % 4 == 3, bias_ref[side, span], 0.0)] * 2
            here, other = grid_ref[side, 0, span], grid_ref[side, 1, span]
            upward = jnp.where(lane < HALF, here, grid_ref[side, 3, span])
            downward = jnp.where(lane < HALF, grid_ref[side, 2, span], here)
            for tap_row in range(7):
                terms = [None, None]
                for tap in range(3):
                    shift = 4 * (tap_row - 3) + (tap if side == 0 else -tap)
                    weight = side_ref[(side * 7 + tap_row) * 3 + tap, span]

                    def moved(slab):
                        return pltpu.roll(slab, -shift % LANES, 1) if shift else slab

                    one, two = moved(here), moved(other)
                    if shift > 0:
                        first = jnp.where(lane < HALF, moved(upward), jnp.where(lane < LANES - shift, one, two))
                        second = jnp.where(lane < LANES - shift, two, one)
                    elif shift < 0:
                        first = jnp.where(lane >= HALF, moved(downward), jnp.where(lane >= -shift, one, two))
                        second = jnp.where(lane >= -shift, two, one)
                    else:
                        first, second = one, two
                    for group, value in enumerate((first, second)):
                        value = weight * value
                        terms[group] = value if terms[group] is None else terms[group] + value
                totals = [total + term.astype(F32) for total, term in zip(totals, terms)]
            for group in range(2):
                edge_ref[side, group, span] = totals[group].astype(BF16)
        return 0

    lax.fori_loop(0, width // 16, corrections, 0)

    def rim(band, _):
        span = pl.ds(pl.multiple_of(band * 16, 16), 16)
        weights = [mix_ref[tap, span] for tap in range(7)]
        for at in range(6):
            terms = []
            for tap in range(7):
                spot = (at if at < 3 else at - 3) + tap
                if at < 3:
                    wave = halo_ref[spot, span] if spot < 3 else edge_wave_ref[spot - 3, span]
                else:
                    wave = edge_wave_ref[6 + spot, span] if spot < 6 else halo_ref[spot - 3, span]
                terms.append(wave[:, :LANES] * weights[tap][:, :LANES])
                terms.append(wave[:, LANES:] * weights[tap][:, LANES:])
            fix_ref[at, span] = tree_sum(terms)
        return 0

    lax.fori_loop(0, width // 16, rim, 0)

    if last:
        held_ref[...] = jnp.zeros_like(held_ref)
    else:
        out_ref[...] = jnp.zeros_like(out_ref)
        low_ref[...] = jnp.zeros_like(low_ref)
        high_ref[...] = jnp.zeros_like(high_ref)

    def normalise(index, slot):
        lane = lane_ids((width, LANES))
        joined = []
        for at in range(GROUP):
            spot = GROUP * index + at
            row = rows_ref[1 + spot]
            place = (row + 16) % 64
            group = place // 32
            turn = lax.rem(LANES - 4 * (place % 32), LANES)
            left = pltpu.roll(edge_ref[0, group], turn, 1)
            right = pltpu.roll(edge_ref[1, group], lax.rem(turn + 4, LANES), 1)
            rim_row = (row < 3) | (row >= height - 3)
            fixed = fix_ref[jnp.clip(jnp.where(row < 3, row, row - (height - 6)), 0, 5)]
            prod = jnp.where(rim_row, fixed, jnp.concatenate([prod_one_ref[spot], prod_two_ref[spot]], axis=0))
            joined.append(jnp.concatenate([prod, jnp.where(lane < 4, left, right)], axis=1))
        depth = dot(jnp.concatenate(joined, axis=0), inverse_ref[...])
        for at in range(GROUP):
            real = depth[at * width:at * width + channels]
            center = jnp.mean(real, axis=0, keepdims=True)
            real = real - center
            spread = jnp.mean(real * real, axis=0, keepdims=True)
            normed = real * lax.rsqrt(spread + 1e-06) * gain_ref[0:channels]
            normed = jnp.concatenate([normed, jnp.ones((width - channels, LANES), F32)], axis=0).astype(BF16)
            normed_ref[slot, :, at * LANES:(at + 1) * LANES] = normed

    def pointwise(index, slot):
        half = dot(expand_ref[block], normed_ref[slot])
        half = half.astype(GELU)
        bend = jnp.tanh(half * (half * half * GELU(8.0 * 0.044715 * ROOT) + GELU(2.0 * ROOT)))
        hidden = (half + half * bend).astype(BF16)
        branch = dot(reduce_ref[block], hidden)
        for at in range(GROUP):
            row = rows_ref[1 + GROUP * index + at]
            value = branch[:, at * LANES:(at + 1) * LANES] + state_ref[row].astype(F32)
            if last:
                held_ref[pl.ds(row, channels, stride=pitch), :] = value[:channels]
            else:
                value = value.astype(BF16)
                out_ref[row] = value
                pack_edges(value, row, low_ref, high_ref)

    def mix(index, _):
        normalise(2 * index + 1, 1)
        pointwise(2 * index, 0)
        normalise(jnp.minimum(2 * index + 2, MOST // GROUP - 1), 0)
        pointwise(2 * index + 1, 1)
        return 0

    @pl.when(count > 0)
    def _():
        normalise(0, 0)
        lax.fori_loop(0, MOST // GROUP // 2, mix, 0)

    if last:
        def finish(index, _):
            out_ref[pl.ds(index * 8, 8)] = held_ref[pl.ds(index * 8 * pitch, 8 * pitch), :].reshape(8, pitch, LANES)[:, :height].astype(BF16)
            return 0

        lax.fori_loop(0, channels // 8, finish, 0)
    else:
        send_edges(flags_ref, out_ref, low_ref, high_ref, (send_row_even_ref, send_row_odd_ref),
                   (send_column_even_ref, send_column_odd_ref))


GELU = jnp.bfloat16
MOST = 48
EARLY = 7


def smem():
    return pl.BlockSpec(memory_space=pltpu.SMEM)


def vmem():
    return pl.BlockSpec(memory_space=pltpu.VMEM)


def shape(*dims, dtype=BF16):
    return jax.ShapeDtypeStruct(dims, dtype)


def params(mib):
    return pltpu.CompilerParams(vmem_limit_bytes=mib * 1024 * 1024)


def edge_shapes(width):
    return [shape(3, width, LANES), shape(3, width, LANES), shape(2, width, LANES), shape(2, width, LANES)]


def run_prepare(coef, table):
    blocks, width, _ = coef.shape
    one = [shape(7, width, 256), shape(42, width, LANES), shape(width, LANES, dtype=F32), shape(2, width, LANES, dtype=F32)]
    return pl.pallas_call(
        functools.partial(prepare_kernel, blocks),
        out_shape=one * blocks,
        in_specs=[vmem(), vmem()],
        out_specs=[vmem()] * (4 * blocks),
        compiler_params=params(24),
        cost_estimate=pl.CostEstimate(flops=2 * blocks * width * 160 * 7552, bytes_accessed=10_000_000, transcendentals=0),
        name="prepare",
    )(coef, table)


def run_stem(rows, flags, inverse, arrived, table, weight, height, width):
    return pl.pallas_call(
        stem_kernel,
        out_shape=[shape(height, width, LANES)] + edge_shapes(width),
        in_specs=[smem(), smem(), smem(), vmem(), vmem(), vmem()],
        out_specs=[vmem()] * 5,
        scratch_shapes=[
            pltpu.VMEM(arrived.shape, BF16),
            pltpu.VMEM((2, width, LANES), BF16),
            pltpu.VMEM((2, width, LANES), BF16),
        ],
        compiler_params=params(24),
        name="stem",
    )(rows, flags, inverse, arrived, table, weight)


def run_transform(state, forward):
    height, width, _ = state.shape
    return pl.pallas_call(
        transform_kernel,
        out_shape=shape(height, width, 2 * LANES),
        grid=(height // 16,),
        in_specs=[pl.BlockSpec((16, width, LANES), lambda i: (i, 0, 0)), pl.BlockSpec((LANES, 2 * LANES), lambda i: (0, 0))],
        out_specs=pl.BlockSpec((16, width, 2 * LANES), lambda i: (i, 0, 0)),
        compiler_params=params(24),
        cost_estimate=pl.CostEstimate(flops=2 * height * width * LANES * 256, bytes_accessed=10_000_000, transcendentals=0),
        name="transform",
    )(state, forward)


def run_product(rows, wave, mix, after, first, bands):
    _, width, _ = wave.shape
    edges = [shape(12, width, 2 * LANES)] if first else []
    return pl.pallas_call(
        functools.partial(product_kernel, first),
        out_shape=[shape(MOST, bands * 16, LANES)] + edges,
        in_specs=[smem(), vmem(), vmem(), pl.BlockSpec(memory_space=pl.ANY)],
        out_specs=[vmem()] * (1 + len(edges)),
        compiler_params=params(24),
        cost_estimate=pl.CostEstimate(flops=28 * MOST * bands * 16 * LANES, bytes_accessed=20_000_000, transcendentals=0),
        name="product",
    )(rows, wave, mix, after)


def corner_kernel(flags_ref, column_even_ref, column_odd_ref, own_even_ref, own_odd_ref, after_ref, corner_ref):
    even_column = flags_ref[1] == 0
    one = column_even_ref[0] - own_odd_ref[0]
    two = column_odd_ref[0] - own_even_ref[0]
    corner_ref[0] = jnp.where(even_column, two, one)
    corner_ref[1] = jnp.where(even_column, one, two)


def run_corner(flags, column_even, column_odd, own_even, own_odd, after):
    return pl.pallas_call(
        corner_kernel,
        out_shape=shape(*own_even.shape),
        in_specs=[smem()] + [vmem()] * 4 + [pl.BlockSpec(memory_space=pl.ANY)],
        out_specs=vmem(),
        compiler_params=params(16),
        cost_estimate=pl.CostEstimate(flops=1000, bytes_accessed=500_000, transcendentals=0),
        name="corner",
    )(flags, column_even, column_odd, own_even, own_odd, after)


def run_block(last, block, rows, flags, state, *arrays):
    height, width, _ = state.shape
    if last:
        out_shape = [shape(200, height, LANES)]
        extra = [pltpu.VMEM((200 * (height + 8), LANES), F32)]
    else:
        out_shape = [shape(height, width, LANES)] + edge_shapes(width)
        extra = [pltpu.VMEM((2, width, LANES), BF16)] * 2
    return pl.pallas_call(
        functools.partial(block_kernel, last, block),
        out_shape=out_shape,
        in_specs=[smem(), smem()] + [vmem()] * (1 + len(arrays)),
        out_specs=[vmem()] * len(out_shape),
        scratch_shapes=[
            pltpu.VMEM((6, width, 2 * LANES), BF16),
            pltpu.VMEM((6, width, LANES), BF16),
            pltpu.VMEM((2, 2, width, LANES), BF16),
            pltpu.VMEM((2, 4, width, LANES), BF16),
            pltpu.VMEM((2, width, GROUP * LANES), BF16),
        ] + extra,
        compiler_params=params(40),
        name="block",
    )(rows, flags, state, *arrays)


def wet_rows(wet):
    height = wet.shape[0]
    count = jnp.sum(wet)
    before = jnp.arange(height)[None, :] <= jnp.arange(height)[:, None]
    rank = jnp.sum(jnp.where(before, wet[None, :], 0), axis=1) - 1
    spot = jnp.minimum(jnp.arange(MOST), count - 1)
    hits = (rank[None, :] == spot[:, None]) & (wet[None, :] > 0)
    rows = jnp.sum(jnp.where(hits, jnp.arange(height)[None, :], 0), axis=1)
    return jnp.concatenate([count[None], rows]).astype(jnp.int32)


def split_high(value):
    high = value.astype(BF16)
    return high, value - high.astype(F32)


def coefficients(depth_weight, depth_bias, norm_gain, width):
    blocks, channels = depth_bias.shape
    taps, rest = split_high(depth_weight.reshape(blocks, channels, 49))
    gain_one, left = split_high(norm_gain[:, :, None])
    gain_two, left = split_high(left)
    bias_one, bias_left = split_high(depth_bias[:, :, None])
    parts = [taps, rest.astype(BF16), taps, gain_one, gain_two, left.astype(BF16), bias_one, bias_left.astype(BF16)]
    coef = jnp.concatenate(parts, axis=2)
    return jnp.pad(coef, ((0, 0), (0, width - channels), (0, 160 - coef.shape[2])))


def pointwise_weights(expand_weight, expand_bias, reduce_weight, width):
    blocks, channels, hidden = expand_weight.shape
    spare = width - channels
    high, low = split_high(0.5 * expand_bias[:, None, :])
    expand = jnp.concatenate(
        [expand_weight * BF16(0.5), high, low.astype(BF16), jnp.zeros((blocks, spare - 2, hidden), BF16)], axis=1
    )
    reduce = jnp.pad(reduce_weight, ((0, 0), (0, 0), (0, spare)))
    return jnp.transpose(expand, (0, 2, 1)), jnp.transpose(reduce, (0, 2, 1))


def body(
    atm_flux,
    owner_map,
    wet_mask,
    stem_weight,
    depth_weight,
    depth_bias,
    norm_gain,
    expand_weight,
    expand_bias,
    reduce_weight,
):
    lon_count = lax.axis_size("gx")
    lat_count = lax.axis_size("gy")
    lon_index = lax.axis_index("gx")
    lat_index = lax.axis_index("gy")
    blocks, channels = depth_bias.shape
    width = (channels + 15) // 16 * 16
    height = wet_mask.shape[0]
    arrived = lax.all_to_all(atm_flux[0], ("gx", "gy"), split_axis=0, concat_axis=0, tiled=True)[:, 0]
    pieces = owner_map.shape[0]
    owner = owner_map[:, 0]
    inverse = jnp.sum(
        jnp.where(owner[None, :] == jnp.arange(pieces)[:, None], jnp.arange(pieces)[None, :], 0), axis=1
    ).astype(jnp.int32)
    rows = wet_rows(wet_mask[:, 0])
    flags = jnp.stack([lat_index % 2, lon_index % 2, lat_index == lat_count - 1]).astype(jnp.int32)
    stem = jnp.transpose(stem_weight, (0, 2, 3, 1)).reshape(channels, -1)
    stem = jnp.pad(stem, ((0, width - channels), (0, 0)))
    forward, back = fourier_tables()
    flipped = jnp.asarray(forward[::-1], BF16)
    forward = jnp.asarray(forward, BF16)
    back = jnp.asarray(back, BF16)
    turn = jnp.asarray(fold_table(), BF16)
    coef = coefficients(depth_weight, depth_bias, norm_gain, width)
    prepared = run_prepare(coef, jnp.asarray(prepare_table(), BF16))
    expand, reduce = pointwise_weights(expand_weight, expand_bias, reduce_weight, width)
    arrived, prepared, expand, reduce = lax.optimization_barrier((arrived, prepared, expand, reduce))
    state, *edges = run_stem(
        rows, flags, inverse, arrived, jnp.asarray(deinterleave_table(), BF16), stem, height, width
    )
    lon_even = [(i, i ^ 1) for i in range(lon_count)]
    lon_odd = [(i, ((i - 1 ^ 1) + 1) % lon_count) for i in range(lon_count)]
    lat_even = [(i, i ^ 1) for i in range(lat_count)]
    top = lat_count - 1
    lat_odd = []
    for lon in range(lon_count):
        for lat in range(1, top):
            lat_odd.append((lon * lat_count + lat, lon * lat_count + (lat - 1 ^ 1) + 1))
        lat_odd.append((lon * lat_count + top, (lon_count - 1 - lon) * lat_count + top))
    for index in range(blocks):
        last = index == blocks - 1
        row_even, row_odd, own_even, own_odd = edges
        column_even = lax.ppermute(own_even, "gx", lon_even)
        column_odd = lax.ppermute(own_odd, "gx", lon_odd)
        row_even = lax.ppermute(row_even, "gy", lat_even)
        row_odd = lax.ppermute(row_odd, ("gx", "gy"), lat_odd)
        mix, side, gain, bias = prepared[4 * index:4 * index + 4]
        bands = width // 16
        wave = run_transform(state, forward)
        prod = run_product(rows, wave, mix, wave, 0, EARLY)
        corner = run_corner(flags, column_even, column_odd, own_even, own_odd, prod[0])
        corner_even = lax.ppermute(corner, "gy", lat_even)
        corner_odd = lax.ppermute(corner, ("gx", "gy"), lat_odd)
        prod += run_product(rows, wave, mix, corner, EARLY, bands - EARLY)
        out = run_block(
            last, index, rows, flags, state, *prod, row_even, row_odd, column_even, column_odd,
            corner_even, corner_odd, own_even, own_odd, mix, side, gain, bias, forward, flipped, back, turn,
            expand, reduce,
        )
        if last:
            return out[0]
        state, *edges = out


def solution(mesh):
    return jax.shard_map(
        body,
        mesh=mesh,
        in_specs=(
            P(("gx", "gy"), None, None, None, None),
            P(None, ("gx", "gy")),
            P("gy", "gx"),
            P(),
            P(),
            P(),
            P(),
            P(),
            P(),
            P(),
        ),
        out_specs=P(None, "gy", "gx"),
        check_vma=False,
    )
```

time: 159 us -> 119 us (0.75)
  other arithmetic: 19.5 us -> 3.08 us
  local copies, waits for them, and re-layouts: 21.1 us -> 11.5 us
  matrix products: 4.56 us -> 0 us
  Pallas kernels: 67.7 us -> 63.2 us
  waiting for transfers between devices: 5.81 us -> 2.27 us
    convert_element_type x5, other arithmetic: 7.76 us -> 0.1 us  [the longest x2 0.05 us: split_high(): high = value.astype(BF16)]
    mul x10 -> x0, local copies, waits for them, and re-layouts: 5.57 us -> none  [the longest x4 2.6 us: block_weights(): by_tap[:, :3, :, None] * left[None, :, None, :]]
    ppermute x10 -> x12, waiting for transfers between devices: 5.81 us -> 0.66 us  [the longest x2 0.63 us: body(): corner_odd = lax.ppermute(corner, ('gx', 'gy'), lat_odd)]
    pallas_call x3 -> x12, Pallas kernels: 67.7 us -> 63.2 us  [the longest x2 33.8 us: run_block(): pl.pallas_call(functools.partial(block_kernel, last, block), out_shape=ou...]
    dot_general x2 -> x0, matrix products: 4.56 us -> none  [block_weights(): jnp.einsum('cuv,vk->uck', taps, table, precision=lax.Precision.HIGHEST)]
    slice x12 -> x0, local copies, waits for them, and re-layouts: 4.2 us -> none  [the longest x6 2.06 us: body(): lower = jnp.concatenate([state[:3], left[:1], right[:1]])]
    unnamed x84 -> x58, local copies, waits for them, and re-layouts: 3.05 us -> 7.17 us
    sub x7 -> x1, other arithmetic: 3.87 us -> 0.01 us  [wet_rows(): rank = jnp.sum(jnp.where(before, wet[None, :], 0), axis=1) - 1]
  transfers between devices with their start and end apart: 11 -> 13, of which waited for: 4 -> 2; matrix products, arithmetic and copies ran while one was open for 24% -> 7% of each run, Pallas kernels for 0% -> 20%
where the time goes in v2:
time: 119 us
  Pallas kernels  63.2 us (53%)
  starting transfers between devices  37.2 us (31%)
  local copies, waits for them, and re-layouts  11.5 us (10%)
  other arithmetic  3.08 us (3%)
  waiting for transfers between devices  2.27 us (2%)
  between operations  1.31 us (1%)
    pallas_call x2, Pallas kernels, run_block(): pl.pallas_call(functools.partial(block_kernel, last, block), out_shape=ou...  33.8 us
    pallas_call x4, Pallas kernels, run_product(): pl.pallas_call(functools.partial(product_kernel, first), out_shape=[shape...  16.1 us
    all_to_all x1, starting transfers between devices, body(): lax.all_to_all(atm_flux[0], ('gx', 'gy'), split_axis=0, concat_axis=0, ti...  11.3 us
    ppermute x2, starting transfers between devices, body(): corner_odd = lax.ppermute(corner, ('gx', 'gy'), lat_odd)  10.3 us
    ppermute x2, starting transfers between devices, body(): row_odd = lax.ppermute(row_odd, ('gx', 'gy'), lat_odd)  7.17 us
    unnamed x58, local copies, waits for them, and re-layouts  7.17 us
    ppermute x2, starting transfers between devices, body(): column_odd = lax.ppermute(own_odd, 'gx', lon_odd)  6.74 us
    pallas_call x1, Pallas kernels, run_stem(): pl.pallas_call(stem_kernel, out_shape=[shape(height, width, LANES)] + edg...  5.62 us
  transfers between devices with their start and end apart: 13, of which 2 were waited for; matrix products, arithmetic and copies ran while one was open for 7% of the time, Pallas kernels for 20%

profile of v2, /device:TPU:7, one launch (start us, length us, event | category | flops | bytes accessed | tf_op | source)
XLA Modules:
  0.0 118.6 jit_solution(4309593937783248119)
XLA Ops:
  0.0 11.3 %all-to-all-start = ((bf16[128,1,16,256]{3,2,1,0:T(8,128)(2,1)}), bf16[128,1,16,256]{3,2,1,0:T(8,128)(2,1)}, u32[]{:S(2)}, u32[]{:S(2)}) async-start(bf16[128,1,16,256]{3,2,1,0:T(8,128)(2,1)} %bitcast.32), calls=%async_computation | async-start | bytes 2097152 | tf_op jit(solution)/shard_map/all_to_all | solution.py:563
  11.3 0.6 reduce_sum.36
  14.2 0.6 pad.14.weight_ref
  15.2 1.0 copy.91
  16.2 1.0 copy.92
  17.9 1.7 %copy-done.16 = bf16[160,7552]{1,0:T(8,128)(2,1)S(1)} copy-done((bf16[160,7552]{1,0:T(8,128)(2,1)S(1)}, bf16[160,7552]{1,0:T(8,128)(2,1)}, u32[]{:S(2)}) %copy-start.16) | copy-done | bytes 2416664
  19.5 1.8 %prepare.1 = (bf16[7,208,256]{2,1,0:T(8,128)(2,1)S(1)}, bf16[42,208,128]{2,1,0:T(8,128)(2,1)S(1)}, f32[208,128]{1,0:T(8,128)S(1)}, f32[2,208,128]{2,1,0:T(8,128)...) custom-call(bf16[2,208,160]{2,1,0:T(8,128)(2,1)S(1)} %pad.12.coef_re, ...), custom_call_target="tpu_custom_call" | custom-call | flops 1005322240 | bytes 10000000 | tf_op jit(solution)/shard_map/prepare/pallas_call | solution.py:406
  21.4 1.4 %copy-done.1 = bf16[42,208,128]{2,1,0:T(8,128)(2,1)} copy-done((bf16[42,208,128]{2,1,0:T(8,128)(2,1)}, bf16[42,208,128]{2,1,0:T(8,128)(2,1)S(1)}, u32[]{:S(2)}) %copy-start.1) | copy-done | bytes 2236440
  22.7 1.4 %copy-done.3 = bf16[42,208,128]{2,1,0:T(8,128)(2,1)} copy-done((bf16[42,208,128]{2,1,0:T(8,128)(2,1)}, bf16[42,208,128]{2,1,0:T(8,128)(2,1)S(1)}, u32[]{:S(2)}) %copy-start.3) | copy-done | bytes 2236440
  24.1 0.8 pad_add_fusion.rows_ref
  25.0 0.6 select_reduce_fusion.inverse_ref
  26.3 1.6 %all-to-all-done = bf16[128,1,16,256]{3,2,1,0:T(8,128)(2,1)} async-done(((bf16[128,1,16,256]{3,2,1,0:T(8,128)(2,1)}), bf16[128,1,16,256]{3,2,1,0:T(8,128)(2,1)}, u32[]{:S(2)}, u32[]{:S(2)}) %all-to-all-start) | async-done | bytes 1048608 | tf_op jit(solution)/shard_map/all_to_all | solution.py:563
  27.9 0.8 copy-done.8
  28.7 0.9 copy-done.10
  30.2 5.6 %stem.1 = (bf16[64,208,128]{2,1,0:T(8,128)(2,1)S(1)}, bf16[3,208,128]{2,1,0:T(8,128)(2,1)S(1)}, bf16[3,208,128]{2,1,0:T(8,128)(2,1)S(1)}, bf16[2,208,128]{2,1,0:T(8,128)(2,1)S(1)}, bf16[2,208,128]{2,1,0:T(8,128)(2,1)S(1)}) custom-call(s32[49]{0:T(128)S(1)} %pad_add_fusion.rows_ref, s32[3]{0:T(128)S(1)} %pad_add_fusion.1.flags_ref, s32[128]{0:T(128)S(1)} %copy-done.15, ...), custom_call_target="tpu_custom_call" | custom-call | tf_op jit(solution)/shard_map/stem/pallas_call | solution.py:418
  35.9 0.6 collective-permute-start
  36.5 3.7 %collective-permute-start.1 = (bf16[2,208,128]{2,1,0:T(8,128)(2,1)S(1)}, bf16[2,208,128]{2,1,0:T(8,128)(2,1)S(1)}, u32[]{:S(2)}, u32[]{:S(2)}) collective-permute-start(bf16[2,208,128]{2,1,0:T(8,128)(2,1)S(1)} %get-tuple-element.50.own_odd_ref), channel_id=1, source_target_pairs={{0,120},{8,16},{16,8},{24,32},{32,24},{40,48},{48,40},{56,64},{64,... | collective-permute-start | bytes 319496 | tf_op jit(solution)/shard_map/ppermute | solution.py:598
  40.3 0.9 collective-permute-start.2
  41.2 2.8 %collective-permute-start.3 = (bf16[3,208,128]{2,1,0:T(8,128)(2,1)S(1)}, bf16[3,208,128]{2,1,0:T(8,128)(2,1)S(1)}, u32[]{:S(2)}, u32[]{:S(2)}) collective-permute-start(bf16[3,208,128]{2,1,0:T(8,128)(2,1)S(1)} %get-tuple-element.54), channel_id=1, source_target_pairs={{1,2},{2,1},{3,4},{4,3},{5,6},{6,5},{7,127},{9,10},{10,9},{11,12},... | collective-permute-start | bytes 479240 | tf_op jit(solution)/shard_map/ppermute | solution.py:600
  44.0 2.4 %transform.2.wave_ref.after_ref = bf16[64,208,256]{2,1,0:T(8,128)(2,1)S(1)} custom-call(bf16[64,208,128]{2,1,0:T(8,128)(2,1)S(1)} %get-tuple-element.47.state_ref, bf16[128,256]{1,0:T(8,128)(2,1)S(1)} %copy-done.5), custom_call_target="tpu_custom_call" | custom-call | flops 872415232 | bytes 10000000 | tf_op jit(solution)/shard_map/transform/pallas_call | solution.py:435
  46.4 4.2 %product.4.after_ref.prod_one_ref = bf16[48,112,128]{2,1,0:T(8,128)(2,1)S(1)} custom-call(s32[49]{0:T(128)S(1)} %pad_add_fusion.rows_ref, bf16[64,208,256]{2,1,0:T(8,128)(2,1)S(1)} %transform.2.wave_ref.after_ref, bf16[7,208,256]{2,1,0:T(8,128)(2,1)S(1)} %get-tuple-element.48.mix_ref, bf16[64,208,256]{2,1,0:T(8,128)(2,1)S(1)} %transform.2.wave_ref.after_ref), custom_call_target="tpu_custom_call" | custom-call | flops 19267584 | bytes 20000000 | tf_op jit(solution)/shard_map/product/pallas_call | solution.py:450
  51.3 5.9 %collective-permute-start.5 = (bf16[2,208,128]{2,1,0:T(8,128)(2,1)S(1)}, bf16[2,208,128]{2,1,0:T(8,128)(2,1)S(1)}, u32[]{:S(2)}, u32[]{:S(2)}) collective-permute-start(bf16[2,208,128]{2,1,0:T(8,128)(2,1)S(1)} %corner.2.after_ref), channel_id=1, source_target_pairs={{1,2},{2,1},{3,4},{4,3},{5,6},{6,5},{7,127},{9,10},{10,9},{11,12},... | collective-permute-start | bytes 319496 | tf_op jit(solution)/shard_map/ppermute | solution.py:607
  57.3 3.8 %product.5 = (bf16[48,96,128]{2,1,0:T(8,128)(2,1)S(1)}, bf16[12,208,256]{2,1,0:T(8,128)(2,1)S(1)}) custom-call(s32[49]{0:T(128)S(1)} %pad_add_fusion.rows_ref, bf16[64,208,256]{2,1,0:T(8,128)(2,1)S(1)} %transform.2.wave_ref.after_ref, bf16[7,208,256]{2,1,0:T(8,128)(2,1)S(1)} %get-tuple-element.48.mix_ref, bf16[2,208,128]{2,1,0:T(8,128)(2,1)S(1)} %corner.2.after_ref), custom_call_target="tpu_custom_call" | custom-call | flops 16515072 | bytes 20000000 | tf_op jit(solution)/shard_map/product/pallas_call | solution.py:450
  61.2 16.6 %block.2 = (bf16[64,208,128]{2,1,0:T(8,128)(2,1)S(1)}, bf16[3,208,128]{2,1,0:T(8,128)(2,1)S(1)}, bf16[3,208,128]{2,1,0:T(8,128)(2,1)S(1)}, bf16[2,208,128]{2,1,0:T(8,128)(2,1)S(1)}, bf16[2,208,128]{2,1,0:T(8,128)(2,1)S(1)}) custom-call(s32[49]{0:T(128)S(1)} %pad_add_fusion.rows_ref, s32[3]{0:T(128)S(1)} %pad_add_fusion.1.flags_ref, ...), custom_call_target="tpu_custom_call" | custom-call | tf_op jit(solution)/shard_map/block/pallas_call | solution.py:489
  77.9 3.0 %collective-permute-start.7 = (bf16[2,208,128]{2,1,0:T(8,128)(2,1)S(1)}, bf16[2,208,128]{2,1,0:T(8,128)(2,1)S(1)}, u32[]{:S(2)}, u32[]{:S(2)}) collective-permute-start(bf16[2,208,128]{2,1,0:T(8,128)(2,1)S(1)} %get-tuple-element.63.own_odd_ref), channel_id=1, source_target_pairs={{0,120},{8,16},{16,8},{24,32},{32,24},{40,48},{48,40},{56,64},{64,... | collective-permute-start | bytes 319496 | tf_op jit(solution)/shard_map/ppermute | solution.py:598
  80.9 4.4 %collective-permute-start.9 = (bf16[3,208,128]{2,1,0:T(8,128)(2,1)S(1)}, bf16[3,208,128]{2,1,0:T(8,128)(2,1)S(1)}, u32[]{:S(2)}, u32[]{:S(2)}) collective-permute-start(bf16[3,208,128]{2,1,0:T(8,128)(2,1)S(1)} %get-tuple-element.67), channel_id=1, source_target_pairs={{1,2},{2,1},{3,4},{4,3},{5,6},{6,5},{7,127},{9,10},{10,9},{11,12},... | collective-permute-start | bytes 479240 | tf_op jit(solution)/shard_map/ppermute | solution.py:600
  85.3 2.4 %transform.3.wave_ref.after_ref = bf16[64,208,256]{2,1,0:T(8,128)(2,1)S(1)} custom-call(bf16[64,208,128]{2,1,0:T(8,128)(2,1)S(1)} %get-tuple-element.60.state_ref, bf16[128,256]{1,0:T(8,128)(2,1)S(1)} %copy-done.5), custom_call_target="tpu_custom_call" | custom-call | flops 872415232 | bytes 10000000 | tf_op jit(solution)/shard_map/transform/pallas_call | solution.py:435
  87.7 4.2 %product.6.after_ref.prod_one_ref = bf16[48,112,128]{2,1,0:T(8,128)(2,1)S(1)} custom-call(s32[49]{0:T(128)S(1)} %pad_add_fusion.rows_ref, bf16[64,208,256]{2,1,0:T(8,128)(2,1)S(1)} %transform.3.wave_ref.after_ref, bf16[7,208,256]{2,1,0:T(8,128)(2,1)S(1)} %get-tuple-element.61.mix_ref, bf16[64,208,256]{2,1,0:T(8,128)(2,1)S(1)} %transform.3.wave_ref.after_ref), custom_call_target="tpu_custom_call" | custom-call | flops 19267584 | bytes 20000000 | tf_op jit(solution)/shard_map/product/pallas_call | solution.py:450
  92.5 4.3 %collective-permute-start.11 = (bf16[2,208,128]{2,1,0:T(8,128)(2,1)S(1)}, bf16[2,208,128]{2,1,0:T(8,128)(2,1)S(1)}, u32[]{:S(2)}, u32[]{:S(2)}) collective-permute-start(bf16[2,208,128]{2,1,0:T(8,128)(2,1)S(1)} %corner.3.after_ref), channel_id=1, source_target_pairs={{1,2},{2,1},{3,4},{4,3},{5,6},{6,5},{7,127},{9,10},{10,9},{11,12},... | collective-permute-start | bytes 319496 | tf_op jit(solution)/shard_map/ppermute | solution.py:607
  97.0 3.8 %product.7 = (bf16[48,96,128]{2,1,0:T(8,128)(2,1)S(1)}, bf16[12,208,256]{2,1,0:T(8,128)(2,1)S(1)}) custom-call(s32[49]{0:T(128)S(1)} %pad_add_fusion.rows_ref, bf16[64,208,256]{2,1,0:T(8,128)(2,1)S(1)} %transform.3.wave_ref.after_ref, bf16[7,208,256]{2,1,0:T(8,128)(2,1)S(1)} %get-tuple-element.61.mix_ref, bf16[2,208,128]{2,1,0:T(8,128)(2,1)S(1)} %corner.3.after_ref), custom_call_target="tpu_custom_call" | custom-call | flops 16515072 | bytes 20000000 | tf_op jit(solution)/shard_map/product/pallas_call | solution.py:450
  100.8 0.6 collective-permute-done.11.corner_odd_ref
  101.5 17.1 %block.3 = bf16[200,64,128]{2,1,0:T(8,128)(2,1)} custom-call(s32[49]{0:T(128)S(1)} %pad_add_fusion.rows_ref, s32[3]{0:T(128)S(1)} %pad_add_fusion.1.flags_ref, bf16[64,208,128]{2,1,0:T(8,128)(2,1)S(1)} %get-tuple-element.60.state_ref, bf16[48,112,128]{2,1,0:T(8,128)(2,1)S(1)} %product.6.after_ref.prod_one_ref, ...), custom_call_target="tpu_custom_call" | custom-call | tf_op jit(solution)/shard_map/block/pallas_call | solution.py:489
  (96 shorter events, 5.2 us)
Async XLA Ops:
  0.0 11.3 %copy-start.26 = (s32[64,1]{0,1:T(1,128)S(1)}, s32[64,1]{0,1:T(1,128)}, u32[]{:S(2)}) copy-start(s32[64,1]{0,1:T(1,128)} %param.18) | copy-start | bytes 772
  0.0 12.7 %copy-start.24 = (f32[2,200]{1,0:T(2,128)S(1)}, f32[2,200]{1,0:T(2,128)}, u32[]{:S(2)}) copy-start(f32[2,200]{1,0:T(2,128)} %param.21) | copy-start | bytes 4804
  0.0 12.8 %copy-start.25 = (f32[2,200]{1,0:T(2,128)S(1)}, f32[2,200]{1,0:T(2,128)}, u32[]{:S(2)}) copy-start(f32[2,200]{1,0:T(2,128)} %param.22) | copy-start | bytes 4804
  0.0 12.8 %copy-start.23 = (f32[2,800]{1,0:T(2,128)S(1)}, f32[2,800]{1,0:T(2,128)}, u32[]{:S(2)}) copy-start(f32[2,800]{1,0:T(2,128)} %param.24) | copy-start | bytes 19204
  0.0 12.8 %copy-start.22 = (bf16[200,16,2,2]{0,3,2,1:T(2,128)(2,1)S(1)}, bf16[200,16,2,2]{0,3,2,1:T(2,128)(2,1)}, u32[]{:S(2)}) copy-start(bf16[200,16,2,2]{0,3,2,1:T(2,128)(2,1)} %param.19) | copy-start | bytes 76804
  0.0 12.9 %copy-start.21 = (f32[2,200,7,7]{1,0,3,2:T(2,128)S(1)}, f32[2,200,7,7]{1,0,3,2:T(2,128)}, u32[]{:S(2)}) copy-start(f32[2,200,7,7]{1,0,3,2:T(2,128)} %param.20) | copy-start | bytes 235204
  0.0 27.9 %all-to-all-start = ((bf16[128,1,16,256]{3,2,1,0:T(8,128)(2,1)}), bf16[128,1,16,256]{3,2,1,0:T(8,128)(2,1)}, u32[]{:S(2)}, u32[]{:S(2)}) async-start(bf16[128,1,16,256]{3,2,1,0:T(8,128)(2,1)} %bitcast.32), calls=%async_computation | async-start | bytes 2097152 | tf_op jit(solution)/shard_map/all_to_all | solution.py:563
  13.7 3.5 %copy-start.19 = (bf16[2,200,800]{2,1,0:T(8,128)(2,1)S(1)}, bf16[2,200,800]{2,1,0:T(8,128)(2,1)}, u32[]{:S(2)}) copy-start(bf16[2,200,800]{2,1,0:T(8,128)(2,1)} %param.23) | copy-start | bytes 1920004
  19.5 5.5 %copy-start.27 = (s32[128,1]{0,1:T(1,128)S(1)}, s32[128,1]{0,1:T(1,128)}, u32[]{:S(2)}) copy-start(s32[128,1]{0,1:T(1,128)} %param.17) | copy-start | bytes 1540
  19.5 6.1 %copy-start.20 = (bf16[2,800,200]{1,2,0:T(8,128)(2,1)S(1)}, bf16[2,800,200]{1,2,0:T(8,128)(2,1)}, u32[]{:S(2)}) copy-start(bf16[2,800,200]{1,2,0:T(8,128)(2,1)} %param.25) | copy-start | bytes 1920004
  24.1 1.7 %copy-start.18 = (bf16[2,1,800]{1,2,0:T(8,128)(2,1)S(1)}, bf16[2,1,800]{1,2,0:T(8,128)(2,1)}, u32[]{:S(2)}) copy-start(bf16[2,1,800]{1,2,0:T(8,128)(2,1)} %copy.92) | copy-start | bytes 9604
  25.8 18.2 %copy-start.5 = (bf16[128,256]{1,0:T(8,128)(2,1)S(1)}, bf16[128,256]{1,0:T(8,128)(2,1)}, u32[]{:S(2)}) copy-start(bf16[128,256]{1,0:T(8,128)(2,1)} %constant.55.clone.forward_ref) | copy-start | bytes 196612
  35.9 10.5 %copy-start = (bf16[64,208,128]{2,1,0:T(8,128)(2,1)}, bf16[64,208,128]{2,1,0:T(8,128)(2,1)S(1)}, u32[]{:S(2)}) copy-start(bf16[64,208,128]{2,1,0:T(8,128)(2,1)S(1)} %get-tuple-element.47.state_ref) | copy-start | bytes 10223620
  35.9 14.7 %collective-permute-start = (bf16[2,208,128]{2,1,0:T(8,128)(2,1)S(1)}, bf16[2,208,128]{2,1,0:T(8,128)(2,1)S(1)}, u32[]{:S(2)}, u32[]{:S(2)}) collective-permute-start(bf16[2,208,128]{2,1,0:T(8,128)(2,1)S(1)} %get-tuple-element.49.own_even_ref), channel_id=1, source_target_pairs={{0,8},{8,0},{16,24},{24,16},{32,40},{40,32},{48,56},{56,48},{64,72... | collective-permute-start | bytes 319496 | tf_op jit(solution)/shard_map/ppermute | solution.py:597
  36.5 14.1 %collective-permute-start.1 = (bf16[2,208,128]{2,1,0:T(8,128)(2,1)S(1)}, bf16[2,208,128]{2,1,0:T(8,128)(2,1)S(1)}, u32[]{:S(2)}, u32[]{:S(2)}) collective-permute-start(bf16[2,208,128]{2,1,0:T(8,128)(2,1)S(1)} %get-tuple-element.50.own_odd_ref), channel_id=1, source_target_pairs={{0,120},{8,16},{16,8},{24,32},{32,24},{40,48},{48,40},{56,64},{64,... | collective-permute-start | bytes 319496 | tf_op jit(solution)/shard_map/ppermute | solution.py:598
  40.3 20.9 %collective-permute-start.2 = (bf16[3,208,128]{2,1,0:T(8,128)(2,1)S(1)}, bf16[3,208,128]{2,1,0:T(8,128)(2,1)S(1)}, u32[]{:S(2)}, u32[]{:S(2)}) collective-permute-start(bf16[3,208,128]{2,1,0:T(8,128)(2,1)S(1)} %get-tuple-element.53), channel_id=1, source_target_pairs={{0,1},{1,0},{2,3},{3,2},{4,5},{5,4},{6,7},{7,6},{8,9},{9,8},{10,11... | collective-permute-start | bytes 479240 | tf_op jit(solution)/shard_map/ppermute | solution.py:599
  41.2 19.9 %collective-permute-start.3 = (bf16[3,208,128]{2,1,0:T(8,128)(2,1)S(1)}, bf16[3,208,128]{2,1,0:T(8,128)(2,1)S(1)}, u32[]{:S(2)}, u32[]{:S(2)}) collective-permute-start(bf16[3,208,128]{2,1,0:T(8,128)(2,1)S(1)} %get-tuple-element.54), channel_id=1, source_target_pairs={{1,2},{2,1},{3,4},{4,3},{5,6},{6,5},{7,127},{9,10},{10,9},{11,12},... | collective-permute-start | bytes 479240 | tf_op jit(solution)/shard_map/ppermute | solution.py:600
  51.2 9.9 %copy-start.4 = (bf16[42,208,128]{2,1,0:T(8,128)(2,1)S(1)}, bf16[42,208,128]{2,1,0:T(8,128)(2,1)}, u32[]{:S(2)}) copy-start(bf16[42,208,128]{2,1,0:T(8,128)(2,1)} %copy-done.3) | copy-start | bytes 6709252
  51.2 9.9 %copy-start.6 = (bf16[256,128]{1,0:T(8,128)(2,1)S(1)}, bf16[256,128]{1,0:T(8,128)(2,1)}, u32[]{:S(2)}) copy-start(bf16[256,128]{1,0:T(8,128)(2,1)} %constant.56.clone.inverse_ref) | copy-start | bytes 196612
  51.2 9.9 %copy-start.7 = (bf16[128,256]{1,0:T(8,128)(2,1)S(1)}, bf16[128,256]{1,0:T(8,128)(2,1)}, u32[]{:S(2)}) copy-start(bf16[128,256]{1,0:T(8,128)(2,1)} %constant.54.clone.flipped_ref) | copy-start | bytes 196612
  51.2 9.9 %copy-start.9 = (bf16[128,128]{1,0:T(8,128)(2,1)S(1)}, bf16[128,128]{1,0:T(8,128)(2,1)}, u32[]{:S(2)}) copy-start(bf16[128,128]{1,0:T(8,128)(2,1)} %constant.57.clone.turn_ref) | copy-start | bytes 98308
  51.2 9.9 %copy-start.14 = (f32[208,128]{1,0:T(8,128)S(1)}, f32[208,128]{1,0:T(8,128)}, u32[]{:S(2)}) copy-start(f32[208,128]{1,0:T(8,128)} %copy-done.13) | copy-start | bytes 319492
  51.3 9.9 %collective-permute-start.5 = (bf16[2,208,128]{2,1,0:T(8,128)(2,1)S(1)}, bf16[2,208,128]{2,1,0:T(8,128)(2,1)S(1)}, u32[]{:S(2)}, u32[]{:S(2)}) collective-permute-start(bf16[2,208,128]{2,1,0:T(8,128)(2,1)S(1)} %corner.2.after_ref), channel_id=1, source_target_pairs={{1,2},{2,1},{3,4},{4,3},{5,6},{6,5},{7,127},{9,10},{10,9},{11,12},... | collective-permute-start | bytes 319496 | tf_op jit(solution)/shard_map/ppermute | solution.py:607
  57.2 3.9 %collective-permute-start.4 = (bf16[2,208,128]{2,1,0:T(8,128)(2,1)S(1)}, bf16[2,208,128]{2,1,0:T(8,128)(2,1)S(1)}, u32[]{:S(2)}, u32[]{:S(2)}) collective-permute-start(bf16[2,208,128]{2,1,0:T(8,128)(2,1)S(1)} %corner.2.after_ref), channel_id=1, source_target_pairs={{0,1},{1,0},{2,3},{3,2},{4,5},{5,4},{6,7},{7,6},{8,9},{9,8},{10,11... | collective-permute-start | bytes 319496 | tf_op jit(solution)/shard_map/ppermute | solution.py:606
  77.8 14.1 %collective-permute-start.6 = (bf16[2,208,128]{2,1,0:T(8,128)(2,1)S(1)}, bf16[2,208,128]{2,1,0:T(8,128)(2,1)S(1)}, u32[]{:S(2)}, u32[]{:S(2)}) collective-permute-start(bf16[2,208,128]{2,1,0:T(8,128)(2,1)S(1)} %get-tuple-element.62.own_even_ref), channel_id=1, source_target_pairs={{0,8},{8,0},{16,24},{24,16},{32,40},{40,32},{48,56},{56,48},{64,72... | collective-permute-start | bytes 319496 | tf_op jit(solution)/shard_map/ppermute | solution.py:597
  77.9 14.0 %collective-permute-start.7 = (bf16[2,208,128]{2,1,0:T(8,128)(2,1)S(1)}, bf16[2,208,128]{2,1,0:T(8,128)(2,1)S(1)}, u32[]{:S(2)}, u32[]{:S(2)}) collective-permute-start(bf16[2,208,128]{2,1,0:T(8,128)(2,1)S(1)} %get-tuple-element.63.own_odd_ref), channel_id=1, source_target_pairs={{0,120},{8,16},{16,8},{24,32},{32,24},{40,48},{48,40},{56,64},{64,... | collective-permute-start | bytes 319496 | tf_op jit(solution)/shard_map/ppermute | solution.py:598
  80.9 19.9 %collective-permute-start.8 = (bf16[3,208,128]{2,1,0:T(8,128)(2,1)S(1)}, bf16[3,208,128]{2,1,0:T(8,128)(2,1)S(1)}, u32[]{:S(2)}, u32[]{:S(2)}) collective-permute-start(bf16[3,208,128]{2,1,0:T(8,128)(2,1)S(1)} %get-tuple-element.66), channel_id=1, source_target_pairs={{0,1},{1,0},{2,3},{3,2},{4,5},{5,4},{6,7},{7,6},{8,9},{9,8},{10,11... | collective-permute-start | bytes 479240 | tf_op jit(solution)/shard_map/ppermute | solution.py:599
  80.9 19.9 %collective-permute-start.9 = (bf16[3,208,128]{2,1,0:T(8,128)(2,1)S(1)}, bf16[3,208,128]{2,1,0:T(8,128)(2,1)S(1)}, u32[]{:S(2)}, u32[]{:S(2)}) collective-permute-start(bf16[3,208,128]{2,1,0:T(8,128)(2,1)S(1)} %get-tuple-element.67), channel_id=1, source_target_pairs={{1,2},{2,1},{3,4},{4,3},{5,6},{6,5},{7,127},{9,10},{10,9},{11,12},... | collective-permute-start | bytes 479240 | tf_op jit(solution)/shard_map/ppermute | solution.py:600
  92.5 8.9 %copy-start.2 = (bf16[42,208,128]{2,1,0:T(8,128)(2,1)S(1)}, bf16[42,208,128]{2,1,0:T(8,128)(2,1)}, u32[]{:S(2)}) copy-start(bf16[42,208,128]{2,1,0:T(8,128)(2,1)} %copy-done.1) | copy-start | bytes 6709252
  92.5 8.9 %copy-start.12 = (f32[208,128]{1,0:T(8,128)S(1)}, f32[208,128]{1,0:T(8,128)}, u32[]{:S(2)}) copy-start(f32[208,128]{1,0:T(8,128)} %copy-done.11) | copy-start | bytes 319492
  92.5 8.9 %collective-permute-start.11 = (bf16[2,208,128]{2,1,0:T(8,128)(2,1)S(1)}, bf16[2,208,128]{2,1,0:T(8,128)(2,1)S(1)}, u32[]{:S(2)}, u32[]{:S(2)}) collective-permute-start(bf16[2,208,128]{2,1,0:T(8,128)(2,1)S(1)} %corner.3.after_ref), channel_id=1, source_target_pairs={{1,2},{2,1},{3,4},{4,3},{5,6},{6,5},{7,127},{9,10},{10,9},{11,12},... | collective-permute-start | bytes 319496 | tf_op jit(solution)/shard_map/ppermute | solution.py:607
  96.9 4.6 %collective-permute-start.10 = (bf16[2,208,128]{2,1,0:T(8,128)(2,1)S(1)}, bf16[2,208,128]{2,1,0:T(8,128)(2,1)S(1)}, u32[]{:S(2)}, u32[]{:S(2)}) collective-permute-start(bf16[2,208,128]{2,1,0:T(8,128)(2,1)S(1)} %corner.3.after_ref), channel_id=1, source_target_pairs={{0,1},{1,0},{2,3},{3,2},{4,5},{5,4},{6,7},{7,6},{8,9},{9,8},{10,11... | collective-permute-start | bytes 319496 | tf_op jit(solution)/shard_map/ppermute | solution.py:606
  (9 other events, 11.7 us)

commit v3 on v2

--- a/solution.py
+++ b/solution.py
@@ -40,14 +40,6 @@
     return forward, inverse
 
 
-def deinterleave_table():
-    table = np.zeros((2 * LANES, 2 * LANES))
-    spot = np.arange(LANES)
-    table[2 * spot, spot] = 1.0
-    table[2 * spot + 1, LANES + spot] = 1.0
-    return table
-
-
 def fold_table():
     table = np.zeros((LANES, LANES))
     spot = np.arange(LANES - 1)
@@ -85,24 +77,33 @@
     column_refs[1][...] = jnp.where(even_column, low_ref[...], high_ref[...])
 
 
-def prepare_kernel(blocks, coef_ref, table_ref, *outs):
+def prepare_kernel(blocks, coef_ref, table_ref, stem_ref, *outs):
+    outs[-1][...] = stem_ref[...]
+    spot = lax.broadcasted_iota(jnp.int32, (coef_ref.shape[2], LANES), 0)
+    phase = lane_ids((coef_ref.shape[2], LANES)) % 4
     for block in range(blocks):
         mix_ref, side_ref, gain_ref, bias_ref = outs[4 * block:4 * block + 4]
         coef = coef_ref[block]
         for tap in range(7):
             mix_ref[tap] = dot(coef, table_ref[:, tap * 256:(tap + 1) * 256]).astype(BF16)
         for pair in range(21):
-            out = dot(coef, table_ref[:, 1792 + pair * 256:2048 + pair * 256]).astype(BF16)
+            tables = []
+            for entry in (2 * pair, 2 * pair + 1):
+                side, row, tap = entry // 21, entry % 21 // 3, entry % 3
+                source = row * 7 + (tap if side == 0 else 6 - tap)
+                inside = phase <= 2 - tap if side == 0 else (phase >= tap) & (phase <= 2)
+                tables.append(jnp.where(((spot == source) | (spot == source + 49)) & inside, 1.0, 0.0).astype(BF16))
+            out = dot(coef, jnp.concatenate(tables, axis=1)).astype(BF16)
             side_ref[2 * pair] = out[:, :LANES]
             side_ref[2 * pair + 1] = out[:, LANES:]
-        out = dot(coef, table_ref[:, 7168:7552])
+        out = dot(coef, table_ref[:, 1792:2176])
         gain_ref[...] = out[:, :LANES]
         bias_ref[0] = out[:, LANES:2 * LANES]
         bias_ref[1] = out[:, 2 * LANES:]
 
 
 def prepare_table():
-    table = np.zeros((160, 7552))
+    table = np.zeros((160, 2176))
     angle = 2.0 * np.pi * np.arange(HALF + 1)[None, :] * (np.arange(7)[:, None] - 3) / LANES
     cos, sin = np.cos(angle), np.sin(angle)
     none = np.zeros((7, 1))
@@ -110,33 +111,38 @@
     imag = np.concatenate([none, -sin[:, 1:HALF], none, sin[:, 1:HALF]], axis=1)
     wave = np.concatenate([real, imag], axis=1)
     wave_high = wave.astype(BF16).astype(np.float64)
-    phase = np.arange(LANES) % 4
     for row in range(7):
         for tap in range(7):
             spot = row * 7 + tap
             table[spot, row * 256:(row + 1) * 256] = wave_high[tap]
             table[49 + spot, row * 256:(row + 1) * 256] = wave_high[tap]
             table[98 + spot, row * 256:(row + 1) * 256] = wave[tap] - wave_high[tap]
-        for tap in range(3):
-            at = 1792 + (row * 3 + tap) * LANES
-            for copy in (0, 49):
-                table[copy + row * 7 + tap, at:at + LANES] = phase + tap <= 2
-                table[copy + row * 7 + 6 - tap, at + 2688:at + 2688 + LANES] = (phase >= tap) & (phase <= 2)
-    table[147:150, 7168:7296] = 1.0
-    table[150, 7296:7424] = 1.0
-    table[151, 7424:7552] = 1.0
+    table[147:150, 1792:1920] = 1.0
+    table[150, 1920:2048] = 1.0
+    table[151, 2048:2176] = 1.0
     return table
 
 
-def stem_kernel(rows_ref, flags_ref, inverse_ref, arrived_ref, table_ref, weight_ref, state_ref, row_even_ref,
-                row_odd_ref, column_even_ref, column_odd_ref, split_ref, low_ref, high_ref):
+def stem_kernel(rows_ref, flags_ref, owner_ref, arrived_ref, weight_ref, state_ref, row_even_ref, row_odd_ref,
+                column_even_ref, column_odd_ref, inverse_ref, split_ref, low_ref, high_ref):
     pieces = arrived_ref.shape[0]
     flux = arrived_ref.shape[1]
     step = 32
 
+    def invert(index, _):
+        for at in range(8):
+            inverse_ref[owner_ref[index * 8 + at]] = index * 8 + at
+        return 0
+
+    lax.fori_loop(0, pieces // 8, invert, 0)
+    source = lax.broadcasted_iota(jnp.int32, (2 * LANES, 2 * LANES), 0)
+    target = lane_ids((2 * LANES, 2 * LANES))
+    wanted = jnp.where(target < LANES, 2 * target, 2 * target - (2 * LANES - 1))
+    table = jnp.where(source == wanted, 1.0, 0.0).astype(BF16)
+
     def split(index, _):
         part = arrived_ref[pl.ds(index * step, step)].reshape(step * flux, 2 * LANES)
-        split_ref[pl.ds(index * step, step)] = dot(part, table_ref[...]).astype(BF16).reshape(step, flux, 2 * LANES)
+        split_ref[pl.ds(index * step, step)] = dot(part, table).astype(BF16).reshape(step, flux, 2 * LANES)
         return 0
 
     lax.fori_loop(0, pieces // step, split, 0)
@@ -207,9 +213,8 @@
 
 
 def block_kernel(last, block, rows_ref, flags_ref, state_ref, prod_one_ref, prod_two_ref, edge_wave_ref, row_even_ref, row_odd_ref,
-                 column_even_ref, column_odd_ref, corner_even_ref, corner_odd_ref, own_even_ref, own_odd_ref,
-                 mix_ref, side_ref, gain_ref, bias_ref, forward_ref, flipped_ref, inverse_ref, turn_ref, expand_ref,
-                 reduce_ref, *rest):
+                 column_even_ref, column_odd_ref, own_even_ref, own_odd_ref, mix_ref, side_ref, gain_ref,
+                 bias_ref, forward_ref, flipped_ref, inverse_ref, turn_ref, expand_ref, reduce_ref, *rest):
     if last:
         out_ref, halo_ref, fix_ref, edge_ref, grid_ref, normed_ref, held_ref = rest
     else:
@@ -232,23 +237,23 @@
     high = jnp.where(even_column, own_even_ref[...], own_odd_ref[...])
     grid_ref[0, 0:2] = left - high
     grid_ref[1, 0:2] = right - low
-    halo_ref[0:3] = wave_of(jnp.where(even_row, row_odd_ref[...], row_even_ref[...]), forward_ref[...])
+    halo_ref[0:3] = wave_of(jnp.where(even_row, row_odd_ref[0:3], row_even_ref[0:3]), forward_ref[...])
     for side in range(2):
-        grid_ref[side, 2] = jnp.where(even_row, corner_odd_ref[side], corner_even_ref[side])
+        grid_ref[side, 2] = jnp.where(even_row, row_odd_ref[3 + side], row_even_ref[3 + side])
 
     @pl.when(jnp.logical_not(fold))
     def _():
-        halo_ref[3:6] = wave_of(jnp.where(even_row, row_even_ref[...], row_odd_ref[...]), forward_ref[...])
+        halo_ref[3:6] = wave_of(jnp.where(even_row, row_even_ref[0:3], row_odd_ref[0:3]), forward_ref[...])
         for side in range(2):
-            grid_ref[side, 3] = jnp.where(even_row, corner_even_ref[side], corner_odd_ref[side])
+            grid_ref[side, 3] = jnp.where(even_row, row_even_ref[3 + side], row_odd_ref[3 + side])
 
     @pl.when(fold)
     def _():
-        waves = wave_of(row_odd_ref[...], flipped_ref[...])
+        waves = wave_of(row_odd_ref[0:3], flipped_ref[...])
         for m in range(3):
             halo_ref[3 + m] = waves[2 - m]
         for side in range(2):
-            grid_ref[side, 3] = dot(corner_odd_ref[1 - side], turn_ref[...]).astype(BF16)
+            grid_ref[side, 3] = dot(row_odd_ref[4 - side], turn_ref[...]).astype(BF16)
 
     def corrections(index, _):
         span = pl.ds(pl.multiple_of(index * 16, 16), 16)
@@ -258,28 +263,27 @@
             here, other = grid_ref[side, 0, span], grid_ref[side, 1, span]
             upward = jnp.where(lane < HALF, here, grid_ref[side, 3, span])
             downward = jnp.where(lane < HALF, grid_ref[side, 2, span], here)
+            slabs = [here, other, upward, downward]
+            turned = [[pltpu.roll(slab, (-tap if side == 0 else tap) % LANES, 1) if tap else slab for tap in range(3)]
+                      for slab in slabs]
             for tap_row in range(7):
-                terms = [None, None]
-                for tap in range(3):
-                    shift = 4 * (tap_row - 3) + (tap if side == 0 else -tap)
-                    weight = side_ref[(side * 7 + tap_row) * 3 + tap, span]
-
-                    def moved(slab):
-                        return pltpu.roll(slab, -shift % LANES, 1) if shift else slab
-
-                    one, two = moved(here), moved(other)
-                    if shift > 0:
-                        first = jnp.where(lane < HALF, moved(upward), jnp.where(lane < LANES - shift, one, two))
-                        second = jnp.where(lane < LANES - shift, two, one)
-                    elif shift < 0:
-                        first = jnp.where(lane >= HALF, moved(downward), jnp.where(lane >= -shift, one, two))
-                        second = jnp.where(lane >= -shift, two, one)
-                    else:
-                        first, second = one, two
-                    for group, value in enumerate((first, second)):
-                        value = weight * value
-                        terms[group] = value if terms[group] is None else terms[group] + value
-                totals = [total + term.astype(F32) for total, term in zip(totals, terms)]
+                shift = 4 * (tap_row - 3)
+                weights = [side_ref[(side * 7 + tap_row) * 3 + tap, span] for tap in range(3)]
+
+                def moved(at):
+                    value = weights[0] * turned[at][0] + weights[1] * turned[at][1] + weights[2] * turned[at][2]
+                    return pltpu.roll(value, -shift % LANES, 1) if shift else value
+
+                first, second = moved(0), moved(1)
+                if shift > 0:
+                    inner = lane < LANES - shift
+                    first, second = jnp.where(inner, first, second), jnp.where(inner, second, first)
+                    first = jnp.where((lane < HALF) & (lane >= HALF - shift), moved(2), first)
+                elif shift < 0:
+                    inner = lane >= -shift
+                    first, second = jnp.where(inner, first, second), jnp.where(inner, second, first)
+                    first = jnp.where((lane >= HALF) & (lane < HALF - shift), moved(3), first)
+                totals = [totals[0] + first.astype(F32), totals[1] + second.astype(F32)]
             for group in range(2):
                 edge_ref[side, group, span] = totals[group].astype(BF16)
         return 0
@@ -344,25 +348,22 @@
         branch = dot(reduce_ref[block], hidden)
         for at in range(GROUP):
             row = rows_ref[1 + GROUP * index + at]
-            value = branch[:, at * LANES:(at + 1) * LANES] + state_ref[row].astype(F32)
+            value = branch[:, at * LANES:(at + 1) * LANES] + state_ref[row].astype(F32)[:channels]
             if last:
-                held_ref[pl.ds(row, channels, stride=pitch), :] = value[:channels]
+                held_ref[pl.ds(row, channels, stride=pitch), :] = value
             else:
-                value = value.astype(BF16)
+                value = jnp.concatenate([value, jnp.zeros((width - channels, LANES), F32)], axis=0).astype(BF16)
                 out_ref[row] = value
                 pack_edges(value, row, low_ref, high_ref)
 
-    def mix(index, _):
-        normalise(2 * index + 1, 1)
-        pointwise(2 * index, 0)
-        normalise(jnp.minimum(2 * index + 2, MOST // GROUP - 1), 0)
-        pointwise(2 * index + 1, 1)
-        return 0
-
     @pl.when(count > 0)
     def _():
+        groups = MOST // GROUP
         normalise(0, 0)
-        lax.fori_loop(0, MOST // GROUP // 2, mix, 0)
+        for index in range(groups):
+            if index < groups - 1:
+                normalise(index + 1, (index + 1) % 2)
+            pointwise(index, index % 2)
 
     if last:
         def finish(index, _):
@@ -377,7 +378,7 @@
 
 GELU = jnp.bfloat16
 MOST = 48
-EARLY = 7
+EARLY = 4
 
 
 def smem():
@@ -400,34 +401,35 @@
     return [shape(3, width, LANES), shape(3, width, LANES), shape(2, width, LANES), shape(2, width, LANES)]
 
 
-def run_prepare(coef, table):
+def run_prepare(coef, table, stem):
     blocks, width, _ = coef.shape
     one = [shape(7, width, 256), shape(42, width, LANES), shape(width, LANES, dtype=F32), shape(2, width, LANES, dtype=F32)]
     return pl.pallas_call(
         functools.partial(prepare_kernel, blocks),
-        out_shape=one * blocks,
-        in_specs=[vmem(), vmem()],
-        out_specs=[vmem()] * (4 * blocks),
-        compiler_params=params(24),
+        out_shape=one * blocks + [shape(*stem.shape)],
+        in_specs=[vmem()] * 3,
+        out_specs=[vmem()] * (4 * blocks + 1),
+        compiler_params=params(16),
         cost_estimate=pl.CostEstimate(flops=2 * blocks * width * 160 * 7552, bytes_accessed=10_000_000, transcendentals=0),
         name="prepare",
-    )(coef, table)
-
-
-def run_stem(rows, flags, inverse, arrived, table, weight, height, width):
+    )(coef, table, stem)
+
+
+def run_stem(rows, flags, owner, arrived, weight, height, width):
     return pl.pallas_call(
         stem_kernel,
         out_shape=[shape(height, width, LANES)] + edge_shapes(width),
-        in_specs=[smem(), smem(), smem(), vmem(), vmem(), vmem()],
+        in_specs=[smem(), smem(), smem(), vmem(), vmem()],
         out_specs=[vmem()] * 5,
         scratch_shapes=[
+            pltpu.SMEM(owner.shape, jnp.int32),
             pltpu.VMEM(arrived.shape, BF16),
             pltpu.VMEM((2, width, LANES), BF16),
             pltpu.VMEM((2, width, LANES), BF16),
         ],
         compiler_params=params(24),
         name="stem",
-    )(rows, flags, inverse, arrived, table, weight)
+    )(rows, flags, owner, arrived, weight)
 
 
 def run_transform(state, forward):
@@ -458,24 +460,28 @@
     )(rows, wave, mix, after)
 
 
-def corner_kernel(flags_ref, column_even_ref, column_odd_ref, own_even_ref, own_odd_ref, after_ref, corner_ref):
+def corner_kernel(flags_ref, column_even_ref, column_odd_ref, own_even_ref, own_odd_ref, strip_even_ref, strip_odd_ref,
+                  after_ref, row_even_ref, row_odd_ref):
     even_column = flags_ref[1] == 0
     one = column_even_ref[0] - own_odd_ref[0]
     two = column_odd_ref[0] - own_even_ref[0]
-    corner_ref[0] = jnp.where(even_column, two, one)
-    corner_ref[1] = jnp.where(even_column, one, two)
-
-
-def run_corner(flags, column_even, column_odd, own_even, own_odd, after):
+    for strip_ref, row_ref in ((strip_even_ref, row_even_ref), (strip_odd_ref, row_odd_ref)):
+        row_ref[0:3] = strip_ref[...]
+        row_ref[3] = jnp.where(even_column, two, one)
+        row_ref[4] = jnp.where(even_column, one, two)
+
+
+def run_corner(flags, column_even, column_odd, own_even, own_odd, strip_even, strip_odd, after):
+    _, width, _ = own_even.shape
     return pl.pallas_call(
         corner_kernel,
-        out_shape=shape(*own_even.shape),
-        in_specs=[smem()] + [vmem()] * 4 + [pl.BlockSpec(memory_space=pl.ANY)],
-        out_specs=vmem(),
+        out_shape=[shape(5, width, LANES)] * 2,
+        in_specs=[smem()] + [vmem()] * 6 + [pl.BlockSpec(memory_space=pl.ANY)],
+        out_specs=[vmem()] * 2,
         compiler_params=params(16),
         cost_estimate=pl.CostEstimate(flops=1000, bytes_accessed=500_000, transcendentals=0),
         name="corner",
-    )(flags, column_even, column_odd, own_even, own_odd, after)
+    )(flags, column_even, column_odd, own_even, own_odd, strip_even, strip_odd, after)
 
 
 def run_block(last, block, rows, flags, state, *arrays):
@@ -498,7 +504,7 @@
             pltpu.VMEM((2, 4, width, LANES), BF16),
             pltpu.VMEM((2, width, GROUP * LANES), BF16),
         ] + extra,
-        compiler_params=params(40),
+        compiler_params=params(28),
         name="block",
     )(rows, flags, state, *arrays)
 
@@ -537,8 +543,7 @@
     expand = jnp.concatenate(
         [expand_weight * BF16(0.5), high, low.astype(BF16), jnp.zeros((blocks, spare - 2, hidden), BF16)], axis=1
     )
-    reduce = jnp.pad(reduce_weight, ((0, 0), (0, 0), (0, spare)))
-    return jnp.transpose(expand, (0, 2, 1)), jnp.transpose(reduce, (0, 2, 1))
+    return jnp.transpose(lax.optimization_barrier(expand), (0, 2, 1)), jnp.transpose(reduce_weight, (0, 2, 1))
 
 
 def body(
@@ -561,11 +566,7 @@
     width = (channels + 15) // 16 * 16
     height = wet_mask.shape[0]
     arrived = lax.all_to_all(atm_flux[0], ("gx", "gy"), split_axis=0, concat_axis=0, tiled=True)[:, 0]
-    pieces = owner_map.shape[0]
     owner = owner_map[:, 0]
-    inverse = jnp.sum(
-        jnp.where(owner[None, :] == jnp.arange(pieces)[:, None], jnp.arange(pieces)[None, :], 0), axis=1
-    ).astype(jnp.int32)
     rows = wet_rows(wet_mask[:, 0])
     flags = jnp.stack([lat_index % 2, lon_index % 2, lat_index == lat_count - 1]).astype(jnp.int32)
     stem = jnp.transpose(stem_weight, (0, 2, 3, 1)).reshape(channels, -1)
@@ -576,12 +577,10 @@
     back = jnp.asarray(back, BF16)
     turn = jnp.asarray(fold_table(), BF16)
     coef = coefficients(depth_weight, depth_bias, norm_gain, width)
-    prepared = run_prepare(coef, jnp.asarray(prepare_table(), BF16))
+    prepared = run_prepare(coef, jnp.asarray(prepare_table(), BF16), stem)
     expand, reduce = pointwise_weights(expand_weight, expand_bias, reduce_weight, width)
     arrived, prepared, expand, reduce = lax.optimization_barrier((arrived, prepared, expand, reduce))
-    state, *edges = run_stem(
-        rows, flags, inverse, arrived, jnp.asarray(deinterleave_table(), BF16), stem, height, width
-    )
+    state, *edges = run_stem(rows, flags, owner, arrived, prepared[-1], height, width)
     lon_even = [(i, i ^ 1) for i in range(lon_count)]
     lon_odd = [(i, ((i - 1 ^ 1) + 1) % lon_count) for i in range(lon_count)]
     lat_even = [(i, i ^ 1) for i in range(lat_count)]
@@ -596,19 +595,17 @@
         row_even, row_odd, own_even, own_odd = edges
         column_even = lax.ppermute(own_even, "gx", lon_even)
         column_odd = lax.ppermute(own_odd, "gx", lon_odd)
-        row_even = lax.ppermute(row_even, "gy", lat_even)
-        row_odd = lax.ppermute(row_odd, ("gx", "gy"), lat_odd)
         mix, side, gain, bias = prepared[4 * index:4 * index + 4]
         bands = width // 16
         wave = run_transform(state, forward)
         prod = run_product(rows, wave, mix, wave, 0, EARLY)
-        corner = run_corner(flags, column_even, column_odd, own_even, own_odd, prod[0])
-        corner_even = lax.ppermute(corner, "gy", lat_even)
-        corner_odd = lax.ppermute(corner, ("gx", "gy"), lat_odd)
-        prod += run_product(rows, wave, mix, corner, EARLY, bands - EARLY)
+        row_even, row_odd = run_corner(flags, column_even, column_odd, own_even, own_odd, row_even, row_odd, prod[0])
+        prod += run_product(rows, wave, mix, row_odd, EARLY, bands - EARLY)
+        row_even = lax.ppermute(row_even, "gy", lat_even)
+        row_odd = lax.ppermute(row_odd, ("gx", "gy"), lat_odd)
         out = run_block(
             last, index, rows, flags, state, *prod, row_even, row_odd, column_even, column_odd,
-            corner_even, corner_odd, own_even, own_odd, mix, side, gain, bias, forward, flipped, back, turn,
+            own_even, own_odd, mix, side, gain, bias, forward, flipped, back, turn,
             expand, reduce,
         )
         if last:

time: 119 us -> 106 us (0.89)
  starting transfers between devices: 37.2 us -> 28.6 us
  Pallas kernels: 63.2 us -> 59.3 us
    ppermute x4 -> x0, starting transfers between devices: 10.4 us -> none  [the longest x2 10.3 us: body(): corner_odd = lax.ppermute(corner, ('gx', 'gy'), lat_odd)]
    pallas_call x2, Pallas kernels: 33.8 us -> 30.3 us  [run_block(): pl.pallas_call(functools.partial(block_kernel, last, block), out_shape=ou...]
    ppermute x2, starting transfers between devices: 7.17 us -> 9.09 us  [body(): row_odd = lax.ppermute(row_odd, ('gx', 'gy'), lat_odd)]
    ppermute x2, waiting for transfers between devices: 0.01 us -> 1.42 us  [body(): row_odd = lax.ppermute(row_odd, ('gx', 'gy'), lat_odd)]
    unnamed x58 -> x60, local copies, waits for them, and re-layouts: 7.17 us -> 7.4 us
  transfers between devices with their start and end apart: 13 -> 9, of which waited for: 2 -> 3; matrix products, arithmetic and copies ran while one was open for 7% -> 6% of each run, Pallas kernels for 20% -> 21%
where the time goes in v3:
time: 106 us
  Pallas kernels  59.3 us (56%)
  starting transfers between devices  28.6 us (27%)
  local copies, waits for them, and re-layouts  11.7 us (11%)
  waiting for transfers between devices  2.67 us (3%)
  other arithmetic  2.22 us (2%)
  between operations  1.11 us (1%)
    pallas_call x2, Pallas kernels, run_block(): pl.pallas_call(functools.partial(block_kernel, last, block), out_shape=ou...  30.3 us
    pallas_call x4, Pallas kernels, run_product(): pl.pallas_call(functools.partial(product_kernel, first), out_shape=[shape...  16.1 us
    all_to_all x1, starting transfers between devices, body(): lax.all_to_all(atm_flux[0], ('gx', 'gy'), split_axis=0, concat_axis=0, ti...  10.8 us
    ppermute x2, starting transfers between devices, body(): row_odd = lax.ppermute(row_odd, ('gx', 'gy'), lat_odd)  9.09 us
    unnamed x60, local copies, waits for them, and re-layouts  7.4 us
    ppermute x2, starting transfers between devices, body(): column_odd = lax.ppermute(own_odd, 'gx', lon_odd)  6.88 us
    pallas_call x1, Pallas kernels, run_stem(): pl.pallas_call(stem_kernel, out_shape=[shape(height, width, LANES)] + edg...  5.19 us
    pallas_call x2, Pallas kernels, run_transform(): pl.pallas_call(transform_kernel, out_shape=shape(height, width, 2 * LANES...  4.72 us
  transfers between devices with their start and end apart: 9, of which 3 were waited for; matrix products, arithmetic and copies ran while one was open for 6% of the time, Pallas kernels for 21%

profile of v3, /device:TPU:7, one launch (start us, length us, event | category | flops | bytes accessed | tf_op | source)
XLA Modules:
  0.0 105.6 jit_solution(17189446628469834089)
XLA Ops:
  0.0 10.8 %all-to-all-start = ((bf16[128,1,16,256]{3,2,1,0:T(8,128)(2,1)}), bf16[128,1,16,256]{3,2,1,0:T(8,128)(2,1)S(1)}, u32[]{:S(2)}, u32[]{:S(2)}) async-start(bf16[128,1,16,256]{3,2,1,0:T(8,128)(2,1)} %bitcast.36), calls=%async_computation | async-start | bytes 2097152 | tf_op jit(solution)/shard_map/all_to_all | solution.py:568
  12.3 0.6 pad.9.stem_ref
  13.3 0.7 pad.8.coef_ref
  14.3 1.0 copy.93
  15.8 0.8 copy-done.21
  17.1 1.8 %prepare.1 = (bf16[7,208,256]{2,1,0:T(8,128)(2,1)S(1)}, bf16[42,208,128]{2,1,0:T(8,128)(2,1)S(1)}, f32[208,128]{1,0:T(8,128)S(1)}, f32[2,208,128]{2,1,0:T(8,128)...) custom-call(bf16[2,208,160]{2,1,0:T(8,128)(2,1)S(1)} %copy-done.10, ...), custom_call_target="tpu_custom_call" | custom-call | flops 1005322240 | bytes 10000000 | tf_op jit(solution)/shard_map/prepare/pallas_call | solution.py:407
  19.0 1.4 %copy-done.1 = bf16[42,208,128]{2,1,0:T(8,128)(2,1)} copy-done((bf16[42,208,128]{2,1,0:T(8,128)(2,1)}, bf16[42,208,128]{2,1,0:T(8,128)(2,1)S(1)}, u32[]{:S(2)}) %copy-start.1) | copy-done | bytes 2236440
  20.3 1.4 %copy-done.3 = bf16[42,208,128]{2,1,0:T(8,128)(2,1)} copy-done((bf16[42,208,128]{2,1,0:T(8,128)(2,1)}, bf16[42,208,128]{2,1,0:T(8,128)(2,1)S(1)}, u32[]{:S(2)}) %copy-start.3) | copy-done | bytes 2236440
  21.7 0.7 copy-done.8
  22.4 0.7 copy-done.11
  23.1 0.6 copy-done.14
  23.7 0.6 copy-done.17
  24.4 0.6 reduce_sum.27
  25.8 0.6 pad_add_fusion.rows_ref
  26.5 1.2 %all-to-all-done = bf16[128,1,16,256]{3,2,1,0:T(8,128)(2,1)S(1)} async-done(((bf16[128,1,16,256]{3,2,1,0:T(8,128)(2,1)}), bf16[128,1,16,256]{3,2,1,0:T(8,128)(2,1)S(1)}, u32[]{:S(2)}, u32[]{:S(2)}) %all-to-all-start) | async-done | bytes 1048608 | tf_op jit(solution)/shard_map/all_to_all | solution.py:568
  27.8 0.8 copy-done.18
  28.6 5.2 %stem.1 = (bf16[64,208,128]{2,1,0:T(8,128)(2,1)S(1)}, bf16[3,208,128]{2,1,0:T(8,128)(2,1)S(1)}, bf16[3,208,128]{2,1,0:T(8,128)(2,1)S(1)}, bf16[2,208,128]{2,1,0:T(8,128)(2,1)S(1)}, bf16[2,208,128]{2,1,0:T(8,128)(2,1)S(1)}) custom-call(s32[49]{0:T(128)S(1)} %pad_add_fusion.rows_ref, s32[3]{0:T(128)S(1)} %pad_add_fusion.1.flags_ref, s32[128]{0:T(128)S(1)} %bitcast.35, ...), custom_call_target="tpu_custom_call" | custom-call | tf_op jit(solution)/shard_map/stem/pallas_call | solution.py:419
  33.8 0.7 collective-permute-start
  34.4 4.1 %collective-permute-start.1 = (bf16[2,208,128]{2,1,0:T(8,128)(2,1)S(1)}, bf16[2,208,128]{2,1,0:T(8,128)(2,1)S(1)}, u32[]{:S(2)}, u32[]{:S(2)}) collective-permute-start(bf16[2,208,128]{2,1,0:T(8,128)(2,1)S(1)} %get-tuple-element.58.own_odd_ref), channel_id=1, source_target_pairs={{0,120},{8,16},{16,8},{24,32},{32,24},{40,48},{48,40},{56,64},{64,... | collective-permute-start | bytes 319496 | tf_op jit(solution)/shard_map/ppermute | solution.py:597
  38.6 2.4 %transform.2.wave_ref.after_ref = bf16[64,208,256]{2,1,0:T(8,128)(2,1)S(1)} custom-call(bf16[64,208,128]{2,1,0:T(8,128)(2,1)S(1)} %get-tuple-element.55.state_ref, bf16[128,256]{1,0:T(8,128)(2,1)S(1)} %copy-done.5), custom_call_target="tpu_custom_call" | custom-call | flops 872415232 | bytes 10000000 | tf_op jit(solution)/shard_map/transform/pallas_call | solution.py:437
  40.9 2.6 %product.4.after_ref.prod_one_ref = bf16[48,64,128]{2,1,0:T(8,128)(2,1)S(1)} custom-call(s32[49]{0:T(128)S(1)} %pad_add_fusion.rows_ref, bf16[64,208,256]{2,1,0:T(8,128)(2,1)S(1)} %transform.2.wave_ref.after_ref, bf16[7,208,256]{2,1,0:T(8,128)(2,1)S(1)} %get-tuple-element.56.mix_ref, bf16[64,208,256]{2,1,0:T(8,128)(2,1)S(1)} %transform.2.wave_ref.after_ref), custom_call_target="tpu_custom_call" | custom-call | flops 11010048 | bytes 20000000 | tf_op jit(solution)/shard_map/product/pallas_call | solution.py:452
  44.2 1.0 collective-permute-start.2
  45.2 4.9 %collective-permute-start.3 = (bf16[5,208,128]{2,1,0:T(8,128)(2,1)S(1)}, bf16[5,208,128]{2,1,0:T(8,128)(2,1)S(1)}, u32[]{:S(2)}, u32[]{:S(2)}) collective-permute-start(bf16[5,208,128]{2,1,0:T(8,128)(2,1)S(1)} %get-tuple-element.61.after_ref), channel_id=1, source_target_pairs={{1,2},{2,1},{3,4},{4,3},{5,6},{6,5},{7,127},{9,10},{10,9},{11,12},... | collective-permute-start | bytes 798728 | tf_op jit(solution)/shard_map/ppermute | solution.py:605
  50.2 5.4 %product.5 = (bf16[48,144,128]{2,1,0:T(8,128)(2,1)S(1)}, bf16[12,208,256]{2,1,0:T(8,128)(2,1)S(1)}) custom-call(s32[49]{0:T(128)S(1)} %pad_add_fusion.rows_ref, bf16[64,208,256]{2,1,0:T(8,128)(2,1)S(1)} %transform.2.wave_ref.after_ref, bf16[7,208,256]{2,1,0:T(8,128)(2,1)S(1)} %get-tuple-element.56.mix_ref, bf16[5,208,128]{2,1,0:T(8,128)(2,1)S(1)} %get-tuple-element.61.after_ref), custom_call_target="tpu_custom_call" | custom-call | flops 24772608 | bytes 20000000 | tf_op jit(solution)/shard_map/product/pallas_call | solution.py:452
  56.0 14.0 %block.2 = (bf16[64,208,128]{2,1,0:T(8,128)(2,1)S(1)}, bf16[3,208,128]{2,1,0:T(8,128)(2,1)S(1)}, bf16[3,208,128]{2,1,0:T(8,128)(2,1)S(1)}, bf16[2,208,128]{2,1,0:T(8,128)(2,1)S(1)}, bf16[2,208,128]{2,1,0:T(8,128)(2,1)S(1)}) custom-call(s32[49]{0:T(128)S(1)} %pad_add_fusion.rows_ref, s32[3]{0:T(128)S(1)} %pad_add_fusion.1.flags_ref, ...), custom_call_target="tpu_custom_call" | custom-call | tf_op jit(solution)/shard_map/block/pallas_call | solution.py:495
  70.1 2.8 %collective-permute-start.5 = (bf16[2,208,128]{2,1,0:T(8,128)(2,1)S(1)}, bf16[2,208,128]{2,1,0:T(8,128)(2,1)S(1)}, u32[]{:S(2)}, u32[]{:S(2)}) collective-permute-start(bf16[2,208,128]{2,1,0:T(8,128)(2,1)S(1)} %get-tuple-element.73.own_odd_ref), channel_id=1, source_target_pairs={{0,120},{8,16},{16,8},{24,32},{32,24},{40,48},{48,40},{56,64},{64,... | collective-permute-start | bytes 319496 | tf_op jit(solution)/shard_map/ppermute | solution.py:597
  72.9 2.4 %transform.3.wave_ref.after_ref = bf16[64,208,256]{2,1,0:T(8,128)(2,1)S(1)} custom-call(bf16[64,208,128]{2,1,0:T(8,128)(2,1)S(1)} %get-tuple-element.70.state_ref, bf16[128,256]{1,0:T(8,128)(2,1)S(1)} %copy-done.5), custom_call_target="tpu_custom_call" | custom-call | flops 872415232 | bytes 10000000 | tf_op jit(solution)/shard_map/transform/pallas_call | solution.py:437
  75.2 2.6 %product.6.after_ref.prod_one_ref = bf16[48,64,128]{2,1,0:T(8,128)(2,1)S(1)} custom-call(s32[49]{0:T(128)S(1)} %pad_add_fusion.rows_ref, bf16[64,208,256]{2,1,0:T(8,128)(2,1)S(1)} %transform.3.wave_ref.after_ref, bf16[7,208,256]{2,1,0:T(8,128)(2,1)S(1)} %get-tuple-element.71.mix_ref, bf16[64,208,256]{2,1,0:T(8,128)(2,1)S(1)} %transform.3.wave_ref.after_ref), custom_call_target="tpu_custom_call" | custom-call | flops 11010048 | bytes 20000000 | tf_op jit(solution)/shard_map/product/pallas_call | solution.py:452
  78.6 4.2 %collective-permute-start.7 = (bf16[5,208,128]{2,1,0:T(8,128)(2,1)S(1)}, bf16[5,208,128]{2,1,0:T(8,128)(2,1)S(1)}, u32[]{:S(2)}, u32[]{:S(2)}) collective-permute-start(bf16[5,208,128]{2,1,0:T(8,128)(2,1)S(1)} %get-tuple-element.76.after_ref), channel_id=1, source_target_pairs={{1,2},{2,1},{3,4},{4,3},{5,6},{6,5},{7,127},{9,10},{10,9},{11,12},... | collective-permute-start | bytes 798728 | tf_op jit(solution)/shard_map/ppermute | solution.py:605
  82.8 5.4 %product.7 = (bf16[48,144,128]{2,1,0:T(8,128)(2,1)S(1)}, bf16[12,208,256]{2,1,0:T(8,128)(2,1)S(1)}) custom-call(s32[49]{0:T(128)S(1)} %pad_add_fusion.rows_ref, bf16[64,208,256]{2,1,0:T(8,128)(2,1)S(1)} %transform.3.wave_ref.after_ref, bf16[7,208,256]{2,1,0:T(8,128)(2,1)S(1)} %get-tuple-element.71.mix_ref, bf16[5,208,128]{2,1,0:T(8,128)(2,1)S(1)} %get-tuple-element.76.after_ref), custom_call_target="tpu_custom_call" | custom-call | flops 24772608 | bytes 20000000 | tf_op jit(solution)/shard_map/product/pallas_call | solution.py:452
  88.2 1.0 collective-permute-done.7.row_odd_ref
  89.2 16.3 %block.3 = bf16[200,64,128]{2,1,0:T(8,128)(2,1)} custom-call(s32[49]{0:T(128)S(1)} %pad_add_fusion.rows_ref, s32[3]{0:T(128)S(1)} %pad_add_fusion.1.flags_ref, bf16[64,208,128]{2,1,0:T(8,128)(2,1)S(1)} %get-tuple-element.70.state_ref, bf16[48,64,128]{2,1,0:T(8,128)(2,1)S(1)} %product.6.after_ref.prod_one_ref, ...), custom_call_target="tpu_custom_call" | custom-call | tf_op jit(solution)/shard_map/block/pallas_call | solution.py:495
  (88 shorter events, 5.1 us)
Async XLA Ops:
  0.0 10.8 %copy-start.26 = (f32[2,200]{1,0:T(2,128)S(1)}, f32[2,200]{1,0:T(2,128)}, u32[]{:S(2)}) copy-start(f32[2,200]{1,0:T(2,128)} %param.20) | copy-start | bytes 4804
  0.0 10.9 %copy-start.27 = (f32[2,200]{1,0:T(2,128)S(1)}, f32[2,200]{1,0:T(2,128)}, u32[]{:S(2)}) copy-start(f32[2,200]{1,0:T(2,128)} %param.21) | copy-start | bytes 4804
  0.0 10.9 %copy-start.25 = (f32[2,800]{1,0:T(2,128)S(1)}, f32[2,800]{1,0:T(2,128)}, u32[]{:S(2)}) copy-start(f32[2,800]{1,0:T(2,128)} %param.23) | copy-start | bytes 19204
  0.0 10.9 %copy-start.24 = (bf16[200,16,2,2]{0,3,2,1:T(2,128)(2,1)S(1)}, bf16[200,16,2,2]{0,3,2,1:T(2,128)(2,1)}, u32[]{:S(2)}) copy-start(bf16[200,16,2,2]{0,3,2,1:T(2,128)(2,1)} %param.18) | copy-start | bytes 76804
  0.0 11.0 %copy-start.23 = (f32[2,200,7,7]{1,0,3,2:T(2,128)S(1)}, f32[2,200,7,7]{1,0,3,2:T(2,128)}, u32[]{:S(2)}) copy-start(f32[2,200,7,7]{1,0,3,2:T(2,128)} %param.19) | copy-start | bytes 235204
  0.0 27.7 %all-to-all-start = ((bf16[128,1,16,256]{3,2,1,0:T(8,128)(2,1)}), bf16[128,1,16,256]{3,2,1,0:T(8,128)(2,1)S(1)}, u32[]{:S(2)}, u32[]{:S(2)}) async-start(bf16[128,1,16,256]{3,2,1,0:T(8,128)(2,1)} %bitcast.36), calls=%async_computation | async-start | bytes 2097152 | tf_op jit(solution)/shard_map/all_to_all | solution.py:568
  11.4 3.9 %copy-start.22 = (bf16[2,200,800]{2,1,0:T(8,128)(2,1)S(1)}, bf16[2,200,800]{2,1,0:T(8,128)(2,1)}, u32[]{:S(2)}) copy-start(bf16[2,200,800]{2,1,0:T(8,128)(2,1)} %param.22) | copy-start | bytes 1920004
  15.6 1.5 %copy-start.10 = (bf16[2,208,160]{2,1,0:T(8,128)(2,1)S(1)}, bf16[2,208,160]{2,1,0:T(8,128)(2,1)}, u32[]{:S(2)}) copy-start(bf16[2,208,160]{2,1,0:T(8,128)(2,1)} %pad.8.coef_ref) | copy-start | bytes 399364
  15.6 1.5 %copy-start.16 = (bf16[208,64]{1,0:T(8,128)(2,1)S(1)}, bf16[208,64]{1,0:T(8,128)(2,1)}, u32[]{:S(2)}) copy-start(bf16[208,64]{1,0:T(8,128)(2,1)} %pad.9.stem_ref) | copy-start | bytes 79876
  15.6 1.5 %copy-start.20 = (bf16[160,2176]{1,0:T(8,128)(2,1)S(1)}, bf16[160,2176]{1,0:T(8,128)(2,1)}, u32[]{:S(2)}) copy-start(bf16[160,2176]{1,0:T(8,128)(2,1)} %constant.56.clone.table_ref) | copy-start | bytes 2088964
  17.1 7.3 %copy-start.28 = (s32[64,1]{0,1:T(1,128)S(1)}, s32[64,1]{0,1:T(1,128)}, u32[]{:S(2)}) copy-start(s32[64,1]{0,1:T(1,128)} %param.17) | copy-start | bytes 772
  17.1 10.7 %copy-start.19 = (s32[128,1]{0,1:T(1,128)S(1)}, s32[128,1]{0,1:T(1,128)}, u32[]{:S(2)}) copy-start(s32[128,1]{0,1:T(1,128)} %param.16) | copy-start | bytes 1540
  17.1 21.4 %copy-start.5 = (bf16[128,256]{1,0:T(8,128)(2,1)S(1)}, bf16[128,256]{1,0:T(8,128)(2,1)}, u32[]{:S(2)}) copy-start(bf16[128,256]{1,0:T(8,128)(2,1)} %constant.53.clone.forward_ref) | copy-start | bytes 196612
  19.0 1.4 %copy-start.1 = (bf16[42,208,128]{2,1,0:T(8,128)(2,1)}, bf16[42,208,128]{2,1,0:T(8,128)(2,1)S(1)}, u32[]{:S(2)}) copy-start(bf16[42,208,128]{2,1,0:T(8,128)(2,1)S(1)} %get-tuple-element.80.side_ref) | copy-start | bytes 6709252
  20.3 1.4 %copy-start.3 = (bf16[42,208,128]{2,1,0:T(8,128)(2,1)}, bf16[42,208,128]{2,1,0:T(8,128)(2,1)S(1)}, u32[]{:S(2)}) copy-start(bf16[42,208,128]{2,1,0:T(8,128)(2,1)S(1)} %get-tuple-element.65.side_ref) | copy-start | bytes 6709252
  33.8 9.8 %collective-permute-start = (bf16[2,208,128]{2,1,0:T(8,128)(2,1)S(1)}, bf16[2,208,128]{2,1,0:T(8,128)(2,1)S(1)}, u32[]{:S(2)}, u32[]{:S(2)}) collective-permute-start(bf16[2,208,128]{2,1,0:T(8,128)(2,1)S(1)} %get-tuple-element.57.own_even_ref), channel_id=1, source_target_pairs={{0,8},{8,0},{16,24},{24,16},{32,40},{40,32},{48,56},{56,48},{64,72... | collective-permute-start | bytes 319496 | tf_op jit(solution)/shard_map/ppermute | solution.py:596
  34.4 9.2 %collective-permute-start.1 = (bf16[2,208,128]{2,1,0:T(8,128)(2,1)S(1)}, bf16[2,208,128]{2,1,0:T(8,128)(2,1)S(1)}, u32[]{:S(2)}, u32[]{:S(2)}) collective-permute-start(bf16[2,208,128]{2,1,0:T(8,128)(2,1)S(1)} %get-tuple-element.58.own_odd_ref), channel_id=1, source_target_pairs={{0,120},{8,16},{16,8},{24,32},{32,24},{40,48},{48,40},{56,64},{64,... | collective-permute-start | bytes 319496 | tf_op jit(solution)/shard_map/ppermute | solution.py:597
  44.2 11.4 %collective-permute-start.2 = (bf16[5,208,128]{2,1,0:T(8,128)(2,1)S(1)}, bf16[5,208,128]{2,1,0:T(8,128)(2,1)S(1)}, u32[]{:S(2)}, u32[]{:S(2)}) collective-permute-start(bf16[5,208,128]{2,1,0:T(8,128)(2,1)S(1)} %get-tuple-element.64), channel_id=1, source_target_pairs={{0,1},{1,0},{2,3},{3,2},{4,5},{5,4},{6,7},{7,6},{8,9},{9,8},{10,11... | collective-permute-start | bytes 798728 | tf_op jit(solution)/shard_map/ppermute | solution.py:604
  45.2 10.8 %copy-start = (bf16[2,800,200]{1,2,0:T(8,128)(2,1)S(1)}, bf16[2,800,200]{1,2,0:T(8,128)(2,1)}, u32[]{:S(2)}) copy-start(bf16[2,800,200]{1,2,0:T(8,128)(2,1)} %param.24) | copy-start | bytes 1920004
  45.2 10.8 %copy-start.4 = (bf16[42,208,128]{2,1,0:T(8,128)(2,1)S(1)}, bf16[42,208,128]{2,1,0:T(8,128)(2,1)}, u32[]{:S(2)}) copy-start(bf16[42,208,128]{2,1,0:T(8,128)(2,1)} %copy-done.3) | copy-start | bytes 6709252
  45.2 10.8 %copy-start.6 = (bf16[256,128]{1,0:T(8,128)(2,1)S(1)}, bf16[256,128]{1,0:T(8,128)(2,1)}, u32[]{:S(2)}) copy-start(bf16[256,128]{1,0:T(8,128)(2,1)} %constant.54.clone.inverse_ref) | copy-start | bytes 196612
  45.2 10.8 %copy-start.7 = (bf16[128,256]{1,0:T(8,128)(2,1)S(1)}, bf16[128,256]{1,0:T(8,128)(2,1)}, u32[]{:S(2)}) copy-start(bf16[128,256]{1,0:T(8,128)(2,1)} %constant.52.clone.flipped_ref) | copy-start | bytes 196612
  45.2 10.8 %copy-start.12 = (f32[2,208,128]{2,1,0:T(8,128)S(1)}, f32[2,208,128]{2,1,0:T(8,128)}, u32[]{:S(2)}) copy-start(f32[2,208,128]{2,1,0:T(8,128)} %copy-done.11) | copy-start | bytes 638980
  45.2 10.8 %copy-start.13 = (bf16[128,128]{1,0:T(8,128)(2,1)S(1)}, bf16[128,128]{1,0:T(8,128)(2,1)}, u32[]{:S(2)}) copy-start(bf16[128,128]{1,0:T(8,128)(2,1)} %constant.55.clone.turn_ref) | copy-start | bytes 98308
  45.2 10.8 %copy-start.15 = (f32[208,128]{1,0:T(8,128)S(1)}, f32[208,128]{1,0:T(8,128)}, u32[]{:S(2)}) copy-start(f32[208,128]{1,0:T(8,128)} %copy-done.14) | copy-start | bytes 319492
  45.2 10.7 %collective-permute-start.3 = (bf16[5,208,128]{2,1,0:T(8,128)(2,1)S(1)}, bf16[5,208,128]{2,1,0:T(8,128)(2,1)S(1)}, u32[]{:S(2)}, u32[]{:S(2)}) collective-permute-start(bf16[5,208,128]{2,1,0:T(8,128)(2,1)S(1)} %get-tuple-element.61.after_ref), channel_id=1, source_target_pairs={{1,2},{2,1},{3,4},{4,3},{5,6},{6,5},{7,127},{9,10},{10,9},{11,12},... | collective-permute-start | bytes 798728 | tf_op jit(solution)/shard_map/ppermute | solution.py:605
  70.0 7.9 %collective-permute-start.4 = (bf16[2,208,128]{2,1,0:T(8,128)(2,1)S(1)}, bf16[2,208,128]{2,1,0:T(8,128)(2,1)S(1)}, u32[]{:S(2)}, u32[]{:S(2)}) collective-permute-start(bf16[2,208,128]{2,1,0:T(8,128)(2,1)S(1)} %get-tuple-element.72.own_even_ref), channel_id=1, source_target_pairs={{0,8},{8,0},{16,24},{24,16},{32,40},{40,32},{48,56},{56,48},{64,72... | collective-permute-start | bytes 319496 | tf_op jit(solution)/shard_map/ppermute | solution.py:596
  70.1 7.8 %collective-permute-start.5 = (bf16[2,208,128]{2,1,0:T(8,128)(2,1)S(1)}, bf16[2,208,128]{2,1,0:T(8,128)(2,1)S(1)}, u32[]{:S(2)}, u32[]{:S(2)}) collective-permute-start(bf16[2,208,128]{2,1,0:T(8,128)(2,1)S(1)} %get-tuple-element.73.own_odd_ref), channel_id=1, source_target_pairs={{0,120},{8,16},{16,8},{24,32},{32,24},{40,48},{48,40},{56,64},{64,... | collective-permute-start | bytes 319496 | tf_op jit(solution)/shard_map/ppermute | solution.py:597
  78.5 9.7 %collective-permute-start.6 = (bf16[5,208,128]{2,1,0:T(8,128)(2,1)S(1)}, bf16[5,208,128]{2,1,0:T(8,128)(2,1)S(1)}, u32[]{:S(2)}, u32[]{:S(2)}) collective-permute-start(bf16[5,208,128]{2,1,0:T(8,128)(2,1)S(1)} %get-tuple-element.79), channel_id=1, source_target_pairs={{0,1},{1,0},{2,3},{3,2},{4,5},{5,4},{6,7},{7,6},{8,9},{9,8},{10,11... | collective-permute-start | bytes 798728 | tf_op jit(solution)/shard_map/ppermute | solution.py:604
  78.6 10.6 %copy-start.2 = (bf16[42,208,128]{2,1,0:T(8,128)(2,1)S(1)}, bf16[42,208,128]{2,1,0:T(8,128)(2,1)}, u32[]{:S(2)}) copy-start(bf16[42,208,128]{2,1,0:T(8,128)(2,1)} %copy-done.1) | copy-start | bytes 6709252
  78.6 10.6 %copy-start.9 = (f32[2,208,128]{2,1,0:T(8,128)S(1)}, f32[2,208,128]{2,1,0:T(8,128)}, u32[]{:S(2)}) copy-start(f32[2,208,128]{2,1,0:T(8,128)} %copy-done.8) | copy-start | bytes 638980
  78.6 10.6 %collective-permute-start.7 = (bf16[5,208,128]{2,1,0:T(8,128)(2,1)S(1)}, bf16[5,208,128]{2,1,0:T(8,128)(2,1)S(1)}, u32[]{:S(2)}, u32[]{:S(2)}) collective-permute-start(bf16[5,208,128]{2,1,0:T(8,128)(2,1)S(1)} %get-tuple-element.76.after_ref), channel_id=1, source_target_pairs={{1,2},{2,1},{3,4},{4,3},{5,6},{6,5},{7,127},{9,10},{10,9},{11,12},... | collective-permute-start | bytes 798728 | tf_op jit(solution)/shard_map/ppermute | solution.py:605
  (6 other events, 4.5 us)

commit v4 on v3

--- a/solution.py
+++ b/solution.py
@@ -195,8 +195,8 @@
         weights = [mix_ref[tap, span] for tap in range(7)]
 
         def some_rows(index, _):
-            for at in range(GROUP):
-                spot = index * GROUP + at
+            for at in range(UNROLL):
+                spot = index * UNROLL + at
                 base = jnp.clip(rows_ref[1 + spot] - 3, 0, height - 7)
                 terms = []
                 for tap in range(7):
@@ -206,7 +206,7 @@
                 prod_ref[spot, target] = tree_sum(terms)
             return 0
 
-        lax.fori_loop(0, MOST // GROUP, some_rows, 0)
+        lax.fori_loop(0, MOST // UNROLL, some_rows, 0)
         return 0
 
     lax.fori_loop(0, prod_ref.shape[1] // 16, channel_band, 0)
@@ -216,7 +216,7 @@
                  column_even_ref, column_odd_ref, own_even_ref, own_odd_ref, mix_ref, side_ref, gain_ref,
                  bias_ref, forward_ref, flipped_ref, inverse_ref, turn_ref, expand_ref, reduce_ref, *rest):
     if last:
-        out_ref, halo_ref, fix_ref, edge_ref, grid_ref, normed_ref, held_ref = rest
+        out_ref, halo_ref, fix_ref, edge_ref, grid_ref, normed_ref, held_ref, wet_ref, ready_ref, copy_sem = rest
     else:
         (out_ref, send_row_even_ref, send_row_odd_ref, send_column_even_ref, send_column_odd_ref,
          halo_ref, fix_ref, edge_ref, grid_ref, normed_ref, low_ref, high_ref) = rest
@@ -309,7 +309,7 @@
     lax.fori_loop(0, width // 16, rim, 0)
 
     if last:
-        held_ref[...] = jnp.zeros_like(held_ref)
+        wet_ref[...] = jnp.zeros_like(wet_ref)
     else:
         out_ref[...] = jnp.zeros_like(out_ref)
         low_ref[...] = jnp.zeros_like(low_ref)
@@ -351,6 +351,7 @@
             value = branch[:, at * LANES:(at + 1) * LANES] + state_ref[row].astype(F32)[:channels]
             if last:
                 held_ref[pl.ds(row, channels, stride=pitch), :] = value
+                wet_ref[pl.ds(row, 1), :] = jnp.ones((1, LANES), F32)
             else:
                 value = jnp.concatenate([value, jnp.zeros((width - channels, LANES), F32)], axis=0).astype(BF16)
                 out_ref[row] = value
@@ -366,11 +367,23 @@
             pointwise(index, index % 2)
 
     if last:
-        def finish(index, _):
-            out_ref[pl.ds(index * 8, 8)] = held_ref[pl.ds(index * 8 * pitch, 8 * pitch), :].reshape(8, pitch, LANES)[:, :height].astype(BF16)
-            return 0
-
-        lax.fori_loop(0, channels // 8, finish, 0)
+        wet = wet_ref[...] > 0.0
+        part = channels // PARTS
+        copies = []
+        for at in range(PARTS):
+            def finish(index, _):
+                base = at * part + index * 8
+                value = held_ref[pl.ds(base * pitch, 8 * pitch), :].reshape(8, pitch, LANES)[:, :height]
+                ready_ref[pl.ds(base, 8)] = jnp.where(wet[None], value, 0.0).astype(BF16)
+                return 0
+
+            lax.fori_loop(0, part // 8, finish, 0)
+            span = pl.ds(at * part, part)
+            copy = pltpu.make_async_copy(ready_ref.at[span], out_ref.at[span], copy_sem.at[at])
+            copy.start()
+            copies.append(copy)
+        for copy in copies:
+            copy.wait()
     else:
         send_edges(flags_ref, out_ref, low_ref, high_ref, (send_row_even_ref, send_row_odd_ref),
                    (send_column_even_ref, send_column_odd_ref))
@@ -378,6 +391,8 @@
 
 GELU = jnp.bfloat16
 MOST = 48
+PARTS = 5
+UNROLL = 24
 EARLY = 4
 
 
@@ -488,7 +503,12 @@
     height, width, _ = state.shape
     if last:
         out_shape = [shape(200, height, LANES)]
-        extra = [pltpu.VMEM((200 * (height + 8), LANES), F32)]
+        extra = [
+            pltpu.VMEM((200 * (height + 8), LANES), F32),
+            pltpu.VMEM((height, LANES), F32),
+            pltpu.VMEM((200, height, LANES), BF16),
+            pltpu.SemaphoreType.DMA((PARTS,)),
+        ]
     else:
         out_shape = [shape(height, width, LANES)] + edge_shapes(width)
         extra = [pltpu.VMEM((2, width, LANES), BF16)] * 2
@@ -496,7 +516,7 @@
         functools.partial(block_kernel, last, block),
         out_shape=out_shape,
         in_specs=[smem(), smem()] + [vmem()] * (1 + len(arrays)),
-        out_specs=[vmem()] * len(out_shape),
+        out_specs=[pl.BlockSpec(memory_space=pl.ANY) if last else vmem()] * len(out_shape),
         scratch_shapes=[
             pltpu.VMEM((6, width, 2 * LANES), BF16),
             pltpu.VMEM((6, width, LANES), BF16),
@@ -579,7 +599,7 @@
     coef = coefficients(depth_weight, depth_bias, norm_gain, width)
     prepared = run_prepare(coef, jnp.asarray(prepare_table(), BF16), stem)
     expand, reduce = pointwise_weights(expand_weight, expand_bias, reduce_weight, width)
-    arrived, prepared, expand, reduce = lax.optimization_barrier((arrived, prepared, expand, reduce))
+    arrived, expand = lax.optimization_barrier((arrived, expand))
     state, *edges = run_stem(rows, flags, owner, arrived, prepared[-1], height, width)
     lon_even = [(i, i ^ 1) for i in range(lon_count)]
     lon_odd = [(i, ((i - 1 ^ 1) + 1) % lon_count) for i in range(lon_count)]

time: 106 us -> 105 us (level)
  Pallas kernels: 59.3 us -> 57.1 us
    pallas_call x4, Pallas kernels: 16.1 us -> 14.7 us  [run_product(): pl.pallas_call(functools.partial(product_kernel, first), out_shape=[shape...]
  transfers between devices with their start and end apart: 9 -> 9, of which waited for: 3 -> 3; matrix products, arithmetic and copies ran while one was open for 6% -> 7% of each run, Pallas kernels for 21% -> 20%
where the time goes in v4:
time: 105 us
  Pallas kernels  57.1 us (54%)
  starting transfers between devices  29 us (28%)
  local copies, waits for them, and re-layouts  11.7 us (11%)
  waiting for transfers between devices  3.53 us (3%)
  other arithmetic  2.22 us (2%)
  between operations  1.29 us (1%)
    pallas_call x2, Pallas kernels, run_block(): pl.pallas_call(functools.partial(block_kernel, last, block), out_shape=ou...  29.5 us
    pallas_call x4, Pallas kernels, run_product(): pl.pallas_call(functools.partial(product_kernel, first), out_shape=[shape...  14.7 us
    all_to_all x1, starting transfers between devices, body(): lax.all_to_all(atm_flux[0], ('gx', 'gy'), split_axis=0, concat_axis=0, ti...  10.8 us
    ppermute x2, starting transfers between devices, body(): row_odd = lax.ppermute(row_odd, ('gx', 'gy'), lat_odd)  9.23 us
    unnamed x60, local copies, waits for them, and re-layouts  7.4 us
    ppermute x2, starting transfers between devices, body(): column_odd = lax.ppermute(own_odd, 'gx', lon_odd)  7.18 us
    pallas_call x1, Pallas kernels, run_stem(): pl.pallas_call(stem_kernel, out_shape=[shape(height, width, LANES)] + edg...  5.18 us
    pallas_call x2, Pallas kernels, run_transform(): pl.pallas_call(transform_kernel, out_shape=shape(height, width, 2 * LANES...  4.71 us
  transfers between devices with their start and end apart: 9, of which 3 were waited for; matrix products, arithmetic and copies ran while one was open for 7% of the time, Pallas kernels for 20%

profile of v4, /device:TPU:7, one launch (start us, length us, event | category | flops | bytes accessed | tf_op | source)
XLA Modules:
  0.0 104.8 jit_solution(8477651205888308027)
XLA Ops:
  0.0 10.8 %all-to-all-start = ((bf16[128,1,16,256]{3,2,1,0:T(8,128)(2,1)}), bf16[128,1,16,256]{3,2,1,0:T(8,128)(2,1)S(1)}, u32[]{:S(2)}, u32[]{:S(2)}) async-start(bf16[128,1,16,256]{3,2,1,0:T(8,128)(2,1)} %bitcast.36), calls=%async_computation | async-start | bytes 2097152 | tf_op jit(solution)/shard_map/all_to_all | solution.py:588
  12.3 0.6 pad.9.stem_ref
  13.3 0.7 pad.8.coef_ref
  14.3 1.0 copy.82
  15.8 0.8 copy-done.21
  17.1 1.8 %prepare.1 = (bf16[7,208,256]{2,1,0:T(8,128)(2,1)S(1)}, bf16[42,208,128]{2,1,0:T(8,128)(2,1)S(1)}, f32[208,128]{1,0:T(8,128)S(1)}, f32[2,208,128]{2,1,0:T(8,128)...) custom-call(bf16[2,208,160]{2,1,0:T(8,128)(2,1)S(1)} %copy-done.10, ...), custom_call_target="tpu_custom_call" | custom-call | flops 1005322240 | bytes 10000000 | tf_op jit(solution)/shard_map/prepare/pallas_call | solution.py:422
  19.0 1.4 %copy-done.1 = bf16[42,208,128]{2,1,0:T(8,128)(2,1)} copy-done((bf16[42,208,128]{2,1,0:T(8,128)(2,1)}, bf16[42,208,128]{2,1,0:T(8,128)(2,1)S(1)}, u32[]{:S(2)}) %copy-start.1) | copy-done | bytes 2236440
  20.3 1.4 %copy-done.3 = bf16[42,208,128]{2,1,0:T(8,128)(2,1)} copy-done((bf16[42,208,128]{2,1,0:T(8,128)(2,1)}, bf16[42,208,128]{2,1,0:T(8,128)(2,1)S(1)}, u32[]{:S(2)}) %copy-start.3) | copy-done | bytes 2236440
  21.7 0.7 copy-done.8
  22.4 0.7 copy-done.11
  23.1 0.6 copy-done.14
  23.7 0.6 copy-done.17
  25.8 0.6 pad_add_fusion.rows_ref
  26.5 1.2 %all-to-all-done = bf16[128,1,16,256]{3,2,1,0:T(8,128)(2,1)S(1)} async-done(((bf16[128,1,16,256]{3,2,1,0:T(8,128)(2,1)}), bf16[128,1,16,256]{3,2,1,0:T(8,128)(2,1)S(1)}, u32[]{:S(2)}, u32[]{:S(2)}) %all-to-all-start) | async-done | bytes 1048608 | tf_op jit(solution)/shard_map/all_to_all | solution.py:588
  27.8 0.8 copy-done.18
  28.6 5.2 %stem.1 = (bf16[64,208,128]{2,1,0:T(8,128)(2,1)S(1)}, bf16[3,208,128]{2,1,0:T(8,128)(2,1)S(1)}, bf16[3,208,128]{2,1,0:T(8,128)(2,1)S(1)}, bf16[2,208,128]{2,1,0:T(8,128)(2,1)S(1)}, bf16[2,208,128]{2,1,0:T(8,128)(2,1)S(1)}) custom-call(s32[49]{0:T(128)S(1)} %pad_add_fusion.rows_ref, s32[3]{0:T(128)S(1)} %pad_add_fusion.1.flags_ref, s32[128]{0:T(128)S(1)} %bitcast.35, ...), custom_call_target="tpu_custom_call" | custom-call | tf_op jit(solution)/shard_map/stem/pallas_call | solution.py:434
  33.8 0.7 collective-permute-start
  34.4 4.1 %collective-permute-start.1 = (bf16[2,208,128]{2,1,0:T(8,128)(2,1)S(1)}, bf16[2,208,128]{2,1,0:T(8,128)(2,1)S(1)}, u32[]{:S(2)}, u32[]{:S(2)}) collective-permute-start(bf16[2,208,128]{2,1,0:T(8,128)(2,1)S(1)} %get-tuple-element.39.own_odd_ref), channel_id=1, source_target_pairs={{0,120},{8,16},{16,8},{24,32},{32,24},{40,48},{48,40},{56,64},{64,... | collective-permute-start | bytes 319496 | tf_op jit(solution)/shard_map/ppermute | solution.py:617
  38.6 2.4 %transform.2.wave_ref.after_ref = bf16[64,208,256]{2,1,0:T(8,128)(2,1)S(1)} custom-call(bf16[64,208,128]{2,1,0:T(8,128)(2,1)S(1)} %get-tuple-element.36.state_ref, bf16[128,256]{1,0:T(8,128)(2,1)S(1)} %copy-done.5), custom_call_target="tpu_custom_call" | custom-call | flops 872415232 | bytes 10000000 | tf_op jit(solution)/shard_map/transform/pallas_call | solution.py:452
  40.9 2.4 %product.4.after_ref.prod_one_ref = bf16[48,64,128]{2,1,0:T(8,128)(2,1)S(1)} custom-call(s32[49]{0:T(128)S(1)} %pad_add_fusion.rows_ref, bf16[64,208,256]{2,1,0:T(8,128)(2,1)S(1)} %transform.2.wave_ref.after_ref, bf16[7,208,256]{2,1,0:T(8,128)(2,1)S(1)} %get-tuple-element.37.mix_ref, bf16[64,208,256]{2,1,0:T(8,128)(2,1)S(1)} %transform.2.wave_ref.after_ref), custom_call_target="tpu_custom_call" | custom-call | flops 11010048 | bytes 20000000 | tf_op jit(solution)/shard_map/product/pallas_call | solution.py:467
  44.0 1.0 collective-permute-start.2
  45.0 5.1 %collective-permute-start.3 = (bf16[5,208,128]{2,1,0:T(8,128)(2,1)S(1)}, bf16[5,208,128]{2,1,0:T(8,128)(2,1)S(1)}, u32[]{:S(2)}, u32[]{:S(2)}) collective-permute-start(bf16[5,208,128]{2,1,0:T(8,128)(2,1)S(1)} %get-tuple-element.42.after_ref), channel_id=1, source_target_pairs={{1,2},{2,1},{3,4},{4,3},{5,6},{6,5},{7,127},{9,10},{10,9},{11,12},... | collective-permute-start | bytes 798728 | tf_op jit(solution)/shard_map/ppermute | solution.py:625
  50.2 4.9 %product.5 = (bf16[48,144,128]{2,1,0:T(8,128)(2,1)S(1)}, bf16[12,208,256]{2,1,0:T(8,128)(2,1)S(1)}) custom-call(s32[49]{0:T(128)S(1)} %pad_add_fusion.rows_ref, bf16[64,208,256]{2,1,0:T(8,128)(2,1)S(1)} %transform.2.wave_ref.after_ref, bf16[7,208,256]{2,1,0:T(8,128)(2,1)S(1)} %get-tuple-element.37.mix_ref, bf16[5,208,128]{2,1,0:T(8,128)(2,1)S(1)} %get-tuple-element.42.after_ref), custom_call_target="tpu_custom_call" | custom-call | flops 24772608 | bytes 20000000 | tf_op jit(solution)/shard_map/product/pallas_call | solution.py:467
  55.1 0.7 collective-permute-done.3.row_odd_ref
  55.8 14.0 %block.2 = (bf16[64,208,128]{2,1,0:T(8,128)(2,1)S(1)}, bf16[3,208,128]{2,1,0:T(8,128)(2,1)S(1)}, bf16[3,208,128]{2,1,0:T(8,128)(2,1)S(1)}, bf16[2,208,128]{2,1,0:T(8,128)(2,1)S(1)}, bf16[2,208,128]{2,1,0:T(8,128)(2,1)S(1)}) custom-call(s32[49]{0:T(128)S(1)} %pad_add_fusion.rows_ref, s32[3]{0:T(128)S(1)} %pad_add_fusion.1.flags_ref, ...), custom_call_target="tpu_custom_call" | custom-call | tf_op jit(solution)/shard_map/block/pallas_call | solution.py:515
  69.9 3.1 %collective-permute-start.5 = (bf16[2,208,128]{2,1,0:T(8,128)(2,1)S(1)}, bf16[2,208,128]{2,1,0:T(8,128)(2,1)S(1)}, u32[]{:S(2)}, u32[]{:S(2)}) collective-permute-start(bf16[2,208,128]{2,1,0:T(8,128)(2,1)S(1)} %get-tuple-element.53.own_odd_ref), channel_id=1, source_target_pairs={{0,120},{8,16},{16,8},{24,32},{32,24},{40,48},{48,40},{56,64},{64,... | collective-permute-start | bytes 319496 | tf_op jit(solution)/shard_map/ppermute | solution.py:617
  73.0 2.3 %transform.3.wave_ref.after_ref = bf16[64,208,256]{2,1,0:T(8,128)(2,1)S(1)} custom-call(bf16[64,208,128]{2,1,0:T(8,128)(2,1)S(1)} %get-tuple-element.50.state_ref, bf16[128,256]{1,0:T(8,128)(2,1)S(1)} %copy-done.5), custom_call_target="tpu_custom_call" | custom-call | flops 872415232 | bytes 10000000 | tf_op jit(solution)/shard_map/transform/pallas_call | solution.py:452
  75.3 2.4 %product.6.after_ref.prod_one_ref = bf16[48,64,128]{2,1,0:T(8,128)(2,1)S(1)} custom-call(s32[49]{0:T(128)S(1)} %pad_add_fusion.rows_ref, bf16[64,208,256]{2,1,0:T(8,128)(2,1)S(1)} %transform.3.wave_ref.after_ref, bf16[7,208,256]{2,1,0:T(8,128)(2,1)S(1)} %get-tuple-element.51.mix_ref, bf16[64,208,256]{2,1,0:T(8,128)(2,1)S(1)} %transform.3.wave_ref.after_ref), custom_call_target="tpu_custom_call" | custom-call | flops 11010048 | bytes 20000000 | tf_op jit(solution)/shard_map/product/pallas_call | solution.py:467
  78.5 4.1 %collective-permute-start.7 = (bf16[5,208,128]{2,1,0:T(8,128)(2,1)S(1)}, bf16[5,208,128]{2,1,0:T(8,128)(2,1)S(1)}, u32[]{:S(2)}, u32[]{:S(2)}) collective-permute-start(bf16[5,208,128]{2,1,0:T(8,128)(2,1)S(1)} %get-tuple-element.56.after_ref), channel_id=1, source_target_pairs={{1,2},{2,1},{3,4},{4,3},{5,6},{6,5},{7,127},{9,10},{10,9},{11,12},... | collective-permute-start | bytes 798728 | tf_op jit(solution)/shard_map/ppermute | solution.py:625
  82.6 4.9 %product.7 = (bf16[48,144,128]{2,1,0:T(8,128)(2,1)S(1)}, bf16[12,208,256]{2,1,0:T(8,128)(2,1)S(1)}) custom-call(s32[49]{0:T(128)S(1)} %pad_add_fusion.rows_ref, bf16[64,208,256]{2,1,0:T(8,128)(2,1)S(1)} %transform.3.wave_ref.after_ref, bf16[7,208,256]{2,1,0:T(8,128)(2,1)S(1)} %get-tuple-element.51.mix_ref, bf16[5,208,128]{2,1,0:T(8,128)(2,1)S(1)} %get-tuple-element.56.after_ref), custom_call_target="tpu_custom_call" | custom-call | flops 24772608 | bytes 20000000 | tf_op jit(solution)/shard_map/product/pallas_call | solution.py:467
  87.5 1.6 %collective-permute-done.7.row_odd_ref = bf16[5,208,128]{2,1,0:T(8,128)(2,1)S(1)} collective-permute-done((bf16[5,208,128]{2,1,0:T(8,128)(2,1)S(1)}, bf16[5,208,128]{2,1,0:T(8,128)(2,1)S(1)}, u32[]{:S(2)}, u32[]{:S(2)}) %collective-permute-start.7) | collective-permute-done | bytes 266272 | tf_op jit(solution)/shard_map/ppermute | solution.py:625
  89.1 15.5 %block.3 = bf16[200,64,128]{2,1,0:T(8,128)(2,1)} custom-call(s32[49]{0:T(128)S(1)} %pad_add_fusion.rows_ref, s32[3]{0:T(128)S(1)} %pad_add_fusion.1.flags_ref, bf16[64,208,128]{2,1,0:T(8,128)(2,1)S(1)} %get-tuple-element.50.state_ref, bf16[48,64,128]{2,1,0:T(8,128)(2,1)S(1)} %product.6.after_ref.prod_one_ref, ...), custom_call_target="tpu_custom_call" | custom-call | tf_op jit(solution)/shard_map/block/pallas_call | solution.py:515
  (88 shorter events, 5.3 us)
Async XLA Ops:
  0.0 10.8 %copy-start.26 = (f32[2,200]{1,0:T(2,128)S(1)}, f32[2,200]{1,0:T(2,128)}, u32[]{:S(2)}) copy-start(f32[2,200]{1,0:T(2,128)} %param.20) | copy-start | bytes 4804
  0.0 10.9 %copy-start.27 = (f32[2,200]{1,0:T(2,128)S(1)}, f32[2,200]{1,0:T(2,128)}, u32[]{:S(2)}) copy-start(f32[2,200]{1,0:T(2,128)} %param.21) | copy-start | bytes 4804
  0.0 10.9 %copy-start.25 = (f32[2,800]{1,0:T(2,128)S(1)}, f32[2,800]{1,0:T(2,128)}, u32[]{:S(2)}) copy-start(f32[2,800]{1,0:T(2,128)} %param.23) | copy-start | bytes 19204
  0.0 10.9 %copy-start.24 = (bf16[200,16,2,2]{0,3,2,1:T(2,128)(2,1)S(1)}, bf16[200,16,2,2]{0,3,2,1:T(2,128)(2,1)}, u32[]{:S(2)}) copy-start(bf16[200,16,2,2]{0,3,2,1:T(2,128)(2,1)} %param.18) | copy-start | bytes 76804
  0.0 11.0 %copy-start.23 = (f32[2,200,7,7]{1,0,3,2:T(2,128)S(1)}, f32[2,200,7,7]{1,0,3,2:T(2,128)}, u32[]{:S(2)}) copy-start(f32[2,200,7,7]{1,0,3,2:T(2,128)} %param.19) | copy-start | bytes 235204
  0.0 27.7 %all-to-all-start = ((bf16[128,1,16,256]{3,2,1,0:T(8,128)(2,1)}), bf16[128,1,16,256]{3,2,1,0:T(8,128)(2,1)S(1)}, u32[]{:S(2)}, u32[]{:S(2)}) async-start(bf16[128,1,16,256]{3,2,1,0:T(8,128)(2,1)} %bitcast.36), calls=%async_computation | async-start | bytes 2097152 | tf_op jit(solution)/shard_map/all_to_all | solution.py:588
  11.4 3.9 %copy-start.22 = (bf16[2,200,800]{2,1,0:T(8,128)(2,1)S(1)}, bf16[2,200,800]{2,1,0:T(8,128)(2,1)}, u32[]{:S(2)}) copy-start(bf16[2,200,800]{2,1,0:T(8,128)(2,1)} %param.22) | copy-start | bytes 1920004
  15.6 1.5 %copy-start.10 = (bf16[2,208,160]{2,1,0:T(8,128)(2,1)S(1)}, bf16[2,208,160]{2,1,0:T(8,128)(2,1)}, u32[]{:S(2)}) copy-start(bf16[2,208,160]{2,1,0:T(8,128)(2,1)} %pad.8.coef_ref) | copy-start | bytes 399364
  15.6 1.5 %copy-start.16 = (bf16[208,64]{1,0:T(8,128)(2,1)S(1)}, bf16[208,64]{1,0:T(8,128)(2,1)}, u32[]{:S(2)}) copy-start(bf16[208,64]{1,0:T(8,128)(2,1)} %pad.9.stem_ref) | copy-start | bytes 79876
  15.6 1.5 %copy-start.20 = (bf16[160,2176]{1,0:T(8,128)(2,1)S(1)}, bf16[160,2176]{1,0:T(8,128)(2,1)}, u32[]{:S(2)}) copy-start(bf16[160,2176]{1,0:T(8,128)(2,1)} %constant.56.clone.table_ref) | copy-start | bytes 2088964
  17.1 7.3 %copy-start.28 = (s32[64,1]{0,1:T(1,128)S(1)}, s32[64,1]{0,1:T(1,128)}, u32[]{:S(2)}) copy-start(s32[64,1]{0,1:T(1,128)} %param.17) | copy-start | bytes 772
  17.1 10.7 %copy-start.19 = (s32[128,1]{0,1:T(1,128)S(1)}, s32[128,1]{0,1:T(1,128)}, u32[]{:S(2)}) copy-start(s32[128,1]{0,1:T(1,128)} %param.16) | copy-start | bytes 1540
  17.1 21.4 %copy-start.5 = (bf16[128,256]{1,0:T(8,128)(2,1)S(1)}, bf16[128,256]{1,0:T(8,128)(2,1)}, u32[]{:S(2)}) copy-start(bf16[128,256]{1,0:T(8,128)(2,1)} %constant.53.clone.forward_ref) | copy-start | bytes 196612
  19.0 1.4 %copy-start.1 = (bf16[42,208,128]{2,1,0:T(8,128)(2,1)}, bf16[42,208,128]{2,1,0:T(8,128)(2,1)S(1)}, u32[]{:S(2)}) copy-start(bf16[42,208,128]{2,1,0:T(8,128)(2,1)S(1)} %get-tuple-element.60.side_ref) | copy-start | bytes 6709252
  20.3 1.4 %copy-start.3 = (bf16[42,208,128]{2,1,0:T(8,128)(2,1)}, bf16[42,208,128]{2,1,0:T(8,128)(2,1)S(1)}, u32[]{:S(2)}) copy-start(bf16[42,208,128]{2,1,0:T(8,128)(2,1)S(1)} %get-tuple-element.46.side_ref) | copy-start | bytes 6709252
  33.8 9.6 %collective-permute-start = (bf16[2,208,128]{2,1,0:T(8,128)(2,1)S(1)}, bf16[2,208,128]{2,1,0:T(8,128)(2,1)S(1)}, u32[]{:S(2)}, u32[]{:S(2)}) collective-permute-start(bf16[2,208,128]{2,1,0:T(8,128)(2,1)S(1)} %get-tuple-element.38.own_even_ref), channel_id=1, source_target_pairs={{0,8},{8,0},{16,24},{24,16},{32,40},{40,32},{48,56},{56,48},{64,72... | collective-permute-start | bytes 319496 | tf_op jit(solution)/shard_map/ppermute | solution.py:616
  34.4 9.0 %collective-permute-start.1 = (bf16[2,208,128]{2,1,0:T(8,128)(2,1)S(1)}, bf16[2,208,128]{2,1,0:T(8,128)(2,1)S(1)}, u32[]{:S(2)}, u32[]{:S(2)}) collective-permute-start(bf16[2,208,128]{2,1,0:T(8,128)(2,1)S(1)} %get-tuple-element.39.own_odd_ref), channel_id=1, source_target_pairs={{0,120},{8,16},{16,8},{24,32},{32,24},{40,48},{48,40},{56,64},{64,... | collective-permute-start | bytes 319496 | tf_op jit(solution)/shard_map/ppermute | solution.py:617
  44.0 11.1 %collective-permute-start.2 = (bf16[5,208,128]{2,1,0:T(8,128)(2,1)S(1)}, bf16[5,208,128]{2,1,0:T(8,128)(2,1)S(1)}, u32[]{:S(2)}, u32[]{:S(2)}) collective-permute-start(bf16[5,208,128]{2,1,0:T(8,128)(2,1)S(1)} %get-tuple-element.45), channel_id=1, source_target_pairs={{0,1},{1,0},{2,3},{3,2},{4,5},{5,4},{6,7},{7,6},{8,9},{9,8},{10,11... | collective-permute-start | bytes 798728 | tf_op jit(solution)/shard_map/ppermute | solution.py:624
  45.0 10.8 %copy-start = (bf16[2,800,200]{1,2,0:T(8,128)(2,1)S(1)}, bf16[2,800,200]{1,2,0:T(8,128)(2,1)}, u32[]{:S(2)}) copy-start(bf16[2,800,200]{1,2,0:T(8,128)(2,1)} %param.24) | copy-start | bytes 1920004
  45.0 10.8 %copy-start.4 = (bf16[42,208,128]{2,1,0:T(8,128)(2,1)S(1)}, bf16[42,208,128]{2,1,0:T(8,128)(2,1)}, u32[]{:S(2)}) copy-start(bf16[42,208,128]{2,1,0:T(8,128)(2,1)} %copy-done.3) | copy-start | bytes 6709252
  45.0 10.8 %copy-start.6 = (bf16[256,128]{1,0:T(8,128)(2,1)S(1)}, bf16[256,128]{1,0:T(8,128)(2,1)}, u32[]{:S(2)}) copy-start(bf16[256,128]{1,0:T(8,128)(2,1)} %constant.54.clone.inverse_ref) | copy-start | bytes 196612
  45.0 10.8 %copy-start.7 = (bf16[128,256]{1,0:T(8,128)(2,1)S(1)}, bf16[128,256]{1,0:T(8,128)(2,1)}, u32[]{:S(2)}) copy-start(bf16[128,256]{1,0:T(8,128)(2,1)} %constant.52.clone.flipped_ref) | copy-start | bytes 196612
  45.0 10.8 %copy-start.12 = (f32[2,208,128]{2,1,0:T(8,128)S(1)}, f32[2,208,128]{2,1,0:T(8,128)}, u32[]{:S(2)}) copy-start(f32[2,208,128]{2,1,0:T(8,128)} %copy-done.11) | copy-start | bytes 638980
  45.0 10.8 %copy-start.13 = (bf16[128,128]{1,0:T(8,128)(2,1)S(1)}, bf16[128,128]{1,0:T(8,128)(2,1)}, u32[]{:S(2)}) copy-start(bf16[128,128]{1,0:T(8,128)(2,1)} %constant.55.clone.turn_ref) | copy-start | bytes 98308
  45.0 10.8 %copy-start.15 = (f32[208,128]{1,0:T(8,128)S(1)}, f32[208,128]{1,0:T(8,128)}, u32[]{:S(2)}) copy-start(f32[208,128]{1,0:T(8,128)} %copy-done.14) | copy-start | bytes 319492
  45.0 10.7 %collective-permute-start.3 = (bf16[5,208,128]{2,1,0:T(8,128)(2,1)S(1)}, bf16[5,208,128]{2,1,0:T(8,128)(2,1)S(1)}, u32[]{:S(2)}, u32[]{:S(2)}) collective-permute-start(bf16[5,208,128]{2,1,0:T(8,128)(2,1)S(1)} %get-tuple-element.42.after_ref), channel_id=1, source_target_pairs={{1,2},{2,1},{3,4},{4,3},{5,6},{6,5},{7,127},{9,10},{10,9},{11,12},... | collective-permute-start | bytes 798728 | tf_op jit(solution)/shard_map/ppermute | solution.py:625
  69.8 8.0 %collective-permute-start.4 = (bf16[2,208,128]{2,1,0:T(8,128)(2,1)S(1)}, bf16[2,208,128]{2,1,0:T(8,128)(2,1)S(1)}, u32[]{:S(2)}, u32[]{:S(2)}) collective-permute-start(bf16[2,208,128]{2,1,0:T(8,128)(2,1)S(1)} %get-tuple-element.52.own_even_ref), channel_id=1, source_target_pairs={{0,8},{8,0},{16,24},{24,16},{32,40},{40,32},{48,56},{56,48},{64,72... | collective-permute-start | bytes 319496 | tf_op jit(solution)/shard_map/ppermute | solution.py:616
  69.9 7.9 %collective-permute-start.5 = (bf16[2,208,128]{2,1,0:T(8,128)(2,1)S(1)}, bf16[2,208,128]{2,1,0:T(8,128)(2,1)S(1)}, u32[]{:S(2)}, u32[]{:S(2)}) collective-permute-start(bf16[2,208,128]{2,1,0:T(8,128)(2,1)S(1)} %get-tuple-element.53.own_odd_ref), channel_id=1, source_target_pairs={{0,120},{8,16},{16,8},{24,32},{32,24},{40,48},{48,40},{56,64},{64,... | collective-permute-start | bytes 319496 | tf_op jit(solution)/shard_map/ppermute | solution.py:617
  78.4 9.1 %collective-permute-start.6 = (bf16[5,208,128]{2,1,0:T(8,128)(2,1)S(1)}, bf16[5,208,128]{2,1,0:T(8,128)(2,1)S(1)}, u32[]{:S(2)}, u32[]{:S(2)}) collective-permute-start(bf16[5,208,128]{2,1,0:T(8,128)(2,1)S(1)} %get-tuple-element.59), channel_id=1, source_target_pairs={{0,1},{1,0},{2,3},{3,2},{4,5},{5,4},{6,7},{7,6},{8,9},{9,8},{10,11... | collective-permute-start | bytes 798728 | tf_op jit(solution)/shard_map/ppermute | solution.py:624
  78.5 10.6 %copy-start.2 = (bf16[42,208,128]{2,1,0:T(8,128)(2,1)S(1)}, bf16[42,208,128]{2,1,0:T(8,128)(2,1)}, u32[]{:S(2)}) copy-start(bf16[42,208,128]{2,1,0:T(8,128)(2,1)} %copy-done.1) | copy-start | bytes 6709252
  78.5 10.6 %copy-start.9 = (f32[2,208,128]{2,1,0:T(8,128)S(1)}, f32[2,208,128]{2,1,0:T(8,128)}, u32[]{:S(2)}) copy-start(f32[2,208,128]{2,1,0:T(8,128)} %copy-done.8) | copy-start | bytes 638980
  78.5 10.6 %collective-permute-start.7 = (bf16[5,208,128]{2,1,0:T(8,128)(2,1)S(1)}, bf16[5,208,128]{2,1,0:T(8,128)(2,1)S(1)}, u32[]{:S(2)}, u32[]{:S(2)}) collective-permute-start(bf16[5,208,128]{2,1,0:T(8,128)(2,1)S(1)} %get-tuple-element.56.after_ref), channel_id=1, source_target_pairs={{1,2},{2,1},{3,4},{4,3},{5,6},{6,5},{7,127},{9,10},{10,9},{11,12},... | collective-permute-start | bytes 798728 | tf_op jit(solution)/shard_map/ppermute | solution.py:625
  (6 other events, 4.5 us)

commit v5 on v4

--- a/solution.py
+++ b/solution.py
@@ -124,7 +124,9 @@
 
 
 def stem_kernel(rows_ref, flags_ref, owner_ref, arrived_ref, weight_ref, state_ref, row_even_ref, row_odd_ref,
-                column_even_ref, column_odd_ref, inverse_ref, split_ref, low_ref, high_ref):
+                column_even_ref, column_odd_ref, inverse_ref, split_ref, low_ref, high_ref, held_weight_ref, weight_sem):
+    copy = pltpu.make_async_copy(weight_ref, held_weight_ref, weight_sem)
+    copy.start()
     pieces = arrived_ref.shape[0]
     flux = arrived_ref.shape[1]
     step = 32
@@ -146,6 +148,7 @@
         return 0
 
     lax.fori_loop(0, pieces // step, split, 0)
+    copy.wait()
     state_ref[...] = jnp.zeros_like(state_ref)
     low_ref[...] = jnp.zeros_like(low_ref)
     high_ref[...] = jnp.zeros_like(high_ref)
@@ -157,7 +160,7 @@
             one = split_ref[inverse_ref[2 * row]]
             two = split_ref[inverse_ref[2 * row + 1]]
             columns.append(jnp.concatenate([one[:, :LANES], one[:, LANES:], two[:, :LANES], two[:, LANES:]], axis=0))
-        out = dot(weight_ref[...], jnp.concatenate(columns, axis=1))
+        out = dot(held_weight_ref[...], jnp.concatenate(columns, axis=1))
         for at, row in enumerate(rows):
             value = out[:, at * LANES:(at + 1) * LANES].astype(BF16)
             state_ref[row] = value
@@ -434,13 +437,15 @@
     return pl.pallas_call(
         stem_kernel,
         out_shape=[shape(height, width, LANES)] + edge_shapes(width),
-        in_specs=[smem(), smem(), smem(), vmem(), vmem()],
+        in_specs=[smem(), smem(), smem(), vmem(), pl.BlockSpec(memory_space=pl.ANY)],
         out_specs=[vmem()] * 5,
         scratch_shapes=[
             pltpu.SMEM(owner.shape, jnp.int32),
             pltpu.VMEM(arrived.shape, BF16),
             pltpu.VMEM((2, width, LANES), BF16),
             pltpu.VMEM((2, width, LANES), BF16),
+            pltpu.VMEM(weight.shape, BF16),
+            pltpu.SemaphoreType.DMA,
         ],
         compiler_params=params(24),
         name="stem",

time: 105 us -> 105 us (level)
  transfers between devices with their start and end apart: 9 -> 9, of which waited for: 3 -> 3; matrix products, arithmetic and copies ran while one was open for 7% -> 6% of each run, Pallas kernels for 20% -> 20%
where the time goes in v5:
time: 105 us
  Pallas kernels  57.1 us (54%)
  starting transfers between devices  29.1 us (28%)
  local copies, waits for them, and re-layouts  11.7 us (11%)
  waiting for transfers between devices  3.53 us (3%)
  other arithmetic  2.22 us (2%)
  between operations  1.29 us (1%)
    pallas_call x2, Pallas kernels, run_block(): pl.pallas_call(functools.partial(block_kernel, last, block), out_shape=ou...  29.5 us
    pallas_call x4, Pallas kernels, run_product(): pl.pallas_call(functools.partial(product_kernel, first), out_shape=[shape...  14.7 us
    all_to_all x1, starting transfers between devices, body(): lax.all_to_all(atm_flux[0], ('gx', 'gy'), split_axis=0, concat_axis=0, ti...  10.8 us
    ppermute x2, starting transfers between devices, body(): row_odd = lax.ppermute(row_odd, ('gx', 'gy'), lat_odd)  9.23 us
    unnamed x60, local copies, waits for them, and re-layouts  7.4 us
    ppermute x2, starting transfers between devices, body(): column_odd = lax.ppermute(own_odd, 'gx', lon_odd)  7.25 us
    pallas_call x1, Pallas kernels, run_stem(): pl.pallas_call(stem_kernel, out_shape=[shape(height, width, LANES)] + edg...  5.29 us
    pallas_call x2, Pallas kernels, run_transform(): pl.pallas_call(transform_kernel, out_shape=shape(height, width, 2 * LANES...  4.7 us
  transfers between devices with their start and end apart: 9, of which 3 were waited for; matrix products, arithmetic and copies ran while one was open for 6% of the time, Pallas kernels for 20%

profile of v5, /device:TPU:7, one launch (start us, length us, event | category | flops | bytes accessed | tf_op | source)
XLA Modules:
  0.0 105.0 jit_solution(5214296533247490707)
XLA Ops:
  0.0 10.8 %all-to-all-start = ((bf16[128,1,16,256]{3,2,1,0:T(8,128)(2,1)}), bf16[128,1,16,256]{3,2,1,0:T(8,128)(2,1)S(1)}, u32[]{:S(2)}, u32[]{:S(2)}) async-start(bf16[128,1,16,256]{3,2,1,0:T(8,128)(2,1)} %bitcast.36), calls=%async_computation | async-start | bytes 2097152 | tf_op jit(solution)/shard_map/all_to_all | solution.py:593
  12.3 0.6 pad.9.stem_ref
  13.3 0.7 pad.8.coef_ref
  14.3 1.0 copy.82
  15.8 0.8 copy-done.21
  17.1 1.8 %prepare.1 = (bf16[7,208,256]{2,1,0:T(8,128)(2,1)S(1)}, bf16[42,208,128]{2,1,0:T(8,128)(2,1)S(1)}, f32[208,128]{1,0:T(8,128)S(1)}, f32[2,208,128]{2,1,0:T(8,128)...) custom-call(bf16[2,208,160]{2,1,0:T(8,128)(2,1)S(1)} %copy-done.10, ...), custom_call_target="tpu_custom_call" | custom-call | flops 1005322240 | bytes 10000000 | tf_op jit(solution)/shard_map/prepare/pallas_call | solution.py:425
  19.0 1.4 %copy-done.1 = bf16[42,208,128]{2,1,0:T(8,128)(2,1)} copy-done((bf16[42,208,128]{2,1,0:T(8,128)(2,1)}, bf16[42,208,128]{2,1,0:T(8,128)(2,1)S(1)}, u32[]{:S(2)}) %copy-start.1) | copy-done | bytes 2236440
  20.3 1.4 %copy-done.3 = bf16[42,208,128]{2,1,0:T(8,128)(2,1)} copy-done((bf16[42,208,128]{2,1,0:T(8,128)(2,1)}, bf16[42,208,128]{2,1,0:T(8,128)(2,1)S(1)}, u32[]{:S(2)}) %copy-start.3) | copy-done | bytes 2236440
  21.7 0.7 copy-done.8
  22.4 0.7 copy-done.11
  23.1 0.6 copy-done.14
  23.7 0.6 copy-done.17
  25.8 0.6 pad_add_fusion.rows_ref
  26.5 1.2 %all-to-all-done = bf16[128,1,16,256]{3,2,1,0:T(8,128)(2,1)S(1)} async-done(((bf16[128,1,16,256]{3,2,1,0:T(8,128)(2,1)}), bf16[128,1,16,256]{3,2,1,0:T(8,128)(2,1)S(1)}, u32[]{:S(2)}, u32[]{:S(2)}) %all-to-all-start) | async-done | bytes 1048608 | tf_op jit(solution)/shard_map/all_to_all | solution.py:593
  27.8 0.8 copy-done.18
  28.6 5.3 %stem.1 = (bf16[64,208,128]{2,1,0:T(8,128)(2,1)S(1)}, bf16[3,208,128]{2,1,0:T(8,128)(2,1)S(1)}, bf16[3,208,128]{2,1,0:T(8,128)(2,1)S(1)}, bf16[2,208,128]{2,1,0:T(8,128)(2,1)S(1)}, bf16[2,208,128]{2,1,0:T(8,128)(2,1)S(1)}) custom-call(s32[49]{0:T(128)S(1)} %pad_add_fusion.rows_ref, s32[3]{0:T(128)S(1)} %pad_add_fusion.1.flags_ref, s32[128]{0:T(128)S(1)} %bitcast.35, ...), custom_call_target="tpu_custom_call" | custom-call | tf_op jit(solution)/shard_map/stem/pallas_call | solution.py:437
  33.9 0.7 collective-permute-start
  34.6 4.1 %collective-permute-start.1 = (bf16[2,208,128]{2,1,0:T(8,128)(2,1)S(1)}, bf16[2,208,128]{2,1,0:T(8,128)(2,1)S(1)}, u32[]{:S(2)}, u32[]{:S(2)}) collective-permute-start(bf16[2,208,128]{2,1,0:T(8,128)(2,1)S(1)} %get-tuple-element.39.own_odd_ref), channel_id=1, source_target_pairs={{0,120},{8,16},{16,8},{24,32},{32,24},{40,48},{48,40},{56,64},{64,... | collective-permute-start | bytes 319496 | tf_op jit(solution)/shard_map/ppermute | solution.py:622
  38.7 2.3 %transform.2.wave_ref.after_ref = bf16[64,208,256]{2,1,0:T(8,128)(2,1)S(1)} custom-call(bf16[64,208,128]{2,1,0:T(8,128)(2,1)S(1)} %get-tuple-element.36.state_ref, bf16[128,256]{1,0:T(8,128)(2,1)S(1)} %copy-done.5), custom_call_target="tpu_custom_call" | custom-call | flops 872415232 | bytes 10000000 | tf_op jit(solution)/shard_map/transform/pallas_call | solution.py:457
  41.0 2.4 %product.4.after_ref.prod_one_ref = bf16[48,64,128]{2,1,0:T(8,128)(2,1)S(1)} custom-call(s32[49]{0:T(128)S(1)} %pad_add_fusion.rows_ref, bf16[64,208,256]{2,1,0:T(8,128)(2,1)S(1)} %transform.2.wave_ref.after_ref, bf16[7,208,256]{2,1,0:T(8,128)(2,1)S(1)} %get-tuple-element.37.mix_ref, bf16[64,208,256]{2,1,0:T(8,128)(2,1)S(1)} %transform.2.wave_ref.after_ref), custom_call_target="tpu_custom_call" | custom-call | flops 11010048 | bytes 20000000 | tf_op jit(solution)/shard_map/product/pallas_call | solution.py:472
  44.1 1.0 collective-permute-start.2
  45.1 5.1 %collective-permute-start.3 = (bf16[5,208,128]{2,1,0:T(8,128)(2,1)S(1)}, bf16[5,208,128]{2,1,0:T(8,128)(2,1)S(1)}, u32[]{:S(2)}, u32[]{:S(2)}) collective-permute-start(bf16[5,208,128]{2,1,0:T(8,128)(2,1)S(1)} %get-tuple-element.42.after_ref), channel_id=1, source_target_pairs={{1,2},{2,1},{3,4},{4,3},{5,6},{6,5},{7,127},{9,10},{10,9},{11,12},... | collective-permute-start | bytes 798728 | tf_op jit(solution)/shard_map/ppermute | solution.py:630
  50.3 4.9 %product.5 = (bf16[48,144,128]{2,1,0:T(8,128)(2,1)S(1)}, bf16[12,208,256]{2,1,0:T(8,128)(2,1)S(1)}) custom-call(s32[49]{0:T(128)S(1)} %pad_add_fusion.rows_ref, bf16[64,208,256]{2,1,0:T(8,128)(2,1)S(1)} %transform.2.wave_ref.after_ref, bf16[7,208,256]{2,1,0:T(8,128)(2,1)S(1)} %get-tuple-element.37.mix_ref, bf16[5,208,128]{2,1,0:T(8,128)(2,1)S(1)} %get-tuple-element.42.after_ref), custom_call_target="tpu_custom_call" | custom-call | flops 24772608 | bytes 20000000 | tf_op jit(solution)/shard_map/product/pallas_call | solution.py:472
  55.2 0.7 collective-permute-done.3.row_odd_ref
  55.9 13.9 %block.2 = (bf16[64,208,128]{2,1,0:T(8,128)(2,1)S(1)}, bf16[3,208,128]{2,1,0:T(8,128)(2,1)S(1)}, bf16[3,208,128]{2,1,0:T(8,128)(2,1)S(1)}, bf16[2,208,128]{2,1,0:T(8,128)(2,1)S(1)}, bf16[2,208,128]{2,1,0:T(8,128)(2,1)S(1)}) custom-call(s32[49]{0:T(128)S(1)} %pad_add_fusion.rows_ref, s32[3]{0:T(128)S(1)} %pad_add_fusion.1.flags_ref, ...), custom_call_target="tpu_custom_call" | custom-call | tf_op jit(solution)/shard_map/block/pallas_call | solution.py:520
  69.9 3.1 %collective-permute-start.5 = (bf16[2,208,128]{2,1,0:T(8,128)(2,1)S(1)}, bf16[2,208,128]{2,1,0:T(8,128)(2,1)S(1)}, u32[]{:S(2)}, u32[]{:S(2)}) collective-permute-start(bf16[2,208,128]{2,1,0:T(8,128)(2,1)S(1)} %get-tuple-element.53.own_odd_ref), channel_id=1, source_target_pairs={{0,120},{8,16},{16,8},{24,32},{32,24},{40,48},{48,40},{56,64},{64,... | collective-permute-start | bytes 319496 | tf_op jit(solution)/shard_map/ppermute | solution.py:622
  73.1 2.3 %transform.3.wave_ref.after_ref = bf16[64,208,256]{2,1,0:T(8,128)(2,1)S(1)} custom-call(bf16[64,208,128]{2,1,0:T(8,128)(2,1)S(1)} %get-tuple-element.50.state_ref, bf16[128,256]{1,0:T(8,128)(2,1)S(1)} %copy-done.5), custom_call_target="tpu_custom_call" | custom-call | flops 872415232 | bytes 10000000 | tf_op jit(solution)/shard_map/transform/pallas_call | solution.py:457
  75.4 2.4 %product.6.after_ref.prod_one_ref = bf16[48,64,128]{2,1,0:T(8,128)(2,1)S(1)} custom-call(s32[49]{0:T(128)S(1)} %pad_add_fusion.rows_ref, bf16[64,208,256]{2,1,0:T(8,128)(2,1)S(1)} %transform.3.wave_ref.after_ref, bf16[7,208,256]{2,1,0:T(8,128)(2,1)S(1)} %get-tuple-element.51.mix_ref, bf16[64,208,256]{2,1,0:T(8,128)(2,1)S(1)} %transform.3.wave_ref.after_ref), custom_call_target="tpu_custom_call" | custom-call | flops 11010048 | bytes 20000000 | tf_op jit(solution)/shard_map/product/pallas_call | solution.py:472
  78.6 4.1 %collective-permute-start.7 = (bf16[5,208,128]{2,1,0:T(8,128)(2,1)S(1)}, bf16[5,208,128]{2,1,0:T(8,128)(2,1)S(1)}, u32[]{:S(2)}, u32[]{:S(2)}) collective-permute-start(bf16[5,208,128]{2,1,0:T(8,128)(2,1)S(1)} %get-tuple-element.56.after_ref), channel_id=1, source_target_pairs={{1,2},{2,1},{3,4},{4,3},{5,6},{6,5},{7,127},{9,10},{10,9},{11,12},... | collective-permute-start | bytes 798728 | tf_op jit(solution)/shard_map/ppermute | solution.py:630
  82.7 4.9 %product.7 = (bf16[48,144,128]{2,1,0:T(8,128)(2,1)S(1)}, bf16[12,208,256]{2,1,0:T(8,128)(2,1)S(1)}) custom-call(s32[49]{0:T(128)S(1)} %pad_add_fusion.rows_ref, bf16[64,208,256]{2,1,0:T(8,128)(2,1)S(1)} %transform.3.wave_ref.after_ref, bf16[7,208,256]{2,1,0:T(8,128)(2,1)S(1)} %get-tuple-element.51.mix_ref, bf16[5,208,128]{2,1,0:T(8,128)(2,1)S(1)} %get-tuple-element.56.after_ref), custom_call_target="tpu_custom_call" | custom-call | flops 24772608 | bytes 20000000 | tf_op jit(solution)/shard_map/product/pallas_call | solution.py:472
  87.6 1.6 %collective-permute-done.7.row_odd_ref = bf16[5,208,128]{2,1,0:T(8,128)(2,1)S(1)} collective-permute-done((bf16[5,208,128]{2,1,0:T(8,128)(2,1)S(1)}, bf16[5,208,128]{2,1,0:T(8,128)(2,1)S(1)}, u32[]{:S(2)}, u32[]{:S(2)}) %collective-permute-start.7) | collective-permute-done | bytes 266272 | tf_op jit(solution)/shard_map/ppermute | solution.py:630
  89.2 15.5 %block.3 = bf16[200,64,128]{2,1,0:T(8,128)(2,1)} custom-call(s32[49]{0:T(128)S(1)} %pad_add_fusion.rows_ref, s32[3]{0:T(128)S(1)} %pad_add_fusion.1.flags_ref, bf16[64,208,128]{2,1,0:T(8,128)(2,1)S(1)} %get-tuple-element.50.state_ref, bf16[48,64,128]{2,1,0:T(8,128)(2,1)S(1)} %product.6.after_ref.prod_one_ref, ...), custom_call_target="tpu_custom_call" | custom-call | tf_op jit(solution)/shard_map/block/pallas_call | solution.py:520
  (88 shorter events, 5.3 us)
Async XLA Ops:
  0.0 10.8 %copy-start.26 = (f32[2,200]{1,0:T(2,128)S(1)}, f32[2,200]{1,0:T(2,128)}, u32[]{:S(2)}) copy-start(f32[2,200]{1,0:T(2,128)} %param.20) | copy-start | bytes 4804
  0.0 10.9 %copy-start.27 = (f32[2,200]{1,0:T(2,128)S(1)}, f32[2,200]{1,0:T(2,128)}, u32[]{:S(2)}) copy-start(f32[2,200]{1,0:T(2,128)} %param.21) | copy-start | bytes 4804
  0.0 10.9 %copy-start.25 = (f32[2,800]{1,0:T(2,128)S(1)}, f32[2,800]{1,0:T(2,128)}, u32[]{:S(2)}) copy-start(f32[2,800]{1,0:T(2,128)} %param.23) | copy-start | bytes 19204
  0.0 10.9 %copy-start.24 = (bf16[200,16,2,2]{0,3,2,1:T(2,128)(2,1)S(1)}, bf16[200,16,2,2]{0,3,2,1:T(2,128)(2,1)}, u32[]{:S(2)}) copy-start(bf16[200,16,2,2]{0,3,2,1:T(2,128)(2,1)} %param.18) | copy-start | bytes 76804
  0.0 11.0 %copy-start.23 = (f32[2,200,7,7]{1,0,3,2:T(2,128)S(1)}, f32[2,200,7,7]{1,0,3,2:T(2,128)}, u32[]{:S(2)}) copy-start(f32[2,200,7,7]{1,0,3,2:T(2,128)} %param.19) | copy-start | bytes 235204
  0.0 27.7 %all-to-all-start = ((bf16[128,1,16,256]{3,2,1,0:T(8,128)(2,1)}), bf16[128,1,16,256]{3,2,1,0:T(8,128)(2,1)S(1)}, u32[]{:S(2)}, u32[]{:S(2)}) async-start(bf16[128,1,16,256]{3,2,1,0:T(8,128)(2,1)} %bitcast.36), calls=%async_computation | async-start | bytes 2097152 | tf_op jit(solution)/shard_map/all_to_all | solution.py:593
  11.4 3.9 %copy-start.22 = (bf16[2,200,800]{2,1,0:T(8,128)(2,1)S(1)}, bf16[2,200,800]{2,1,0:T(8,128)(2,1)}, u32[]{:S(2)}) copy-start(bf16[2,200,800]{2,1,0:T(8,128)(2,1)} %param.22) | copy-start | bytes 1920004
  15.6 1.5 %copy-start.10 = (bf16[2,208,160]{2,1,0:T(8,128)(2,1)S(1)}, bf16[2,208,160]{2,1,0:T(8,128)(2,1)}, u32[]{:S(2)}) copy-start(bf16[2,208,160]{2,1,0:T(8,128)(2,1)} %pad.8.coef_ref) | copy-start | bytes 399364
  15.6 1.5 %copy-start.16 = (bf16[208,64]{1,0:T(8,128)(2,1)S(1)}, bf16[208,64]{1,0:T(8,128)(2,1)}, u32[]{:S(2)}) copy-start(bf16[208,64]{1,0:T(8,128)(2,1)} %pad.9.stem_ref) | copy-start | bytes 79876
  15.6 1.5 %copy-start.20 = (bf16[160,2176]{1,0:T(8,128)(2,1)S(1)}, bf16[160,2176]{1,0:T(8,128)(2,1)}, u32[]{:S(2)}) copy-start(bf16[160,2176]{1,0:T(8,128)(2,1)} %constant.56.clone.table_ref) | copy-start | bytes 2088964
  17.1 7.3 %copy-start.28 = (s32[64,1]{0,1:T(1,128)S(1)}, s32[64,1]{0,1:T(1,128)}, u32[]{:S(2)}) copy-start(s32[64,1]{0,1:T(1,128)} %param.17) | copy-start | bytes 772
  17.1 10.7 %copy-start.19 = (s32[128,1]{0,1:T(1,128)S(1)}, s32[128,1]{0,1:T(1,128)}, u32[]{:S(2)}) copy-start(s32[128,1]{0,1:T(1,128)} %param.16) | copy-start | bytes 1540
  17.1 21.6 %copy-start.5 = (bf16[128,256]{1,0:T(8,128)(2,1)S(1)}, bf16[128,256]{1,0:T(8,128)(2,1)}, u32[]{:S(2)}) copy-start(bf16[128,256]{1,0:T(8,128)(2,1)} %constant.53.clone.forward_ref) | copy-start | bytes 196612
  19.0 1.4 %copy-start.1 = (bf16[42,208,128]{2,1,0:T(8,128)(2,1)}, bf16[42,208,128]{2,1,0:T(8,128)(2,1)S(1)}, u32[]{:S(2)}) copy-start(bf16[42,208,128]{2,1,0:T(8,128)(2,1)S(1)} %get-tuple-element.60.side_ref) | copy-start | bytes 6709252
  20.3 1.4 %copy-start.3 = (bf16[42,208,128]{2,1,0:T(8,128)(2,1)}, bf16[42,208,128]{2,1,0:T(8,128)(2,1)S(1)}, u32[]{:S(2)}) copy-start(bf16[42,208,128]{2,1,0:T(8,128)(2,1)S(1)} %get-tuple-element.46.side_ref) | copy-start | bytes 6709252
  33.9 9.6 %collective-permute-start = (bf16[2,208,128]{2,1,0:T(8,128)(2,1)S(1)}, bf16[2,208,128]{2,1,0:T(8,128)(2,1)S(1)}, u32[]{:S(2)}, u32[]{:S(2)}) collective-permute-start(bf16[2,208,128]{2,1,0:T(8,128)(2,1)S(1)} %get-tuple-element.38.own_even_ref), channel_id=1, source_target_pairs={{0,8},{8,0},{16,24},{24,16},{32,40},{40,32},{48,56},{56,48},{64,72... | collective-permute-start | bytes 319496 | tf_op jit(solution)/shard_map/ppermute | solution.py:621
  34.6 8.9 %collective-permute-start.1 = (bf16[2,208,128]{2,1,0:T(8,128)(2,1)S(1)}, bf16[2,208,128]{2,1,0:T(8,128)(2,1)S(1)}, u32[]{:S(2)}, u32[]{:S(2)}) collective-permute-start(bf16[2,208,128]{2,1,0:T(8,128)(2,1)S(1)} %get-tuple-element.39.own_odd_ref), channel_id=1, source_target_pairs={{0,120},{8,16},{16,8},{24,32},{32,24},{40,48},{48,40},{56,64},{64,... | collective-permute-start | bytes 319496 | tf_op jit(solution)/shard_map/ppermute | solution.py:622
  44.1 11.1 %collective-permute-start.2 = (bf16[5,208,128]{2,1,0:T(8,128)(2,1)S(1)}, bf16[5,208,128]{2,1,0:T(8,128)(2,1)S(1)}, u32[]{:S(2)}, u32[]{:S(2)}) collective-permute-start(bf16[5,208,128]{2,1,0:T(8,128)(2,1)S(1)} %get-tuple-element.45), channel_id=1, source_target_pairs={{0,1},{1,0},{2,3},{3,2},{4,5},{5,4},{6,7},{7,6},{8,9},{9,8},{10,11... | collective-permute-start | bytes 798728 | tf_op jit(solution)/shard_map/ppermute | solution.py:629
  45.1 10.8 %copy-start = (bf16[2,800,200]{1,2,0:T(8,128)(2,1)S(1)}, bf16[2,800,200]{1,2,0:T(8,128)(2,1)}, u32[]{:S(2)}) copy-start(bf16[2,800,200]{1,2,0:T(8,128)(2,1)} %param.24) | copy-start | bytes 1920004
  45.1 10.8 %copy-start.4 = (bf16[42,208,128]{2,1,0:T(8,128)(2,1)S(1)}, bf16[42,208,128]{2,1,0:T(8,128)(2,1)}, u32[]{:S(2)}) copy-start(bf16[42,208,128]{2,1,0:T(8,128)(2,1)} %copy-done.3) | copy-start | bytes 6709252
  45.1 10.8 %copy-start.6 = (bf16[256,128]{1,0:T(8,128)(2,1)S(1)}, bf16[256,128]{1,0:T(8,128)(2,1)}, u32[]{:S(2)}) copy-start(bf16[256,128]{1,0:T(8,128)(2,1)} %constant.54.clone.inverse_ref) | copy-start | bytes 196612
  45.1 10.8 %copy-start.7 = (bf16[128,256]{1,0:T(8,128)(2,1)S(1)}, bf16[128,256]{1,0:T(8,128)(2,1)}, u32[]{:S(2)}) copy-start(bf16[128,256]{1,0:T(8,128)(2,1)} %constant.52.clone.flipped_ref) | copy-start | bytes 196612
  45.1 10.8 %copy-start.12 = (f32[2,208,128]{2,1,0:T(8,128)S(1)}, f32[2,208,128]{2,1,0:T(8,128)}, u32[]{:S(2)}) copy-start(f32[2,208,128]{2,1,0:T(8,128)} %copy-done.11) | copy-start | bytes 638980
  45.1 10.8 %copy-start.13 = (bf16[128,128]{1,0:T(8,128)(2,1)S(1)}, bf16[128,128]{1,0:T(8,128)(2,1)}, u32[]{:S(2)}) copy-start(bf16[128,128]{1,0:T(8,128)(2,1)} %constant.55.clone.turn_ref) | copy-start | bytes 98308
  45.1 10.8 %copy-start.15 = (f32[208,128]{1,0:T(8,128)S(1)}, f32[208,128]{1,0:T(8,128)}, u32[]{:S(2)}) copy-start(f32[208,128]{1,0:T(8,128)} %copy-done.14) | copy-start | bytes 319492
  45.1 10.7 %collective-permute-start.3 = (bf16[5,208,128]{2,1,0:T(8,128)(2,1)S(1)}, bf16[5,208,128]{2,1,0:T(8,128)(2,1)S(1)}, u32[]{:S(2)}, u32[]{:S(2)}) collective-permute-start(bf16[5,208,128]{2,1,0:T(8,128)(2,1)S(1)} %get-tuple-element.42.after_ref), channel_id=1, source_target_pairs={{1,2},{2,1},{3,4},{4,3},{5,6},{6,5},{7,127},{9,10},{10,9},{11,12},... | collective-permute-start | bytes 798728 | tf_op jit(solution)/shard_map/ppermute | solution.py:630
  69.8 8.0 %collective-permute-start.4 = (bf16[2,208,128]{2,1,0:T(8,128)(2,1)S(1)}, bf16[2,208,128]{2,1,0:T(8,128)(2,1)S(1)}, u32[]{:S(2)}, u32[]{:S(2)}) collective-permute-start(bf16[2,208,128]{2,1,0:T(8,128)(2,1)S(1)} %get-tuple-element.52.own_even_ref), channel_id=1, source_target_pairs={{0,8},{8,0},{16,24},{24,16},{32,40},{40,32},{48,56},{56,48},{64,72... | collective-permute-start | bytes 319496 | tf_op jit(solution)/shard_map/ppermute | solution.py:621
  69.9 8.0 %collective-permute-start.5 = (bf16[2,208,128]{2,1,0:T(8,128)(2,1)S(1)}, bf16[2,208,128]{2,1,0:T(8,128)(2,1)S(1)}, u32[]{:S(2)}, u32[]{:S(2)}) collective-permute-start(bf16[2,208,128]{2,1,0:T(8,128)(2,1)S(1)} %get-tuple-element.53.own_odd_ref), channel_id=1, source_target_pairs={{0,120},{8,16},{16,8},{24,32},{32,24},{40,48},{48,40},{56,64},{64,... | collective-permute-start | bytes 319496 | tf_op jit(solution)/shard_map/ppermute | solution.py:622
  78.5 9.1 %collective-permute-start.6 = (bf16[5,208,128]{2,1,0:T(8,128)(2,1)S(1)}, bf16[5,208,128]{2,1,0:T(8,128)(2,1)S(1)}, u32[]{:S(2)}, u32[]{:S(2)}) collective-permute-start(bf16[5,208,128]{2,1,0:T(8,128)(2,1)S(1)} %get-tuple-element.59), channel_id=1, source_target_pairs={{0,1},{1,0},{2,3},{3,2},{4,5},{5,4},{6,7},{7,6},{8,9},{9,8},{10,11... | collective-permute-start | bytes 798728 | tf_op jit(solution)/shard_map/ppermute | solution.py:629
  78.6 10.6 %copy-start.2 = (bf16[42,208,128]{2,1,0:T(8,128)(2,1)S(1)}, bf16[42,208,128]{2,1,0:T(8,128)(2,1)}, u32[]{:S(2)}) copy-start(bf16[42,208,128]{2,1,0:T(8,128)(2,1)} %copy-done.1) | copy-start | bytes 6709252
  78.6 10.6 %copy-start.9 = (f32[2,208,128]{2,1,0:T(8,128)S(1)}, f32[2,208,128]{2,1,0:T(8,128)}, u32[]{:S(2)}) copy-start(f32[2,208,128]{2,1,0:T(8,128)} %copy-done.8) | copy-start | bytes 638980
  78.6 10.6 %collective-permute-start.7 = (bf16[5,208,128]{2,1,0:T(8,128)(2,1)S(1)}, bf16[5,208,128]{2,1,0:T(8,128)(2,1)S(1)}, u32[]{:S(2)}, u32[]{:S(2)}) collective-permute-start(bf16[5,208,128]{2,1,0:T(8,128)(2,1)S(1)} %get-tuple-element.56.after_ref), channel_id=1, source_target_pairs={{1,2},{2,1},{3,4},{4,3},{5,6},{6,5},{7,127},{9,10},{10,9},{11,12},... | collective-permute-start | bytes 798728 | tf_op jit(solution)/shard_map/ppermute | solution.py:630
  (6 other events, 4.5 us)
